TPU v7x, 256 devices: a whole 4x4x8 slice. The times are simulated.
256 devices in a mesh: section: 2 (over x_lo), seq: 64 (over z, y, x_hi), head: 2 (over core).
Axes of the slice: x: 4 (x_hi: 2, x_lo: 2; x = x_hi * 2 + x_lo), y: 4, z: 8, core: 2. Of those that a mesh axis runs over, the one named last changes fastest.
Arguments:
- query_nope: bfloat16 [2, 8192, 64, 128], P('section', 'seq', 'head'), may hold values from -6 to 6
- query_rope: bfloat16 [2, 8192, 4096], P('section', 'seq', 'head'), may hold values from -8 to 8
- latent: bfloat16 [2, 8192, 576], P('section', ('seq', 'head')), may hold values from -8 to 8
- up_key: bfloat16 [64, 512, 128], P('head'), may hold values from -0.25 to 0.25
- value_up_weight: bfloat16 [64, 512, 128], P('head'), may hold values from -1.5 to 1.5
- lengths: int32 [32], replicated, may hold values from 1 to 4224, 8192 in all
- owner_request_table: int32 [256], replicated, may hold values from 0 to 255, each once
Outputs:
- attended: bfloat16 [2, 8192, 64, 128], P('section', 'seq', 'head')
Inputs may be any that keep to these rules, and one draw needn't show every extreme that they name: The 32 lengths sum to 8192; one is exactly 4224. `owner_request_table`: every request 0 to 255 appears once.
All inputs are finite; a program needn't handle non-finite values.
Results may differ from a plain program's by a relative error of at most 0.0075.
Values may be sent and summed in bfloat16 or wider, within the bound.
A program may use at most 128 MiB of HBM per device.

v0:
```python
import functools
import math

import jax
import jax.numpy as jnp
from jax import lax
from jax.experimental import pallas as pl
from jax.experimental.pallas import tpu as pltpu
from jax.sharding import PartitionSpec as P

SAMPLES = 8
STEPS = 4
BLOCK = 64

scale_top = 448.0
tiny_eps = 1e-06
masked_low = -1e30

KEY_BLOCK = 512
EDGE_BLOCK = 256
ROW_TILE = 512
LANES = 128


def dequantized(rows):
    blocks = rows.astype(jnp.float32).reshape(-1, BLOCK, rows.shape[1])
    largest = jnp.max(jnp.abs(blocks), axis=(1, 2))
    block_scale = ((largest + tiny_eps) / scale_top).astype(jnp.bfloat16)
    factor = block_scale.astype(jnp.float32)[:, None, None]
    stored = (blocks / factor).astype(jnp.bfloat16)
    keys = (stored.astype(jnp.float32) * factor).astype(jnp.bfloat16)
    return keys.reshape(rows.shape)


def token_start(positions, starts):
    return jnp.max(jnp.where(starts[None, :] <= positions[:, None], starts[None, :], 0), axis=1)


def over_lanes(value, width):
    return jnp.concatenate([value] * (width // LANES), axis=1)


def flash_kernel(
    kv_rank,
    exponent_scale,
    plan,
    q_ref,
    keys,
    own_keys,
    low_ref,
    bias_ref,
    out_ref,
    acc,
    top,
    total,
):
    band = pl.program_id(0)
    heads, tokens, width = q_ref.shape
    rows = heads * tokens
    first, full_from, full_to, last = (plan[i, band] for i in range(4))
    q = q_ref[...].reshape(rows, width)
    own = own_keys[...]
    nt = (((1,), (1,)), ((), ()))

    scores = lax.dot_general(q, own, nt, preferred_element_type=jnp.float32)
    bias = jnp.broadcast_to(bias_ref[...][None], (heads, tokens, tokens)).reshape(rows, tokens)
    scores = scores + bias
    own_top = jnp.max(scores, axis=1, keepdims=True)
    expo = jnp.exp2((scores - own_top) * exponent_scale)
    lane = lax.broadcasted_iota(jnp.int32, (rows, LANES), 1)
    total[...] = jnp.where(lane == 0, jnp.sum(expo, axis=1, keepdims=True), 0.0)
    top[...] = jnp.broadcast_to(own_top, (rows, LANES))
    acc[...] = jnp.dot(
        expo.astype(jnp.bfloat16), own[:, :kv_rank], preferred_element_type=jnp.float32
    )

    def fold(at, count, masked):
        at = pl.multiple_of(at, 16)
        key_block = keys[pl.ds(at, count), :]
        for r in range(0, rows, ROW_TILE):
            part = pl.ds(r, ROW_TILE)
            s = lax.dot_general(
                q[r : r + ROW_TILE], key_block, nt, preferred_element_type=jnp.float32
            )
            if masked:
                low = jnp.broadcast_to(
                    low_ref[...][None], (ROW_TILE // tokens, tokens, 1)
                ).reshape(ROW_TILE, 1)
                spot = at + lax.broadcasted_iota(jnp.int32, (1, count), 1)
                s = jnp.where((spot >= low) & (spot < last), s, masked_low)
            before = top[part, :]
            now = jnp.maximum(before, jnp.max(s, axis=1, keepdims=True))
            shrink = jnp.exp2((before - now) * exponent_scale)
            expo = jnp.exp2((s - over_lanes(now, count)) * exponent_scale)
            top[part, :] = now
            summed = total[part, :] * shrink
            for c in range(0, count, LANES):
                summed = summed + expo[:, c : c + LANES]
            total[part, :] = summed
            acc[part, :] = acc[part, :] * over_lanes(shrink, kv_rank) + jnp.dot(
                expo.astype(jnp.bfloat16),
                key_block[:, :kv_rank],
                preferred_element_type=jnp.float32,
            )

    big = (full_to - full_from) // KEY_BLOCK

    @pl.loop(0, (full_from - first + EDGE_BLOCK - 1) // EDGE_BLOCK)
    def _(i):
        fold(first + i * EDGE_BLOCK, EDGE_BLOCK, True)

    @pl.loop(0, big)
    def _(i):
        fold(full_from + i * KEY_BLOCK, KEY_BLOCK, False)

    rest = full_from + big * KEY_BLOCK

    @pl.loop(0, (last - rest + EDGE_BLOCK - 1) // EDGE_BLOCK)
    def _(i):
        fold(rest + i * EDGE_BLOCK, EDGE_BLOCK, True)

    norm = 1.0 / jnp.sum(total[...], axis=1, keepdims=True)
    out_ref[...] = (acc[...] * norm).astype(jnp.bfloat16).reshape(heads, tokens, kv_rank)


def shards(query_nope, query_rope, latent, up_key, value_up_weight, lengths, owner_request_table):
    section_index = lax.axis_index("section")
    owner_index = lax.axis_index("seq")
    is_prefill = section_index == 0
    seq_count = lax.axis_size("seq")
    tok_dev, head_dev, nope_dim = query_nope.shape[1:]
    rope_dim = query_rope.shape[2] // head_dev
    kv_rank = up_key.shape[1]
    width = kv_rank + rope_dim
    tokens_all = tok_dev * seq_count
    req_dev = owner_request_table.shape[0] // seq_count
    groups = owner_request_table.shape[0] // lengths.shape[0]
    band_tokens = tok_dev // req_dev
    exponent_scale = math.log2(math.e) / math.sqrt(nope_dim + rope_dim)

    own_part = dequantized(latent[0])
    came = lax.ppermute(own_part, "section", [(0, 1)])
    part = jnp.where(is_prefill, own_part, came)
    keys = lax.all_gather(part, ("seq", "head"), axis=0, tiled=True)
    keys = jnp.pad(keys, ((0, EDGE_BLOCK), (0, 0)))
    own_keys = lax.all_gather(
        jnp.where(is_prefill, own_part, latent[0]), "head", axis=0, tiled=True
    )

    lifted = jnp.einsum("thn,hkn->htk", query_nope[0], up_key, preferred_element_type=jnp.float32)
    rope_part = query_rope[0].reshape(tok_dev, head_dev, rope_dim).swapaxes(0, 1)
    queries = jnp.concatenate([lifted.astype(jnp.bfloat16), rope_part], axis=2)

    prompt_ends = jnp.cumsum(lengths)
    starts = prompt_ends - lengths
    positions = owner_index * tok_dev + jnp.arange(tok_dev, dtype=jnp.int32)
    prefill_low = token_start(positions, starts)
    band_at = owner_index * tok_dev + band_tokens * jnp.arange(req_dev, dtype=jnp.int32)
    own_requests = (
        lax.dynamic_slice_in_dim(owner_request_table, owner_index * req_dev, req_dev, 0) // groups
    )
    chosen = own_requests[:, None] == jnp.arange(lengths.shape[0], dtype=jnp.int32)[None, :]
    slot_low = jnp.sum(jnp.where(chosen, starts[None, :], 0), axis=1)
    slot_high = jnp.sum(jnp.where(chosen, prompt_ends[None, :], 0), axis=1)
    row_low = jnp.where(is_prefill, prefill_low, jnp.repeat(slot_low, band_tokens))
    by_band = row_low.reshape(req_dev, band_tokens)
    last = jnp.where(is_prefill, jnp.maximum(band_at, by_band[:, 0]), slot_high)
    first = jnp.minimum(by_band[:, 0], last) // 16 * 16
    highest_low = jnp.minimum(by_band[:, -1], last)
    full_from = jnp.minimum((highest_low + 15) // 16 * 16, last // 16 * 16)
    full_from = jnp.maximum(full_from, first)
    full_from = jnp.where(first == highest_low, first, full_from)
    full_from = first + (full_from - first + EDGE_BLOCK - 1) // EDGE_BLOCK * EDGE_BLOCK
    full_from = jnp.minimum(full_from, tokens_all)
    full_to = jnp.maximum(last, full_from)
    last_seen = last
    plan = jnp.stack([first, full_from, full_to, last_seen]).astype(jnp.int32)

    here = jnp.arange(band_tokens, dtype=jnp.int32)
    same_sample = here[None, :] % SAMPLES == here[:, None] % SAMPLES
    earlier_step = here[None, :] // SAMPLES <= here[:, None] // SAMPLES
    decode_seen = jnp.broadcast_to(
        (same_sample & earlier_step)[None], (req_dev, band_tokens, band_tokens)
    )
    prefill_seen = (here[None, None, :] <= here[None, :, None]) & (
        band_at[:, None, None] + here[None, None, :] >= by_band[:, :, None]
    )
    seen = jnp.where(is_prefill, prefill_seen, decode_seen)
    bias = jnp.where(seen, 0.0, masked_low).astype(jnp.float32).reshape(tok_dev, band_tokens)

    rows = head_dev * band_tokens
    latent_out = pl.pallas_call(
        functools.partial(flash_kernel, kv_rank, exponent_scale),
        out_shape=jax.ShapeDtypeStruct((head_dev, tok_dev, kv_rank), jnp.bfloat16),
        grid_spec=pltpu.PrefetchScalarGridSpec(
            num_scalar_prefetch=1,
            grid=(req_dev,),
            in_specs=[
                pl.BlockSpec((head_dev, band_tokens, width), lambda i, s: (0, i, 0)),
                pl.BlockSpec(memory_space=pltpu.VMEM),
                pl.BlockSpec((band_tokens, width), lambda i, s: (i, 0)),
                pl.BlockSpec((band_tokens, 1), lambda i, s: (i, 0)),
                pl.BlockSpec((band_tokens, band_tokens), lambda i, s: (i, 0)),
            ],
            out_specs=pl.BlockSpec((head_dev, band_tokens, kv_rank), lambda i, s: (0, i, 0)),
            scratch_shapes=[
                pltpu.VMEM((rows, kv_rank), jnp.float32),
                pltpu.VMEM((rows, LANES), jnp.float32),
                pltpu.VMEM((rows, LANES), jnp.float32),
            ],
        ),
        compiler_params=pltpu.CompilerParams(vmem_limit_bytes=48 << 20),
    )(plan, queries, keys, own_keys, row_low[:, None], bias)

    attended = jnp.einsum(
        "htk,hkv->thv", latent_out, value_up_weight, preferred_element_type=jnp.float32
    )
    return attended.astype(jnp.bfloat16)[None]


def solution(mesh):
    in_specs = (
        P("section", "seq", "head", None),
        P("section", "seq", "head"),
        P("section", ("seq", "head"), None),
        P("head", None, None),
        P("head", None, None),
        P(),
        P(),
    )
    out_specs = P("section", "seq", "head", None)
    return jax.shard_map(shards, mesh=mesh, in_specs=in_specs, out_specs=out_specs, check_vma=False)
```

profile of v0, /device:TPU:245, one launch (start us, length us, event | category | flops | bytes accessed | tf_op | source)
XLA Modules:
  0.0 249.3 jit_solution(4519468181527575905)
XLA Ops:
  6.5 0.0 copy-start.1
  6.5 0.0 all-gather.2.cloned.1.call-start
  6.5 1.6 fusion.2
  8.8 0.9 fusion.4
  9.7 2.8 %collective-permute-start = (bf16[64,576]{1,0:T(8,128)(2,1)S(1)}, bf16[64,576]{1,0:T(8,128)(2,1)S(1)}, u32[]{:S(2)}, u32[]{:S(2)}) collective-permute-start(bf16[64,576]{1,0:T(8,128)(2,1)S(1)} %fusion.4), channel_id=1, source_target_pairs={{0,128},{1,129},{2,130},{3,131},{4,132},{5,133},{6,134},{7,135},{8... | collective-permute-start | bytes 221192 | tf_op jit(solution)/shard_map/ppermute | solution.py:142
  12.6 1.5 collective-permute-done
  14.0 1.6 bitcast_select_fusion
  15.7 0.0 all-gather.2.cloned.1.call-update
  15.7 0.7 copy.18
  16.4 0.1 reduce-window.8
  16.5 0.1 reduce.1
  16.6 0.7 sub.48
  17.3 0.8 and_select_fusion.6
  18.0 0.2 select_reduce_fusion.1
  18.2 0.1 broadcast_in_dim.72
  18.3 0.1 broadcast_in_dim.74
  18.4 0.1 reshape.598
  18.5 0.1 select_reduce_fusion
  18.6 0.1 reduce_max.23
  18.7 0.1 copy.22
  18.8 1.3 copy.20
  20.1 0.5 copy.21
  20.6 0.1 iota_add_fusion
  20.7 0.1 compare_and_fusion
  20.8 0.1 fusion.7.bias_ref
  20.9 0.1 broadcast_select_fusion.2
  21.0 0.2 slice_reduce_fusion
  21.2 0.0 copy-done.1
  21.2 3.4 %convolution_convert_fusion = bf16[32,128,512]{2,1,0:T(8,128)(2,1)S(1)} fusion(bf16[32,512,128]{2,1,0:T(8,128)(2,1)} %param.10, bf16[128,32,128]{2,1,0:T(8,128)(2,1)S(1)} %bitcast.53), kind=kOutput, calls=%fused_computation.1 | convolution fusion | flops 538968064 | bytes 9437184 | tf_op jit(solution)/shard_map/thn,hkn->htk/dot_general | solution.py:150
  24.7 3.1 %pad_maximum_fusion.q_ref = bf16[32,128,576]{2,1,0:T(8,128)(2,1)} fusion(bf16[32,128,64]{2,1,0:T(8,128)(2,1)S(1)} %bitcast.51, bf16[32,128,512]{2,1,0:T(8,128)(2,1)S(1)} %convolution_convert_fusion), kind=kLoop, calls=%fused_computation | loop fusion | flops 9437184 | bytes 9437184 | tf_op jit(solution)/shard_map/concatenate | solution.py:152
  27.8 3.1 %all_gather.7.own_keys = bf16[128,576]{1,0:T(8,128)(2,1)S(1)} all-gather(bf16[64,576]{1,0:T(8,128)(2,1)S(1)} %get-tuple-element.13), channel_id=1, replica_groups=mesh['section'=2,'seq'=64,'head'=2] {'head'}, dimensions={0}, use_global_device_ids=true | all-gather | bytes 221184 | tf_op jit(solution)/shard_map/all_gather | solution.py:146
  30.9 118.1 %all-gather.2.cloned.1.call-done = bf16[8192,576]{1,0:T(8,128)(2,1)} async-done(((bf16[64,576]{1,0:T(8,128)(2,1)}), bf16[8192,576]{1,0:T(8,128)(2,1)}) %all-gather.2.cloned.1.call-update) | async-done | bytes 9437200 | tf_op jit(solution)/shard_map/all_gather | solution.py:144
  149.1 9.9 %pad.4.keys = bf16[8448,576]{1,0:T(8,128)(2,1)} pad(bf16[8192,576]{1,0:T(8,128)(2,1)} %all-gather.2.cloned.1.call-done, bf16[]{:T(256)} %constant.138.clone.1), padding=0_256x0_0 | pad | bytes 19169282 | tf_op jit(solution)/shard_map/jit(_pad)/pad | solution.py:145
  159.0 0.0 copy-start
  159.0 80.6 %shard_map.73 = bf16[32,128,512]{2,1,0:T(8,128)(2,1)S(1)} custom-call(s32[4,4]{1,0:T(4,128)S(1)} %pad_add_fusion.plan, bf16[32,128,576]{2,1,0:T(8,128)(2,1)} %pad_maximum_fusion.q_ref, bf16[8448,576]{1,0:T(8,128)(2,1)} %pad.4.keys, bf16[128,576]{1,0:T(8,128)(2,1)S(1)} %all_gather.7.own_keys, s32[128,1]{1,0:T(8,128)S(1)} %broadcast_select_fusion.1.low_ref, ...), custom_call_target="tpu_custom_call" | custom-call | tf_op jit(solution)/shard_map/pallas_call | solution.py:192
  239.6 0.0 copy-done
  239.6 1.2 fusion
  240.9 1.6 copy.24
  (8 shorter events, 0.1 us)
Async XLA Ops:
  6.5 14.7 %copy-start.1 = (bf16[1,128,32,128]{3,2,1,0:T(8,128)(2,1)S(1)}, bf16[1,128,32,128]{3,2,1,0:T(8,128)(2,1)}, u32[]{:S(2)}) copy-start(bf16[1,128,32,128]{3,2,1,0:T(8,128)(2,1)} %param.7) | copy-start | bytes 3145732
  6.5 142.5 %all-gather.2.cloned.1.call-start = ((), (), s32[]{:S(2)}) async-start(), calls=%async_computation | async-start | bytes 10567680 | tf_op jit(solution)/shard_map/all_gather | solution.py:144
  9.7 4.3 %collective-permute-start = (bf16[64,576]{1,0:T(8,128)(2,1)S(1)}, bf16[64,576]{1,0:T(8,128)(2,1)S(1)}, u32[]{:S(2)}, u32[]{:S(2)}) collective-permute-start(bf16[64,576]{1,0:T(8,128)(2,1)S(1)} %fusion.4), channel_id=1, source_target_pairs={{0,128},{1,129},{2,130},{3,131},{4,132},{5,133},{6,134},{7,135},{8... | collective-permute-start | bytes 221192 | tf_op jit(solution)/shard_map/ppermute | solution.py:142
  159.0 80.6 %copy-start = (bf16[32,512,128]{2,1,0:T(8,128)(2,1)S(1)}, bf16[32,512,128]{2,1,0:T(8,128)(2,1)}, u32[]{:S(2)}) copy-start(bf16[32,512,128]{2,1,0:T(8,128)(2,1)} %param.11) | copy-start | bytes 12582916
Sparse Core Ops, SparseCore 0:
  15.8 133.2 all-gather.1
where the time goes:
time: 250 us; the launch traced here: 249 us
  waiting for transfers between devices  120 us (48%)
  Pallas kernels  80.6 us (32%)
  local copies, waits for them, and re-layouts  14.8 us (6%)
  between operations  14.2 us (6%)
  other arithmetic  9.56 us (4%)
  matrix products  4.69 us (2%)
  blocking collectives  3.08 us (1%)
  starting transfers between devices  2.83 us (1%)
    all_gather x1, waiting for transfers between devices, shards(): keys = lax.all_gather(part, ('seq', 'head'), axis=0, tiled=True)  118 us
    pallas_call x1, Pallas kernels, shards(): pl.pallas_call(functools.partial(flash_kernel, kv_rank, exponent_scale),...  80.6 us
    pad x1, local copies, waits for them, and re-layouts, shards(): keys = jnp.pad(keys, ((0, EDGE_BLOCK), (0, 0)))  9.95 us
  transfers between devices with their start and end apart: 2, of which 2 were waited for; matrix products, arithmetic and copies ran while one was open for 5% of the time, Pallas kernels for 0%

commit v1 on v0

v1 whole, which is shorter than its diff:
```python
import functools
import math

import jax
import jax.numpy as jnp
from jax import lax
from jax.experimental import pallas as pl
from jax.experimental.pallas import tpu as pltpu
from jax.sharding import PartitionSpec as P

SAMPLES = 8
STEPS = 4
BLOCK = 64

scale_top = 448.0
tiny_eps = 1e-06
masked_low = -1e30

KEY_BLOCK = 1024
EDGE_BLOCK = 512
LANES = 128


def gather_kernel(
    z_count, y_count, own_in, keys, own_out, block, mine_sem, x_send, x_recv, own_sems,
    z_send, z_recv, y_send, y_recv, sib_send, sib_recv,
):
    section = lax.axis_index("section")
    seq = lax.axis_index("seq")
    core = lax.axis_index("head")
    z = seq // (2 * y_count)
    y = seq // 2 % y_count
    hi = seq % 2

    def place(dz, dy):
        return lax.rem(z + dz + z_count, z_count), lax.rem(y + dy + y_count, y_count)

    def device(dz=0, dy=0, to_hi=None, to_section=None, to_core=None):
        tz, ty = place(dz, dy)
        th = hi if to_hi is None else to_hi
        return (
            section if to_section is None else to_section,
            (tz * y_count + ty) * 2 + th,
            core if to_core is None else to_core,
        )

    barrier = pltpu.get_barrier_semaphore()
    peers = [
        device(to_core=1 - core),
        device(to_section=1 - section),
        device(to_hi=1 - hi),
        device(to_section=1 - section, to_hi=1 - hi),
        device(dz=1),
        device(dz=-1),
        device(dy=1),
        device(dy=-1),
    ]
    for peer in peers:
        pl.semaphore_signal(barrier, inc=1, device_id=peer, device_id_type=pl.DeviceIdType.MESH)

    @pl.when(section == 0)
    def _():
        rows = own_in[...].astype(jnp.float32)
        largest = jnp.max(jnp.abs(rows))
        spread = jnp.full((8, LANES), largest, jnp.float32)
        scale = ((spread + tiny_eps) / scale_top).astype(jnp.bfloat16).astype(jnp.float32)
        factor = scale[:1, :1]
        stored = (rows / factor).astype(jnp.bfloat16)
        block[...] = (stored.astype(jnp.float32) * factor).astype(jnp.bfloat16)

    @pl.when(section == 1)
    def _():
        block[...] = own_in[...]

    pl.semaphore_wait(barrier, len(peers))

    def send(src, dst, to, send_sem, recv_sem):
        copy = pltpu.make_async_remote_copy(
            src_ref=src,
            dst_ref=dst,
            send_sem=send_sem,
            recv_sem=recv_sem,
            device_id=to,
            device_id_type=pl.DeviceIdType.MESH,
        )
        copy.start()
        return copy

    def arrive(dst, recv_sem):
        pltpu.make_async_remote_copy(
            src_ref=dst,
            dst_ref=dst,
            send_sem=recv_sem,
            recv_sem=recv_sem,
            device_id=device(to_core=1 - core),
            device_id_type=pl.DeviceIdType.MESH,
        ).wait_recv()

    own_local = pltpu.make_async_copy(block, own_out.at[core], own_sems.at[0])
    own_local.start()
    own_away = send(
        block, own_out.at[core], device(to_core=1 - core), own_sems.at[1], own_sems.at[2]
    )

    @pl.when(section == 0)
    def _():
        spot = keys.at[z, y, hi, core]
        local = pltpu.make_async_copy(block, spot, mine_sem)
        local.start()
        went = [
            send(block, spot, device(to_section=1), x_send.at[0], x_recv.at[0]),
            send(block, spot, device(to_section=1, to_hi=1 - hi), x_send.at[1], x_recv.at[1]),
            send(block, spot, device(to_hi=1 - hi), x_send.at[2], x_recv.at[1]),
        ]
        local.wait()
        arrive(keys.at[z, y, 1 - hi, core], x_recv.at[1])
        for copy in went:
            copy.wait_send()

    @pl.when(section == 1)
    def _():
        arrive(keys.at[z, y, hi, core], x_recv.at[0])
        arrive(keys.at[z, y, 1 - hi, core], x_recv.at[1])

    half = z_count // 2

    @pl.when(core == 0)
    def _():
        c = 0
        went = [
            send(keys.at[z, y, :, c], keys.at[z, y, :, c], device(dy=1), y_send.at[0, 0], y_recv.at[0, 0]),
            send(keys.at[z, y, :, c], keys.at[z, y, :, c], device(dy=-1), y_send.at[0, 1], y_recv.at[0, 1]),
        ]
        _, low = place(0, -1)
        _, high = place(0, 1)
        _, far = place(0, 2)
        arrive(keys.at[z, low, :, c], y_recv.at[0, 0])
        went.append(
            send(keys.at[z, low, 0, c], keys.at[z, low, 0, c], device(dy=1), y_send.at[0, 2], y_recv.at[0, 2])
        )
        arrive(keys.at[z, high, :, c], y_recv.at[0, 1])
        went.append(
            send(keys.at[z, high, 1, c], keys.at[z, high, 1, c], device(dy=-1), y_send.at[0, 3], y_recv.at[0, 3])
        )
        arrive(keys.at[z, far, 0, c], y_recv.at[0, 2])
        arrive(keys.at[z, far, 1, c], y_recv.at[0, 3])

        def plane(at):
            return keys.at[at, :, :, c]

        def ahead(at, step, up):
            d = 1 if up else -1
            if step < half - 1:
                part = plane(at)
            else:
                part = keys.at[at, pl.ds(0 if up else y_count // 2, y_count // 2), :, c]
            j = 0 if up else 1
            went.append(send(part, part, device(dz=d), z_send.at[j, step], z_recv.at[j, step]))

        def to_sibling(at, n):
            went.append(
                send(plane(at), plane(at), device(to_core=1), sib_send.at[n], sib_recv.at[n])
            )

        ahead(z, 0, True)
        ahead(z, 0, False)
        to_sibling(z, 0)
        for s in range(1, half):
            below, _ = place(-s, 0)
            above, _ = place(s, 0)
            arrive(plane(below), z_recv.at[0, s - 1])
            ahead(below, s, True)
            arrive(plane(above), z_recv.at[1, s - 1])
            ahead(above, s, False)
            to_sibling(below, 2 * s - 1)
            to_sibling(above, 2 * s)
        across, _ = place(half, 0)
        arrive(keys.at[across, pl.ds(0, y_count // 2), :, c], z_recv.at[0, half - 1])
        arrive(keys.at[across, pl.ds(y_count // 2, y_count // 2), :, c], z_recv.at[1, half - 1])
        to_sibling(across, z_count - 1)
        for copy in went:
            copy.wait_send()

    @pl.when(core == 1)
    def _():
        c = 1
        went = []
        planes = [place(0, 0)[0]]
        for s in range(1, half):
            planes += [place(-s, 0)[0], place(s, 0)[0]]
        planes.append(place(half, 0)[0])
        _, low = place(0, -1)
        _, high = place(0, 1)
        _, far = place(0, 2)

        def ahead(at, step, up):
            d = 1 if up else -1
            j = 0 if up else 1
            if step < half - 1:
                part = keys.at[at, y, :, c]
            else:
                part = keys.at[at, y, 0 if up else 1, c]
            went.append(send(part, part, device(dz=d), z_send.at[j, step], z_recv.at[j, step]))

        def spread(n):
            part = keys.at[planes[n], y, :, c]
            went.append(send(part, part, device(dy=1), y_send.at[n, 0], y_recv.at[n, 0]))
            went.append(send(part, part, device(dy=-1), y_send.at[n, 1], y_recv.at[n, 1]))

        def spread_on(n):
            at = planes[n]
            arrive(keys.at[at, low, :, c], y_recv.at[n, 0])
            part = keys.at[at, low, 0, c]
            went.append(send(part, part, device(dy=1), y_send.at[n, 2], y_recv.at[n, 2]))
            arrive(keys.at[at, high, :, c], y_recv.at[n, 1])
            part = keys.at[at, high, 1, c]
            went.append(send(part, part, device(dy=-1), y_send.at[n, 3], y_recv.at[n, 3]))

        def finish(n):
            at = planes[n]
            arrive(keys.at[at, far, 0, c], y_recv.at[n, 2])
            arrive(keys.at[at, far, 1, c], y_recv.at[n, 3])
            part = keys.at[at, :, :, c]
            went.append(send(part, part, device(to_core=0), sib_send.at[n], sib_recv.at[n]))

        ahead(planes[0], 0, True)
        ahead(planes[0], 0, False)
        spread(0)
        for s in range(1, half):
            arrive(keys.at[planes[2 * s - 1], y, :, c], z_recv.at[0, s - 1])
            ahead(planes[2 * s - 1], s, True)
            arrive(keys.at[planes[2 * s], y, :, c], z_recv.at[1, s - 1])
            ahead(planes[2 * s], s, False)
            spread(2 * s - 1)
            spread(2 * s)
        arrive(keys.at[planes[-1], y, 0, c], z_recv.at[0, half - 1])
        arrive(keys.at[planes[-1], y, 1, c], z_recv.at[1, half - 1])
        spread(z_count - 1)
        for n in range(z_count):
            spread_on(n)
            if n >= 1:
                finish(n - 1)
        finish(z_count - 1)
        for copy in went:
            copy.wait_send()

    other = 1 - core
    order = [place(0, 0)[0]]
    for s in range(1, half):
        order += [place(-s, 0)[0], place(s, 0)[0]]
    order.append(place(half, 0)[0])
    for n, at in enumerate(order):
        arrive(keys.at[at, :, :, other], sib_recv.at[n])
    arrive(own_out.at[other], own_sems.at[2])
    own_away.wait_send()
    own_local.wait()


def gathered(own, seq_count):
    rows, width = own.shape
    y_count = 4
    z_count = seq_count // (2 * y_count)
    dma = pltpu.SemaphoreType.DMA
    keys, pair = pl.pallas_call(
        functools.partial(gather_kernel, z_count, y_count),
        out_shape=[
            jax.ShapeDtypeStruct((z_count, y_count, 2, 2, rows, width), own.dtype),
            jax.ShapeDtypeStruct((2, rows, width), own.dtype),
        ],
        in_specs=[pl.BlockSpec(memory_space=pltpu.VMEM)],
        out_specs=[pl.BlockSpec(memory_space=pl.ANY), pl.BlockSpec(memory_space=pl.ANY)],
        scratch_shapes=[
            pltpu.VMEM((rows, width), own.dtype),
            dma(()),
            dma((3,)),
            dma((2,)),
            dma((3,)),
            dma((2, z_count // 2)),
            dma((2, z_count // 2)),
            dma((z_count, 4)),
            dma((z_count, 4)),
            dma((z_count,)),
            dma((z_count,)),
        ],
        compiler_params=pltpu.CompilerParams(collective_id=0, has_side_effects=True),
    )(own)
    return keys.reshape(-1, width), pair.reshape(-1, width)


def token_start(positions, starts):
    return jnp.max(jnp.where(starts[None, :] <= positions[:, None], starts[None, :], 0), axis=1)


def over_lanes(value, width):
    return jnp.concatenate([value] * (width // LANES), axis=1)


def flash_kernel(
    kv_rank,
    exponent_scale,
    plan,
    q_ref,
    keys,
    own_keys,
    low_ref,
    bias_ref,
    out_ref,
    acc,
    top,
    total,
    held,
    sems,
):
    band = pl.program_id(0)
    heads, tokens, width = q_ref.shape
    rows = heads * tokens
    all_keys = keys.shape[0]
    first, full_from, last = (plan[i, band] for i in range(3))
    chunks = (last - first + KEY_BLOCK - 1) // KEY_BLOCK

    def chunk_at(i):
        return pl.multiple_of(jnp.minimum(first + i * KEY_BLOCK, all_keys - KEY_BLOCK), 16)

    def fetch(i):
        slot = lax.rem(i, 2)
        return pltpu.make_async_copy(
            keys.at[pl.ds(chunk_at(i), KEY_BLOCK), :], held.at[slot], sems.at[slot]
        )

    @pl.when(chunks > 0)
    def _():
        fetch(0).start()

    q = q_ref[...].reshape(rows, width)
    own = own_keys[...]
    nt = (((1,), (1,)), ((), ()))

    scores = lax.dot_general(q, own, nt, preferred_element_type=jnp.float32)
    bias = jnp.broadcast_to(bias_ref[...][None], (heads, tokens, tokens)).reshape(rows, tokens)
    scores = scores + bias
    own_top = jnp.max(scores, axis=1, keepdims=True)
    expo = jnp.exp2((scores - own_top) * exponent_scale)
    lane = lax.broadcasted_iota(jnp.int32, (rows, LANES), 1)
    total[...] = jnp.where(lane == 0, jnp.sum(expo, axis=1, keepdims=True), 0.0)
    top[...] = jnp.broadcast_to(own_top, (rows, LANES))
    acc[...] = jnp.dot(
        expo.astype(jnp.bfloat16), own[:, :kv_rank], preferred_element_type=jnp.float32
    )

    def fold(key_block, low_spot, at):
        count = key_block.shape[0]
        s = lax.dot_general(q, key_block, nt, preferred_element_type=jnp.float32)
        if low_spot is not None:
            low = jnp.broadcast_to(low_ref[...][None], (heads, tokens, 1)).reshape(rows, 1)
            spot = at + lax.broadcasted_iota(jnp.int32, (1, count), 1)
            s = jnp.where((spot >= jnp.maximum(low, low_spot)) & (spot < last), s, masked_low)
        before = top[...]
        now = jnp.maximum(before, jnp.max(s, axis=1, keepdims=True))
        shrink = jnp.exp2((before - now) * exponent_scale)
        expo = jnp.exp2((s - over_lanes(now, count)) * exponent_scale)
        top[...] = now
        summed = total[...] * shrink
        for c in range(0, count, LANES):
            summed = summed + expo[:, c : c + LANES]
        total[...] = summed
        acc[...] = acc[...] * over_lanes(shrink, kv_rank) + jnp.dot(
            expo.astype(jnp.bfloat16), key_block[:, :kv_rank], preferred_element_type=jnp.float32
        )

    @pl.loop(0, chunks)
    def _(i):
        slot = lax.rem(i, 2)
        fetch(i).wait()

        @pl.when(i + 1 < chunks)
        def _():
            fetch(i + 1).start()

        nominal = first + i * KEY_BLOCK
        at = chunk_at(i)
        whole = (nominal >= full_from) & (nominal + KEY_BLOCK <= last)

        @pl.when(whole)
        def _():
            fold(held[slot], None, None)

        @pl.when(jnp.logical_not(whole))
        def _():
            skip = (nominal - at) // EDGE_BLOCK

            @pl.loop(skip, (jnp.minimum(last - at, KEY_BLOCK) + EDGE_BLOCK - 1) // EDGE_BLOCK)
            def _(j):
                here = pl.multiple_of(j * EDGE_BLOCK, EDGE_BLOCK)
                fold(held[slot, pl.ds(here, EDGE_BLOCK), :], nominal, at + here)

    norm = 1.0 / jnp.sum(total[...], axis=1, keepdims=True)
    out_ref[...] = (acc[...] * norm).astype(jnp.bfloat16).reshape(heads, tokens, kv_rank)


def shards(query_nope, query_rope, latent, up_key, value_up_weight, lengths, owner_request_table):
    section_index = lax.axis_index("section")
    owner_index = lax.axis_index("seq")
    is_prefill = section_index == 0
    seq_count = lax.axis_size("seq")
    tok_dev, head_dev, nope_dim = query_nope.shape[1:]
    rope_dim = query_rope.shape[2] // head_dev
    kv_rank = up_key.shape[1]
    width = kv_rank + rope_dim
    req_dev = owner_request_table.shape[0] // seq_count
    groups = owner_request_table.shape[0] // lengths.shape[0]
    band_tokens = tok_dev // req_dev
    exponent_scale = math.log2(math.e) / math.sqrt(nope_dim + rope_dim)

    keys, own_keys = gathered(latent[0], seq_count)

    lifted = jnp.einsum("thn,hkn->htk", query_nope[0], up_key, preferred_element_type=jnp.float32)
    rope_part = query_rope[0].reshape(tok_dev, head_dev, rope_dim).swapaxes(0, 1)
    queries = jnp.concatenate([lifted.astype(jnp.bfloat16), rope_part], axis=2)

    prompt_ends = jnp.cumsum(lengths)
    starts = prompt_ends - lengths
    positions = owner_index * tok_dev + jnp.arange(tok_dev, dtype=jnp.int32)
    prefill_low = token_start(positions, starts)
    band_at = owner_index * tok_dev + band_tokens * jnp.arange(req_dev, dtype=jnp.int32)
    own_requests = (
        lax.dynamic_slice_in_dim(owner_request_table, owner_index * req_dev, req_dev, 0) // groups
    )
    chosen = own_requests[:, None] == jnp.arange(lengths.shape[0], dtype=jnp.int32)[None, :]
    slot_low = jnp.sum(jnp.where(chosen, starts[None, :], 0), axis=1)
    slot_high = jnp.sum(jnp.where(chosen, prompt_ends[None, :], 0), axis=1)
    row_low = jnp.where(is_prefill, prefill_low, jnp.repeat(slot_low, band_tokens))
    by_band = row_low.reshape(req_dev, band_tokens)
    last = jnp.where(is_prefill, jnp.maximum(band_at, by_band[:, 0]), slot_high)
    first = jnp.minimum(by_band[:, 0], last) // 16 * 16
    highest_low = jnp.minimum(by_band[:, -1], last)
    plan = jnp.stack([first, highest_low, last]).astype(jnp.int32)

    here = jnp.arange(band_tokens, dtype=jnp.int32)
    same_sample = here[None, :] % SAMPLES == here[:, None] % SAMPLES
    earlier_step = here[None, :] // SAMPLES <= here[:, None] // SAMPLES
    decode_seen = jnp.broadcast_to(
        (same_sample & earlier_step)[None], (req_dev, band_tokens, band_tokens)
    )
    prefill_seen = (here[None, None, :] <= here[None, :, None]) & (
        band_at[:, None, None] + here[None, None, :] >= by_band[:, :, None]
    )
    seen = jnp.where(is_prefill, prefill_seen, decode_seen)
    bias = jnp.where(seen, 0.0, masked_low).astype(jnp.float32).reshape(tok_dev, band_tokens)

    rows = head_dev * band_tokens
    latent_out = pl.pallas_call(
        functools.partial(flash_kernel, kv_rank, exponent_scale),
        out_shape=jax.ShapeDtypeStruct((head_dev, tok_dev, kv_rank), jnp.bfloat16),
        grid_spec=pltpu.PrefetchScalarGridSpec(
            num_scalar_prefetch=1,
            grid=(req_dev,),
            in_specs=[
                pl.BlockSpec((head_dev, band_tokens, width), lambda i, s: (0, i, 0)),
                pl.BlockSpec(memory_space=pl.ANY),
                pl.BlockSpec((band_tokens, width), lambda i, s: (i, 0)),
                pl.BlockSpec((band_tokens, 1), lambda i, s: (i, 0)),
                pl.BlockSpec((band_tokens, band_tokens), lambda i, s: (i, 0)),
            ],
            out_specs=pl.BlockSpec((head_dev, band_tokens, kv_rank), lambda i, s: (0, i, 0)),
            scratch_shapes=[
                pltpu.VMEM((rows, kv_rank), jnp.float32),
                pltpu.VMEM((rows, LANES), jnp.float32),
                pltpu.VMEM((rows, LANES), jnp.float32),
                pltpu.VMEM((2, KEY_BLOCK, width), jnp.bfloat16),
                pltpu.SemaphoreType.DMA((2,)),
            ],
        ),
        compiler_params=pltpu.CompilerParams(vmem_limit_bytes=48 << 20),
    )(plan, queries, keys, own_keys, row_low[:, None], bias)

    attended = jnp.einsum(
        "htk,hkv->thv", latent_out, value_up_weight, preferred_element_type=jnp.float32
    )
    return attended.astype(jnp.bfloat16)[None]


def solution(mesh):
    in_specs = (
        P("section", "seq", "head", None),
        P("section", "seq", "head"),
        P("section", ("seq", "head"), None),
        P("head", None, None),
        P("head", None, None),
        P(),
        P(),
    )
    out_specs = P("section", "seq", "head", None)
    return jax.shard_map(shards, mesh=mesh, in_specs=in_specs, out_specs=out_specs, check_vma=False)
```

time: 250 us -> 143 us (0.57)
  the two profiles are of different devices: /device:TPU:245 before, /device:TPU:133 now
where the time goes in v1:
time: 143 us; the launch traced here: 142 us
  Pallas kernels  126 us (88%)
  local copies, waits for them, and re-layouts  5.8 us (4%)
  other arithmetic  5.43 us (4%)
  matrix products  5.02 us (4%)
    pallas_call x1, Pallas kernels, shards(): pl.pallas_call(functools.partial(flash_kernel, kv_rank, exponent_scale),...  66.8 us
    pallas_call x1, Pallas kernels, gathered(): pl.pallas_call(functools.partial(gather_kernel, z_count, y_count), out_sh...  59.1 us
    dot_general x1, matrix products, shards(): jnp.einsum('thn,hkn->htk', query_nope[0], up_key, preferred_element_type=...  3.77 us
    concatenate x1, other arithmetic, shards(): queries = jnp.concatenate([lifted.astype(jnp.bfloat16), rope_part], axis=2)  3.2 us

profile of v1, /device:TPU:133, one launch (start us, length us, event | category | flops | bytes accessed | tf_op | source)
XLA Modules:
  0.0 142.2 jit_solution(3457864648070844160)
XLA Ops:
  0.0 0.8 and_select_fusion.3
  0.8 0.1 iota_add_fusion
  0.9 0.1 compare_and_fusion
  0.9 0.7 copy.18
  1.7 0.1 reduce-window.8
  1.7 0.1 reduce
  1.9 0.7 sub.20
  2.5 0.1 select_reduce_fusion
  2.6 0.2 select_reduce_fusion.1
  2.8 0.1 broadcast_in_dim.71
  2.9 0.1 broadcast_in_dim.73
  3.0 0.1 reduce_max.14
  3.0 0.1 broadcast_select_fusion.1
  3.1 0.2 slice_reduce_fusion
  3.4 0.1 fusion.4.bias_ref
  3.4 0.1 reshape.391
  3.6 0.1 copy.22
  3.7 1.3 copy.20
  5.0 0.5 copy.21
  5.6 3.8 %convolution_convert_fusion = bf16[32,128,512]{2,1,0:T(8,128)(2,1)S(1)} fusion(bf16[32,512,128]{2,1,0:T(8,128)(2,1)} %param.10, bf16[128,32,128]{2,1,0:T(8,128)(2,1)} %bitcast.46), kind=kOutput, calls=%fused_computation.1 | convolution fusion | flops 538968064 | bytes 9437184 | tf_op jit(solution)/shard_map/thn,hkn->htk/dot_general | solution.py:416
  9.3 3.2 %pad_maximum_fusion.q_ref = bf16[32,128,576]{2,1,0:T(8,128)(2,1)} fusion(bf16[32,128,64]{2,1,0:T(8,128)(2,1)S(1)} %bitcast.44, bf16[32,128,512]{2,1,0:T(8,128)(2,1)S(1)} %convolution_convert_fusion), kind=kLoop, calls=%fused_computation | loop fusion | flops 9437184 | bytes 9437184 | tf_op jit(solution)/shard_map/concatenate | solution.py:418
  12.5 59.1 %shard_map.73 = (bf16[8,4,2,2,64,576]{5,4,3,2,1,0:T(8,128)(2,1)}, bf16[2,64,576]{2,1,0:T(8,128)(2,1)}) custom-call(bf16[64,576]{1,0:T(8,128)(2,1)} %bitcast.47), custom_call_target="tpu_custom_call" | custom-call | tf_op jit(solution)/shard_map/pallas_call | solution.py:264
  71.6 0.0 copy-start
  71.6 0.9 copy-done
  72.5 0.0 copy-start.1
  72.5 66.8 %shard_map.74 = bf16[32,128,512]{2,1,0:T(8,128)(2,1)S(1)} custom-call(s32[3,4]{1,0:T(4,128)S(1)} %pad_add_fusion.plan, bf16[32,128,576]{2,1,0:T(8,128)(2,1)} %pad_maximum_fusion.q_ref, bf16[8192,576]{1,0:T(8,128)(2,1)} %bitcast.43, bf16[128,576]{1,0:T(8,128)(2,1)S(1)} %bitcast.42, s32[128,1]{1,0:T(8,128)S(1)} %broadcast_select_fusion.low_ref, ...), custom_call_target="tpu_custom_call" | custom-call | tf_op jit(solution)/shard_map/pallas_call | solution.py:451
  139.3 0.0 copy-done.1
  139.3 1.2 fusion
  140.6 1.6 %copy.24 = bf16[1,128,32,128]{3,2,1,0:T(8,128)(2,1)} copy(bf16[1,128,32,128]{3,1,2,0:T(8,128)(2,1)S(1)} %fusion) | data formatting | bytes 2097152 | tf_op jit(solution)/shard_map/broadcast_in_dim | solution.py:479
  (9 shorter events, 0.1 us)
Async XLA Ops:
  71.6 0.9 copy-start
  72.5 66.8 %copy-start.1 = (bf16[32,512,128]{2,1,0:T(8,128)(2,1)S(1)}, bf16[32,512,128]{2,1,0:T(8,128)(2,1)}, u32[]{:S(2)}) copy-start(bf16[32,512,128]{2,1,0:T(8,128)(2,1)} %param.11) | copy-start | bytes 12582916

commit v2 on v0

v2 whole, which is shorter than its diff:
```python
import functools
import math

import jax
import jax.numpy as jnp
from jax import lax
from jax.experimental import pallas as pl
from jax.experimental.pallas import tpu as pltpu
from jax.sharding import PartitionSpec as P

SAMPLES = 8
STEPS = 4
BLOCK = 64

scale_top = 448.0
tiny_eps = 1e-06
masked_low = -1e30

KEY_BLOCK = 1024
EDGE_BLOCK = 512
LANES = 128


def prefill_kernel(
    z_count, y_count, kv_rank, exponent_scale, own_in, q_nope, q_rope, up_key, lengths,
    keys, own_out, q_out, latent_out, block, nope, up, q, acc, top, total, held, bias,
    in_sems, out_sems, held_sems, x_send, x_recv, own_sems,
    z_send, z_recv, y_send, y_recv, sib_send, sib_recv,
):
    section = lax.axis_index("section")
    seq = lax.axis_index("seq")
    core = lax.axis_index("head")
    z = seq // (2 * y_count)
    y = seq // 2 % y_count
    hi = seq % 2
    half = z_count // 2
    heads, tokens, width = q.shape
    plane_blocks = 2 * y_count
    at_block = seq % plane_blocks
    plane_keys = plane_blocks * tokens
    nt = (((1,), (1,)), ((), ()))

    def plane_at(dz):
        return lax.rem(z + dz + z_count, z_count)

    def row_at(dy):
        return lax.rem(y + dy + y_count, y_count)

    def device(dz=0, dy=0, to_hi=None, to_section=None, to_core=None):
        th = hi if to_hi is None else to_hi
        return (
            section if to_section is None else to_section,
            (plane_at(dz) * y_count + row_at(dy)) * 2 + th,
            core if to_core is None else to_core,
        )

    loads = [
        pltpu.make_async_copy(q_nope, nope, in_sems.at[0]),
        pltpu.make_async_copy(up_key, up, in_sems.at[1]),
    ]
    for load in loads:
        load.start()

    barrier = pltpu.get_barrier_semaphore()
    peers = [
        device(to_core=1 - core),
        device(to_section=1 - section),
        device(to_hi=1 - hi),
        device(to_section=1 - section, to_hi=1 - hi),
        device(dz=1),
        device(dz=-1),
        device(dy=1),
        device(dy=-1),
    ]
    for peer in peers:
        pl.semaphore_signal(barrier, inc=1, device_id=peer, device_id_type=pl.DeviceIdType.MESH)

    @pl.when(section == 0)
    def _():
        rows = own_in[...].astype(jnp.float32)
        largest = jnp.max(jnp.abs(rows))
        spread = jnp.full((8, LANES), largest, jnp.float32)
        scale = ((spread + tiny_eps) / scale_top).astype(jnp.bfloat16).astype(jnp.float32)
        factor = scale[:1, :1]
        stored = (rows / factor).astype(jnp.bfloat16)
        block[...] = (stored.astype(jnp.float32) * factor).astype(jnp.bfloat16)

    @pl.when(section == 1)
    def _():
        block[...] = own_in[...]

    pl.semaphore_wait(barrier, len(peers))

    def remote(src, dst, to, send_sem, recv_sem):
        return pltpu.make_async_remote_copy(
            src_ref=src,
            dst_ref=dst,
            send_sem=send_sem,
            recv_sem=recv_sem,
            device_id=to,
            device_id_type=pl.DeviceIdType.MESH,
        )

    def arrive(dst, recv_sem):
        remote(dst, dst, device(to_core=1 - core), recv_sem, recv_sem).wait_recv()

    def own_local():
        return pltpu.make_async_copy(block, own_out.at[core], own_sems.at[0])

    def own_away():
        to = device(to_core=1 - core)
        return remote(block, own_out.at[core], to, own_sems.at[1], own_sems.at[2])

    def x_copies():
        spot = keys.at[z, y, hi, core]
        return [
            remote(block, spot, device(to_section=1), x_send.at[0], x_recv.at[0]),
            remote(block, spot, device(to_hi=1 - hi), x_send.at[2], x_recv.at[1]),
            remote(block, spot, device(to_section=1, to_hi=1 - hi), x_send.at[1], x_recv.at[1]),
        ]

    def x_local():
        return pltpu.make_async_copy(block, keys.at[z, y, hi, core], x_send.at[3])

    @pl.when(section == 0)
    def _():
        x_local().start()
        for copy in x_copies():
            copy.start()

    own_local().start()
    own_away().start()

    for load in loads:
        load.wait()

    @pl.loop(0, heads // 2)
    def _(pair):
        rope = q_rope[:, pl.ds(pl.multiple_of(pair * LANES, LANES), LANES)]
        for side in range(2):
            head = pair * 2 + side
            lifted = lax.dot_general(nope[head], up[head], nt, preferred_element_type=jnp.float32)
            q[head, :, :kv_rank] = lifted.astype(jnp.bfloat16)
            q[head, :, kv_rank:] = rope[:, side * (LANES // 2) : (side + 1) * (LANES // 2)]

    @pl.when(section == 1)
    def _():
        pltpu.make_async_copy(q, q_out, out_sems.at[0]).start()

    @pl.when(section == 0)
    def _():
        x_local().wait()
        arrive(keys.at[z, y, 1 - hi, core], x_recv.at[1])

    @pl.when(section == 1)
    def _():
        arrive(keys.at[z, y, hi, core], x_recv.at[0])
        arrive(keys.at[z, y, 1 - hi, core], x_recv.at[1])

    low, high, far = row_at(-1), row_at(1), row_at(2)
    planes = [z]
    for s in range(1, half):
        planes += [plane_at(-s), plane_at(s)]
    planes.append(plane_at(half))
    steps = [[0]] + [[2 * s - 1, 2 * s] for s in range(1, half)] + [[z_count - 1]]

    a_went = []

    def a_send(src, to, send_sem, recv_sem):
        copy = lambda: remote(src(), src(), to(), send_sem(), recv_sem())
        a_went.append(copy)
        copy().start()

    def a_plane(n):
        return lambda: keys.at[planes[n], :, :, 0]

    def a_ahead(n, step, up_way):
        d, j = (1, 0) if up_way else (-1, 1)
        part = a_plane(n)
        if step == half - 1:
            part = lambda: keys.at[planes[n], pl.ds(j * (y_count // 2), y_count // 2), :, 0]
        a_send(
            part, lambda: device(dz=d), lambda: z_send.at[j, step], lambda: z_recv.at[j, step]
        )

    def a_sibling(n):
        a_send(
            a_plane(n), lambda: device(to_core=1), lambda: sib_send.at[n], lambda: sib_recv.at[n]
        )

    def a_y(src, d, k):
        a_send(src, lambda: device(dy=d), lambda: y_send.at[0, k], lambda: y_recv.at[0, k])

    def a_start():
        mine = lambda: keys.at[z, y, :, 0]
        a_y(mine, 1, 0)
        a_y(mine, -1, 1)
        arrive(keys.at[z, low, :, 0], y_recv.at[0, 0])
        a_y(lambda: keys.at[z, low, 0, 0], 1, 2)
        arrive(keys.at[z, high, :, 0], y_recv.at[0, 1])
        a_y(lambda: keys.at[z, high, 1, 0], -1, 3)
        arrive(keys.at[z, far, 0, 0], y_recv.at[0, 2])
        arrive(keys.at[z, far, 1, 0], y_recv.at[0, 3])
        a_ahead(0, 0, True)
        a_ahead(0, 0, False)
        a_sibling(0)

    def a_point(s):
        if s < half:
            below, above = steps[s]
            arrive(a_plane(below)(), z_recv.at[0, s - 1])
            a_ahead(below, s, True)
            arrive(a_plane(above)(), z_recv.at[1, s - 1])
            a_ahead(above, s, False)
            a_sibling(below)
            a_sibling(above)
        else:
            for j in range(2):
                part = keys.at[planes[-1], pl.ds(j * (y_count // 2), y_count // 2), :, 0]
                arrive(part, z_recv.at[j, half - 1])
            a_sibling(z_count - 1)

    b_went = []

    def b_send(src, to, send_sem, recv_sem):
        copy = lambda: remote(src(), src(), to(), send_sem(), recv_sem())
        b_went.append(copy)
        copy().start()

    def b_ahead(n, step, up_way):
        d, j = (1, 0) if up_way else (-1, 1)
        if step < half - 1:
            part = lambda: keys.at[planes[n], y, :, 1]
        else:
            part = lambda: keys.at[planes[n], y, j, 1]
        b_send(
            part, lambda: device(dz=d), lambda: z_send.at[j, step], lambda: z_recv.at[j, step]
        )

    def b_y(src, d, n, k):
        b_send(src, lambda: device(dy=d), lambda: y_send.at[n, k], lambda: y_recv.at[n, k])

    def b_spread(n):
        b_y(lambda: keys.at[planes[n], y, :, 1], 1, n, 0)
        b_y(lambda: keys.at[planes[n], y, :, 1], -1, n, 1)

    def b_spread_on(n):
        arrive(keys.at[planes[n], low, :, 1], y_recv.at[n, 0])
        b_y(lambda: keys.at[planes[n], low, 0, 1], 1, n, 2)
        arrive(keys.at[planes[n], high, :, 1], y_recv.at[n, 1])
        b_y(lambda: keys.at[planes[n], high, 1, 1], -1, n, 3)

    def b_finish(n):
        arrive(keys.at[planes[n], far, 0, 1], y_recv.at[n, 2])
        arrive(keys.at[planes[n], far, 1, 1], y_recv.at[n, 3])
        b_send(
            lambda: keys.at[planes[n], :, :, 1],
            lambda: device(to_core=0),
            lambda: sib_send.at[n],
            lambda: sib_recv.at[n],
        )

    def b_chain(s):
        if s < half:
            below, above = steps[s]
            arrive(keys.at[planes[below], y, :, 1], z_recv.at[0, s - 1])
            b_ahead(below, s, True)
            arrive(keys.at[planes[above], y, :, 1], z_recv.at[1, s - 1])
            b_ahead(above, s, False)
        else:
            arrive(keys.at[planes[-1], y, 0, 1], z_recv.at[0, half - 1])
            arrive(keys.at[planes[-1], y, 1, 1], z_recv.at[1, half - 1])
        for n in steps[s]:
            b_spread(n)

    def b_start():
        b_ahead(0, 0, True)
        b_ahead(0, 0, False)
        b_spread(0)
        b_spread_on(0)
        b_chain(1)
        b_finish(0)

    def b_point(s):
        for n in steps[s]:
            b_spread_on(n)
        if s < half:
            b_chain(s + 1)
        for n in steps[s]:
            b_finish(n)

    def point(s):
        @pl.when(core == 0)
        def _():
            a_start() if s == 0 else a_point(s)

        @pl.when(core == 1)
        def _():
            b_start() if s == 0 else b_point(s)

    def from_sibling(s):
        for n in steps[s]:
            arrive(keys.at[planes[n], :, :, 1 - core], sib_recv.at[n])

    @pl.when(section == 0)
    def _():
        top[...] = jnp.full(top.shape, masked_low, jnp.float32)
        total[...] = jnp.zeros(total.shape, jnp.float32)
        acc[...] = jnp.zeros(acc.shape, jnp.float32)

    token = lax.broadcasted_iota(jnp.int32, (tokens, 1), 0)
    position = seq * tokens + token
    count = lengths.shape[0]
    before_it = lax.broadcasted_iota(jnp.int32, (count, count), 0) < lax.broadcasted_iota(
        jnp.int32, (count, count), 1
    )
    starts = jnp.sum(
        jnp.where(before_it, lengths[...].astype(jnp.float32), 0.0), axis=0, keepdims=True
    )
    row_low = jnp.max(
        jnp.where(starts <= position.astype(jnp.float32), starts, 0.0), axis=1, keepdims=True
    ).astype(jnp.int32)

    chunk = plane_keys // 2
    tile_heads = 8
    rows = tile_heads * tokens

    def fold(first_spot, side):
        spot = first_spot + lax.broadcasted_iota(jnp.int32, (1, chunk), 1)
        seen = (spot >= row_low) & (spot <= position)
        bias[...] = jnp.where(seen, 0.0, masked_low)

        @pl.loop(0, heads // tile_heads)
        def _(tile):
            part = pl.ds(pl.multiple_of(tile * rows, rows), rows)
            asked = q[pl.ds(tile * tile_heads, tile_heads)].reshape(rows, width)
            s = lax.dot_general(asked, held[side].reshape(chunk, width), nt, preferred_element_type=jnp.float32)
            s = (s.reshape(tile_heads, tokens, chunk) + bias[...][None]).reshape(rows, chunk)
            before = top[part, :]
            now = jnp.maximum(before, jnp.max(s, axis=1, keepdims=True))
            shrink = jnp.exp2((before - now) * exponent_scale)
            expo = jnp.exp2((s - over_lanes(now, chunk)) * exponent_scale)
            top[part, :] = now
            summed = total[part, :] * shrink
            for c in range(0, chunk, LANES):
                summed = summed + expo[:, c : c + LANES]
            total[part, :] = summed
            acc[part, :] = acc[part, :] * over_lanes(shrink, kv_rank) + jnp.dot(
                expo.astype(jnp.bfloat16),
                held[side].reshape(chunk, width)[:, :kv_rank],
                preferred_element_type=jnp.float32,
            )

    @pl.loop(0, 2 * half + 3)
    def _(i):
        for s in range(half + 1):

            @pl.when(i == max(2 * s - 1, 0))
            def _():
                point(s)

            @pl.when(i == 2 * s)
            def _():
                from_sibling(s)

        back = i // 2
        last_step = i == 2 * half + 2
        side = jnp.where(last_step, 1, i % 2)
        plane = lax.rem(z - back + z_count, z_count)
        reached = (section == 0) & (z >= back)
        reached = reached & (jnp.logical_not(last_step) | (at_block == 0))

        def load(part):
            here = keys.at[plane, pl.ds(part * (y_count // 2), y_count // 2)]
            return pltpu.make_async_copy(here, held.at[part], held_sems.at[part])

        @pl.when(reached & (i % 2 == 0) & jnp.logical_not(last_step))
        def _():
            load(0).start()
            load(1).start()

        @pl.when(reached & last_step)
        def _():
            load(1).start()

        @pl.when(reached)
        def _():
            load(side).wait()

        needed = reached & ((i != 1) | (at_block >= plane_blocks // 2))
        needed = needed & ((i != 2 * half) | (at_block <= plane_blocks // 2))

        @pl.when(needed)
        def _():
            fold((z - back) * plane_keys + side * chunk, side)

    @pl.when(section == 0)
    def _():
        @pl.loop(0, heads)
        def _(head):
            part = pl.ds(pl.multiple_of(head * tokens, tokens), tokens)
            norm = 1.0 / jnp.sum(total[part, :], axis=1, keepdims=True)
            q[head, :, :kv_rank] = (acc[part, :] * norm).astype(jnp.bfloat16)

        done = pltpu.make_async_copy(q.at[:, :, pl.ds(0, kv_rank)], latent_out, out_sems.at[1])
        done.start()
        done.wait()
        for copy in x_copies():
            copy.wait_send()

    @pl.when(section == 1)
    def _():
        pltpu.make_async_copy(q, q_out, out_sems.at[0]).wait()

    @pl.when(core == 0)
    def _():
        for copy in a_went:
            copy().wait_send()

    @pl.when(core == 1)
    def _():
        for copy in b_went:
            copy().wait_send()

    arrive(own_out.at[1 - core], own_sems.at[2])
    own_away().wait_send()
    own_local().wait()


def prefill_part(own, q_nope, q_rope, up_key, lengths, seq_count, exponent_scale):
    rows, width = own.shape
    heads, tokens, _ = q_nope.shape
    kv_rank = up_key.shape[1]
    y_count = 4
    z_count = seq_count // (2 * y_count)
    dma = pltpu.SemaphoreType.DMA
    bf16 = own.dtype
    chunk = y_count * tokens
    vmem = pl.BlockSpec(memory_space=pltpu.VMEM)
    hbm = pl.BlockSpec(memory_space=pl.ANY)
    return pl.pallas_call(
        functools.partial(prefill_kernel, z_count, y_count, kv_rank, exponent_scale),
        out_shape=[
            jax.ShapeDtypeStruct((z_count, y_count, 2, 2, rows, width), bf16),
            jax.ShapeDtypeStruct((2, rows, width), bf16),
            jax.ShapeDtypeStruct((heads, tokens, width), bf16),
            jax.ShapeDtypeStruct((heads, tokens, kv_rank), bf16),
        ],
        in_specs=[vmem, hbm, vmem, hbm, vmem],
        out_specs=[hbm] * 4,
        scratch_shapes=[
            pltpu.VMEM((rows, width), bf16),
            pltpu.VMEM(q_nope.shape, bf16),
            pltpu.VMEM(up_key.shape, bf16),
            pltpu.VMEM((heads, tokens, width), bf16),
            pltpu.VMEM((heads * tokens, kv_rank), jnp.float32),
            pltpu.VMEM((heads * tokens, LANES), jnp.float32),
            pltpu.VMEM((heads * tokens, LANES), jnp.float32),
            pltpu.VMEM((2, y_count // 2, 2, 2, rows, width), bf16),
            pltpu.VMEM((tokens, chunk), jnp.float32),
            dma((2,)),
            dma((2,)),
            dma((2,)),
            dma((4,)),
            dma((2,)),
            dma((3,)),
            dma((2, z_count // 2)),
            dma((2, z_count // 2)),
            dma((z_count, 4)),
            dma((z_count, 4)),
            dma((z_count,)),
            dma((z_count,)),
        ],
        compiler_params=pltpu.CompilerParams(
            collective_id=0, has_side_effects=True, vmem_limit_bytes=56 << 20
        ),
    )(own, q_nope, q_rope, up_key, lengths)


def over_lanes(value, width):
    return jnp.concatenate([value] * (width // LANES), axis=1)


def decode_kernel(
    kv_rank,
    groups,
    exponent_scale,
    lengths,
    table,
    q_ref,
    keys,
    own_keys,
    _,
    out_ref,
    acc,
    top,
    total,
    held,
    ready,
    sems,
    out_sem,
):
    band = pl.program_id(0)
    heads, tokens, width = q_ref.shape
    rows = heads * tokens
    all_keys = keys.shape[0]
    nt = (((1,), (1,)), ((), ()))

    @pl.when(lax.axis_index("section") == 1)
    def _():
        prompt = table[lax.axis_index("seq") * pl.num_programs(0) + band] // groups
        low = lax.fori_loop(0, prompt, lambda k, at: at + lengths[k], jnp.int32(0))
        last = low + lengths[prompt]
        first = low // 16 * 16
        chunks = (last - first + KEY_BLOCK - 1) // KEY_BLOCK

        def chunk_at(i):
            return pl.multiple_of(jnp.minimum(first + i * KEY_BLOCK, all_keys - KEY_BLOCK), 16)

        def fetch(i):
            slot = lax.rem(i, 2)
            return pltpu.make_async_copy(
                keys.at[pl.ds(chunk_at(i), KEY_BLOCK), :], held.at[slot], sems.at[slot]
            )

        fetch(0).start()

        q = q_ref[...].reshape(rows, width)
        own = own_keys[...]
        scores = lax.dot_general(q, own, nt, preferred_element_type=jnp.float32)
        asked = lax.broadcasted_iota(jnp.int32, (tokens, tokens), 0)
        key = lax.broadcasted_iota(jnp.int32, (tokens, tokens), 1)
        seen = (asked % SAMPLES == key % SAMPLES) & (key // SAMPLES <= asked // SAMPLES)
        bias = jnp.where(seen, 0.0, masked_low)
        bias = jnp.broadcast_to(bias[None], (heads, tokens, tokens)).reshape(rows, tokens)
        scores = scores + bias
        own_top = jnp.max(scores, axis=1, keepdims=True)
        expo = jnp.exp2((scores - own_top) * exponent_scale)
        lane = lax.broadcasted_iota(jnp.int32, (rows, LANES), 1)
        total[...] = jnp.where(lane == 0, jnp.sum(expo, axis=1, keepdims=True), 0.0)
        top[...] = jnp.broadcast_to(own_top, (rows, LANES))
        acc[...] = jnp.dot(
            expo.astype(jnp.bfloat16), own[:, :kv_rank], preferred_element_type=jnp.float32
        )

        def fold(key_block, low_spot, at):
            count = key_block.shape[0]
            s = lax.dot_general(q, key_block, nt, preferred_element_type=jnp.float32)
            if low_spot is not None:
                spot = at + lax.broadcasted_iota(jnp.int32, (1, count), 1)
                here = (spot >= jnp.maximum(low, low_spot)) & (spot < last)
                s = s + jnp.where(here, 0.0, masked_low)
            before = top[...]
            now = jnp.maximum(before, jnp.max(s, axis=1, keepdims=True))
            shrink = jnp.exp2((before - now) * exponent_scale)
            expo = jnp.exp2((s - over_lanes(now, count)) * exponent_scale)
            top[...] = now
            summed = total[...] * shrink
            for c in range(0, count, LANES):
                summed = summed + expo[:, c : c + LANES]
            total[...] = summed
            acc[...] = acc[...] * over_lanes(shrink, kv_rank) + jnp.dot(
                expo.astype(jnp.bfloat16),
                key_block[:, :kv_rank],
                preferred_element_type=jnp.float32,
            )

        @pl.loop(0, chunks)
        def _(i):
            slot = lax.rem(i, 2)
            fetch(i).wait()

            @pl.when(i + 1 < chunks)
            def _():
                fetch(i + 1).start()

            nominal = first + i * KEY_BLOCK
            at = chunk_at(i)
            whole = (nominal >= low) & (nominal + KEY_BLOCK <= last)

            @pl.when(whole)
            def _():
                fold(held[slot], None, None)

            @pl.when(jnp.logical_not(whole))
            def _():
                skip = (nominal - at) // EDGE_BLOCK

                @pl.loop(skip, (jnp.minimum(last - at, KEY_BLOCK) + EDGE_BLOCK - 1) // EDGE_BLOCK)
                def _(j):
                    here = pl.multiple_of(j * EDGE_BLOCK, EDGE_BLOCK)
                    fold(held[slot, pl.ds(here, EDGE_BLOCK), :], nominal, at + here)

        norm = 1.0 / jnp.sum(total[...], axis=1, keepdims=True)
        ready[...] = (acc[...] * norm).astype(jnp.bfloat16).reshape(heads, tokens, kv_rank)
        spot = pl.ds(pl.multiple_of(band * tokens, tokens), tokens)
        done = pltpu.make_async_copy(ready, out_ref.at[:, spot, :], out_sem)
        done.start()
        done.wait()


def shards(query_nope, query_rope, latent, up_key, value_up_weight, lengths, owner_request_table):
    seq_count = lax.axis_size("seq")
    tok_dev, head_dev, nope_dim = query_nope.shape[1:]
    rope_dim = query_rope.shape[2] // head_dev
    kv_rank = up_key.shape[1]
    width = kv_rank + rope_dim
    req_dev = owner_request_table.shape[0] // seq_count
    groups = owner_request_table.shape[0] // lengths.shape[0]
    band_tokens = tok_dev // req_dev
    exponent_scale = math.log2(math.e) / math.sqrt(nope_dim + rope_dim)

    keys, pair, queries, latent_out = prefill_part(
        latent[0],
        query_nope[0].swapaxes(0, 1),
        query_rope[0],
        up_key,
        lengths[:, None],
        seq_count,
        exponent_scale,
    )
    rows = head_dev * band_tokens
    latent_out = pl.pallas_call(
        functools.partial(decode_kernel, kv_rank, groups, exponent_scale),
        out_shape=jax.ShapeDtypeStruct((head_dev, tok_dev, kv_rank), jnp.bfloat16),
        grid_spec=pltpu.PrefetchScalarGridSpec(
            num_scalar_prefetch=2,
            grid=(req_dev,),
            in_specs=[
                pl.BlockSpec((head_dev, band_tokens, width), lambda i, *_: (0, i, 0)),
                pl.BlockSpec(memory_space=pl.ANY),
                pl.BlockSpec((band_tokens, width), lambda i, *_: (i, 0)),
                pl.BlockSpec(memory_space=pl.ANY),
            ],
            out_specs=pl.BlockSpec(memory_space=pl.ANY),
            scratch_shapes=[
                pltpu.VMEM((rows, kv_rank), jnp.float32),
                pltpu.VMEM((rows, LANES), jnp.float32),
                pltpu.VMEM((rows, LANES), jnp.float32),
                pltpu.VMEM((2, KEY_BLOCK, width), jnp.bfloat16),
                pltpu.VMEM((head_dev, band_tokens, kv_rank), jnp.bfloat16),
                pltpu.SemaphoreType.DMA((2,)),
                pltpu.SemaphoreType.DMA,
            ],
        ),
        input_output_aliases={5: 0},
        compiler_params=pltpu.CompilerParams(vmem_limit_bytes=48 << 20),
    )(
        lengths,
        owner_request_table,
        queries,
        keys.reshape(-1, width),
        pair.reshape(-1, width),
        latent_out,
    )

    attended = jnp.einsum(
        "htk,hkv->thv", latent_out, value_up_weight, preferred_element_type=jnp.float32
    )
    return attended.astype(jnp.bfloat16)[None]


def solution(mesh):
    in_specs = (
        P("section", "seq", "head", None),
        P("section", "seq", "head"),
        P("section", ("seq", "head"), None),
        P("head", None, None),
        P("head", None, None),
        P(),
        P(),
    )
    out_specs = P("section", "seq", "head", None)
    return jax.shard_map(shards, mesh=mesh, in_specs=in_specs, out_specs=out_specs, check_vma=False)
```

time: 250 us -> 144 us (0.58)
  the two profiles are of different devices: /device:TPU:245 before, /device:TPU:161 now
where the time goes in v2:
time: 144 us; the launch traced here: 143 us
  Pallas kernels  133 us (92%)
  local copies, waits for them, and re-layouts  8.76 us (6%)
    pallas_call x1, Pallas kernels, prefill_part(): pl.pallas_call(functools.partial(prefill_kernel, z_count, y_count, kv_ran...  129 us
    unnamed x11, local copies, waits for them, and re-layouts  5.71 us
    pallas_call x1, Pallas kernels, shards(): pl.pallas_call(functools.partial(decode_kernel, kv_rank, groups, exponent...  3.98 us

profile of v2, /device:TPU:161, one launch (start us, length us, event | category | flops | bytes accessed | tf_op | source)
XLA Modules:
  0.0 143.0 jit_solution(2962151613068471579)
XLA Ops:
  0.0 0.0 copy-start.2
  0.0 0.0 copy-start.3
  0.0 1.4 copy.10.lengths
  1.4 2.6 %copy.13 = bf16[1,128,32,128]{3,1,2,0:T(8,128)(2,1)} copy(bf16[1,128,32,128]{3,2,1,0:T(8,128)(2,1)} %param.7) | data formatting | bytes 2097152 | tf_op args[0]
  4.0 129.0 %shard_map.73 = (bf16[8,4,2,2,64,576]{5,4,3,2,1,0:T(8,128)(2,1)}, bf16[2,64,576]{2,1,0:T(8,128)(2,1)}, bf16[32,128,576]{2,1,0:T(8,128)(2,1)}, bf16[32,128,512]{2,1,0:T(8,128)(2,1)}) custom-call(bf16[64,576]{1,0:T(8,128)(2,1)} %bitcast.21, bf16[32,128,128]{2,1,0:T(8,128)(2,1)} %bitcast.19, bf16[128,2048]{1,0:T(8,128)(2,1)} %bitcast.20, ...), custom_call_target="tpu_custom_call" | custom-call | tf_op jit(solution)/shard_map/pallas_call | solution.py:441
  133.0 0.0 copy-done.2
  133.0 0.0 copy-done.3
  133.0 0.0 copy-start
  133.0 2.2 %copy-done = bf16[32,128,512]{2,1,0:T(8,128)(2,1)S(1)} copy-done((bf16[32,128,512]{2,1,0:T(8,128)(2,1)S(1)}, bf16[32,128,512]{2,1,0:T(8,128)(2,1)}, u32[]{:S(2)}) %copy-start) | copy-done | bytes 4194328
  135.2 0.0 copy-start.1
  135.2 0.9 copy-done.1
  136.1 0.0 copy-start.4
  136.1 4.0 %shard_map.74 = bf16[32,128,512]{2,1,0:T(8,128)(2,1)S(1)} custom-call(s32[32]{0:T(128)S(1)} %copy-done.2, s32[256]{0:T(256)S(1)} %copy-done.3, bf16[32,128,576]{2,1,0:T(8,128)(2,1)} %get-tuple-element.9.q_ref, bf16[8192,576]{1,0:T(8,128)(2,1)} %bitcast.18, bf16[128,576]{1,0:T(8,128)(2,1)S(1)} %bitcast.16, ...), custom_call_target="tpu_custom_call", output_to_operand_aliasing={{}: (5, {})} | custom-call | tf_op jit(solution)/shard_map/pallas_call | solution.py:623
  140.1 0.0 copy-done.4
  140.1 1.2 fusion
  141.4 1.6 %copy.11 = bf16[1,128,32,128]{3,2,1,0:T(8,128)(2,1)} copy(bf16[1,128,32,128]{3,1,2,0:T(8,128)(2,1)S(1)} %fusion) | data formatting | bytes 2097152 | tf_op jit(solution)/shard_map/broadcast_in_dim | solution.py:660
Async XLA Ops:
  0.0 133.0 %copy-start.2 = (s32[32]{0:T(128)S(1)}, s32[32]{0:T(128)}, u32[]{:S(2)}) copy-start(s32[32]{0:T(128)} %lengths.1) | copy-start | bytes 388
  0.0 133.0 %copy-start.3 = (s32[256]{0:T(256)S(1)}, s32[256]{0:T(256)}, u32[]{:S(2)}) copy-start(s32[256]{0:T(256)} %table.1) | copy-start | bytes 3076
  133.0 2.2 %copy-start = (bf16[32,128,512]{2,1,0:T(8,128)(2,1)S(1)}, bf16[32,128,512]{2,1,0:T(8,128)(2,1)}, u32[]{:S(2)}) copy-start(bf16[32,128,512]{2,1,0:T(8,128)(2,1)} %get-tuple-element.12._) | copy-start | bytes 12582916
  135.2 0.9 copy-start.1
  136.1 4.0 %copy-start.4 = (bf16[32,512,128]{2,1,0:T(8,128)(2,1)S(1)}, bf16[32,512,128]{2,1,0:T(8,128)(2,1)}, u32[]{:S(2)}) copy-start(bf16[32,512,128]{2,1,0:T(8,128)(2,1)} %param.11) | copy-start | bytes 12582916

commit v3 on v2

--- a/solution.py
+++ b/solution.py
@@ -158,149 +158,220 @@
         arrive(keys.at[z, y, 1 - hi, core], x_recv.at[1])
 
     low, high, far = row_at(-1), row_at(1), row_at(2)
+    columns = [y, low, high, far]
     planes = [z]
     for s in range(1, half):
         planes += [plane_at(-s), plane_at(s)]
     planes.append(plane_at(half))
     steps = [[0]] + [[2 * s - 1, 2 * s] for s in range(1, half)] + [[z_count - 1]]
 
-    a_went = []
-
-    def a_send(src, to, send_sem, recv_sem):
-        copy = lambda: remote(src(), src(), to(), send_sem(), recv_sem())
-        a_went.append(copy)
-        copy().start()
-
-    def a_plane(n):
-        return lambda: keys.at[planes[n], :, :, 0]
-
-    def a_ahead(n, step, up_way):
-        d, j = (1, 0) if up_way else (-1, 1)
-        part = a_plane(n)
-        if step == half - 1:
-            part = lambda: keys.at[planes[n], pl.ds(j * (y_count // 2), y_count // 2), :, 0]
-        a_send(
-            part, lambda: device(dz=d), lambda: z_send.at[j, step], lambda: z_recv.at[j, step]
-        )
-
-    def a_sibling(n):
-        a_send(
-            a_plane(n), lambda: device(to_core=1), lambda: sib_send.at[n], lambda: sib_recv.at[n]
-        )
-
-    def a_y(src, d, k):
-        a_send(src, lambda: device(dy=d), lambda: y_send.at[0, k], lambda: y_recv.at[0, k])
-
-    def a_start():
-        mine = lambda: keys.at[z, y, :, 0]
-        a_y(mine, 1, 0)
-        a_y(mine, -1, 1)
-        arrive(keys.at[z, low, :, 0], y_recv.at[0, 0])
-        a_y(lambda: keys.at[z, low, 0, 0], 1, 2)
-        arrive(keys.at[z, high, :, 0], y_recv.at[0, 1])
-        a_y(lambda: keys.at[z, high, 1, 0], -1, 3)
-        arrive(keys.at[z, far, 0, 0], y_recv.at[0, 2])
-        arrive(keys.at[z, far, 1, 0], y_recv.at[0, 3])
-        a_ahead(0, 0, True)
-        a_ahead(0, 0, False)
-        a_sibling(0)
-
-    def a_point(s):
-        if s < half:
-            below, above = steps[s]
-            arrive(a_plane(below)(), z_recv.at[0, s - 1])
-            a_ahead(below, s, True)
-            arrive(a_plane(above)(), z_recv.at[1, s - 1])
-            a_ahead(above, s, False)
-            a_sibling(below)
-            a_sibling(above)
-        else:
-            for j in range(2):
-                part = keys.at[planes[-1], pl.ds(j * (y_count // 2), y_count // 2), :, 0]
-                arrive(part, z_recv.at[j, half - 1])
-            a_sibling(z_count - 1)
-
-    b_went = []
-
-    def b_send(src, to, send_sem, recv_sem):
-        copy = lambda: remote(src(), src(), to(), send_sem(), recv_sem())
-        b_went.append(copy)
-        copy().start()
-
-    def b_ahead(n, step, up_way):
-        d, j = (1, 0) if up_way else (-1, 1)
-        if step < half - 1:
-            part = lambda: keys.at[planes[n], y, :, 1]
-        else:
-            part = lambda: keys.at[planes[n], y, j, 1]
-        b_send(
-            part, lambda: device(dz=d), lambda: z_send.at[j, step], lambda: z_recv.at[j, step]
-        )
-
-    def b_y(src, d, n, k):
-        b_send(src, lambda: device(dy=d), lambda: y_send.at[n, k], lambda: y_recv.at[n, k])
-
-    def b_spread(n):
-        b_y(lambda: keys.at[planes[n], y, :, 1], 1, n, 0)
-        b_y(lambda: keys.at[planes[n], y, :, 1], -1, n, 1)
-
-    def b_spread_on(n):
-        arrive(keys.at[planes[n], low, :, 1], y_recv.at[n, 0])
-        b_y(lambda: keys.at[planes[n], low, 0, 1], 1, n, 2)
-        arrive(keys.at[planes[n], high, :, 1], y_recv.at[n, 1])
-        b_y(lambda: keys.at[planes[n], high, 1, 1], -1, n, 3)
-
-    def b_finish(n):
-        arrive(keys.at[planes[n], far, 0, 1], y_recv.at[n, 2])
-        arrive(keys.at[planes[n], far, 1, 1], y_recv.at[n, 3])
-        b_send(
-            lambda: keys.at[planes[n], :, :, 1],
-            lambda: device(to_core=0),
+    def sender(went):
+        def send(src, to, send_sem, recv_sem):
+            copy = lambda: remote(src(), src(), to(), send_sem(), recv_sem())
+            went.append(copy)
+            copy().start()
+
+        return send
+
+    went = {(section_of, core_of): [] for section_of in range(2) for core_of in range(2)}
+
+    def along_y(send, n, c, src, d, k):
+        send(src, lambda: device(dy=d), lambda: y_send.at[n, k], lambda: y_recv.at[n, k])
+
+    def spread(send, n, c):
+        mine = lambda: keys.at[planes[n], y, :, c]
+        along_y(send, n, c, mine, 1, 0)
+        along_y(send, n, c, mine, -1, 1)
+
+    def spread_on(send, n, c):
+        arrive(keys.at[planes[n], low, :, c], y_recv.at[n, 0])
+        along_y(send, n, c, lambda: keys.at[planes[n], low, 0, c], 1, 2)
+        arrive(keys.at[planes[n], high, :, c], y_recv.at[n, 1])
+        along_y(send, n, c, lambda: keys.at[planes[n], high, 1, c], -1, 3)
+
+    def spread_end(n, c):
+        arrive(keys.at[planes[n], far, 0, c], y_recv.at[n, 2])
+        arrive(keys.at[planes[n], far, 1, c], y_recv.at[n, 3])
+
+    def to_sibling(send, n, c):
+        send(
+            lambda: keys.at[planes[n], :, :, c],
+            lambda: device(to_core=1 - c),
             lambda: sib_send.at[n],
             lambda: sib_recv.at[n],
         )
 
-    def b_chain(s):
+    def along_z(send, src, up_way, step, k):
+        d, j = (1, 0) if up_way else (-1, 1)
+        send(
+            src,
+            lambda: device(dz=d),
+            lambda: z_send.at[j, step, k],
+            lambda: z_recv.at[j, step, k],
+        )
+
+    def decode_a():
+        send = sender(went[1, 0])
+        ways = ((0, True), (1, False))
+
+        def cell(n, k):
+            return lambda: keys.at[planes[n], columns[k], :, 0]
+
+        def column(k):
+            for _, up_way in ways:
+                along_z(send, cell(0, k), up_way, 0, k)
+
+        spread(send, 0, 0)
+        column(0)
+        arrive(keys.at[z, low, :, 0], y_recv.at[0, 0])
+        along_y(send, 0, 0, lambda: keys.at[z, low, 0, 0], 1, 2)
+        column(1)
+        arrive(keys.at[z, high, :, 0], y_recv.at[0, 1])
+        along_y(send, 0, 0, lambda: keys.at[z, high, 1, 0], -1, 3)
+        column(2)
+        spread_end(0, 0)
+        column(3)
+        to_sibling(send, 0, 0)
+        for s in range(1, half):
+            for k in range(y_count):
+                for n, (j, up_way) in zip(steps[s], ways):
+                    arrive(cell(n, k)(), z_recv.at[j, s - 1, k])
+                    if s < half - 1 or k // 2 == j:
+                        along_z(send, cell(n, k), up_way, s, k)
+            for n in steps[s]:
+                to_sibling(send, n, 0)
+        for k in range(y_count):
+            arrive(cell(z_count - 1, k)(), z_recv.at[k // 2, half - 1, k])
+        to_sibling(send, z_count - 1, 0)
+
+    def decode_b():
+        send = sender(went[1, 1])
+        ways = ((0, True), (1, False))
+
+        def ahead(n, s, j, up_way):
+            if s < half - 1:
+                part = lambda: keys.at[planes[n], y, :, 1]
+            else:
+                part = lambda: keys.at[planes[n], y, j, 1]
+            along_z(send, part, up_way, s, 0)
+
+        for j, up_way in ways:
+            ahead(0, 0, j, up_way)
+        spread(send, 0, 1)
+        for s in range(1, half):
+            for n, (j, up_way) in zip(steps[s], ways):
+                arrive(keys.at[planes[n], y, :, 1], z_recv.at[j, s - 1, 0])
+                ahead(n, s, j, up_way)
+                spread(send, n, 1)
+            if s == 1:
+                spread_on(send, 0, 1)
+        for j in range(2):
+            arrive(keys.at[planes[-1], y, j, 1], z_recv.at[j, half - 1, 0])
+        spread(send, z_count - 1, 1)
+        for n in range(z_count):
+            if n >= 1:
+                spread_on(send, n, 1)
+                spread_end(n - 1, 1)
+                to_sibling(send, n - 1, 1)
+        spread_end(z_count - 1, 1)
+        to_sibling(send, z_count - 1, 1)
+
+    behind = [0] + [2 * s - 1 for s in range(1, half)] + [z_count - 1]
+    past = planes[2 * (half - 1)]
+
+    def prefill_a_start():
+        send = sender(went[0, 0])
+        spread(send, 0, 0)
+        spread_on(send, 0, 0)
+        spread_end(0, 0)
+        along_z(send, lambda: keys.at[z, :, :, 0], True, 0, 0)
+        to_sibling(send, 0, 0)
+
+    def prefill_a(s):
+        send = sender(went[0, 0])
+        n = behind[s]
+        arrive(keys.at[planes[n], :, :, 0], z_recv.at[0, s - 1, 0])
         if s < half:
-            below, above = steps[s]
-            arrive(keys.at[planes[below], y, :, 1], z_recv.at[0, s - 1])
-            b_ahead(below, s, True)
-            arrive(keys.at[planes[above], y, :, 1], z_recv.at[1, s - 1])
-            b_ahead(above, s, False)
+            along_z(send, lambda: keys.at[planes[n], :, :, 0], True, s, 0)
         else:
-            arrive(keys.at[planes[-1], y, 0, 1], z_recv.at[0, half - 1])
-            arrive(keys.at[planes[-1], y, 1, 1], z_recv.at[1, half - 1])
-        for n in steps[s]:
-            b_spread(n)
-
-    def b_start():
-        b_ahead(0, 0, True)
-        b_ahead(0, 0, False)
-        b_spread(0)
-        b_spread_on(0)
-        b_chain(1)
-        b_finish(0)
-
-    def b_point(s):
-        for n in steps[s]:
-            b_spread_on(n)
+            along_z(send, lambda: keys.at[planes[n], y_count - 1, 1, 0], True, 0, 1)
+        to_sibling(send, n, 0)
+
+    def prefill_a_end():
+        send = sender(went[0, 0])
+        spot = lambda: keys.at[past, y_count - 1, 1, 0]
+        arrive(spot(), z_recv.at[0, 0, 1])
+        send(
+            spot,
+            lambda: device(to_core=1),
+            lambda: sib_send.at[2 * (half - 1)],
+            lambda: sib_recv.at[2 * (half - 1)],
+        )
+
+    def prefill_b_start():
+        send = sender(went[0, 1])
+        along_z(send, lambda: keys.at[z, y, :, 1], True, 0, 0)
+        spread(send, 0, 1)
+        spread_on(send, 0, 1)
+        spread_end(0, 1)
+        to_sibling(send, 0, 1)
+
+    def prefill_b_chain(s):
+        send = sender(went[0, 1])
+        n = behind[s]
+        arrive(keys.at[planes[n], y, :, 1], z_recv.at[0, s - 1, 0])
         if s < half:
-            b_chain(s + 1)
-        for n in steps[s]:
-            b_finish(n)
-
-    def point(s):
+            along_z(send, lambda: keys.at[planes[n], y, :, 1], True, s, 0)
+        else:
+            along_z(send, lambda: keys.at[planes[n], y, 1, 1], True, 0, 1)
+        spread(send, n, 1)
+
+    def prefill_b_on(s):
+        spread_on(sender(went[0, 1]), behind[s], 1)
+
+    def prefill_b_end(s):
+        spread_end(behind[s], 1)
+        to_sibling(sender(went[0, 1]), behind[s], 1)
+
+    def prefill_b_past():
+        arrive(keys.at[past, y, 1, 1], z_recv.at[0, 0, 1])
+        n = 2 * (half - 1)
+        along_y(sender(went[0, 1]), n, 1, lambda: keys.at[past, y, 1, 1], 1, 0)
+
+    def prefill_b_past_end():
+        n = 2 * (half - 1)
+        spot = lambda: keys.at[past, low, 1, 1]
+        arrive(spot(), y_recv.at[n, 0])
+        sender(went[0, 1])(
+            spot, lambda: device(to_core=0), lambda: sib_send.at[n], lambda: sib_recv.at[n]
+        )
+
+    def from_sibling(n):
+        arrive(keys.at[planes[n], :, :, 1 - core], sib_recv.at[n])
+
+    def past_from_sibling():
+        n = 2 * (half - 1)
+
         @pl.when(core == 0)
         def _():
-            a_start() if s == 0 else a_point(s)
+            arrive(keys.at[past, low, 1, 1], sib_recv.at[n])
 
         @pl.when(core == 1)
         def _():
-            b_start() if s == 0 else b_point(s)
-
-    def from_sibling(s):
-        for n in steps[s]:
-            arrive(keys.at[planes[n], :, :, 1 - core], sib_recv.at[n])
+            arrive(keys.at[past, y_count - 1, 1, 0], sib_recv.at[n])
+
+    def on_core(at, c, *events):
+        @pl.when((core == c) if at is True else (at & (core == c)))
+        def _():
+            for event in events:
+                event()
+
+    @pl.when(section == 1)
+    def _():
+        on_core(True, 0, decode_a)
+        on_core(True, 1, decode_b)
+        for n in range(z_count):
+            from_sibling(n)
 
     @pl.when(section == 0)
     def _():
@@ -310,13 +381,15 @@
 
     token = lax.broadcasted_iota(jnp.int32, (tokens, 1), 0)
     position = seq * tokens + token
-    count = lengths.shape[0]
+    count = lengths.shape[1]
     before_it = lax.broadcasted_iota(jnp.int32, (count, count), 0) < lax.broadcasted_iota(
         jnp.int32, (count, count), 1
     )
-    starts = jnp.sum(
-        jnp.where(before_it, lengths[...].astype(jnp.float32), 0.0), axis=0, keepdims=True
-    )
+    earlier = jnp.where(before_it, 1.0, 0.0).astype(jnp.bfloat16)
+    wide = jnp.broadcast_to(lengths[...], (8, count))
+    digits = [(wide // 64).astype(jnp.bfloat16), (wide % 64).astype(jnp.bfloat16)]
+    upper, lower = [jnp.dot(d, earlier, preferred_element_type=jnp.float32) for d in digits]
+    starts = (upper * 64.0 + lower)[:1]
     row_low = jnp.max(
         jnp.where(starts <= position.astype(jnp.float32), starts, 0.0), axis=1, keepdims=True
     ).astype(jnp.int32)
@@ -324,75 +397,121 @@
     chunk = plane_keys // 2
     tile_heads = 8
     rows = tile_heads * tokens
-
-    def fold(first_spot, side):
-        spot = first_spot + lax.broadcasted_iota(jnp.int32, (1, chunk), 1)
+    tiles = heads // tile_heads
+
+    def fold(tile, key_block):
+        count = key_block.shape[0]
+        part = pl.ds(pl.multiple_of(tile * rows, rows), rows)
+        asked = q[pl.ds(tile * tile_heads, tile_heads)].reshape(rows, width)
+        s = lax.dot_general(asked, key_block, nt, preferred_element_type=jnp.float32)
+        s = (s.reshape(tile_heads, tokens, count) + bias[:, :count][None]).reshape(rows, count)
+        before = top[part, :]
+        now = jnp.maximum(before, jnp.max(s, axis=1, keepdims=True))
+        shrink = jnp.exp2((before - now) * exponent_scale)
+        expo = jnp.exp2((s - over_lanes(now, count)) * exponent_scale)
+        top[part, :] = now
+        summed = total[part, :] * shrink
+        for c in range(0, count, LANES):
+            summed = summed + expo[:, c : c + LANES]
+        total[part, :] = summed
+        acc[part, :] = acc[part, :] * over_lanes(shrink, kv_rank) + jnp.dot(
+            expo.astype(jnp.bfloat16),
+            key_block[:, :kv_rank],
+            preferred_element_type=jnp.float32,
+        )
+
+    def hide(first_spot, count):
+        spot = first_spot + lax.broadcasted_iota(jnp.int32, (1, count), 1)
         seen = (spot >= row_low) & (spot <= position)
-        bias[...] = jnp.where(seen, 0.0, masked_low)
-
-        @pl.loop(0, heads // tile_heads)
-        def _(tile):
-            part = pl.ds(pl.multiple_of(tile * rows, rows), rows)
-            asked = q[pl.ds(tile * tile_heads, tile_heads)].reshape(rows, width)
-            s = lax.dot_general(asked, held[side].reshape(chunk, width), nt, preferred_element_type=jnp.float32)
-            s = (s.reshape(tile_heads, tokens, chunk) + bias[...][None]).reshape(rows, chunk)
-            before = top[part, :]
-            now = jnp.maximum(before, jnp.max(s, axis=1, keepdims=True))
-            shrink = jnp.exp2((before - now) * exponent_scale)
-            expo = jnp.exp2((s - over_lanes(now, chunk)) * exponent_scale)
-            top[part, :] = now
-            summed = total[part, :] * shrink
-            for c in range(0, chunk, LANES):
-                summed = summed + expo[:, c : c + LANES]
-            total[part, :] = summed
-            acc[part, :] = acc[part, :] * over_lanes(shrink, kv_rank) + jnp.dot(
-                expo.astype(jnp.bfloat16),
-                held[side].reshape(chunk, width)[:, :kv_rank],
-                preferred_element_type=jnp.float32,
-            )
-
-    @pl.loop(0, 2 * half + 3)
-    def _(i):
-        for s in range(half + 1):
-
-            @pl.when(i == max(2 * s - 1, 0))
+        bias[:, :count] = jnp.where(seen, 0.0, masked_low)
+
+    last_step = 4 * (half + 1)
+
+    @pl.when(section == 0)
+    def _():
+        @pl.loop(0, last_step + 1)
+        def _(step):
+            on_core(step == 0, 0, prefill_a_start)
+            on_core(step == 0, 1, prefill_b_start)
+            for s in range(1, half + 1):
+                on_core(step == 4 * s - 1, 0, functools.partial(prefill_a, s))
+                on_core(step == 4 * s - 3, 1, functools.partial(prefill_b_chain, s))
+                on_core(step == 4 * s - 2, 1, functools.partial(prefill_b_on, s))
+                on_core(step == 4 * s - 1, 1, functools.partial(prefill_b_end, s))
+            on_core(step == last_step - 1, 0, prefill_a_end)
+            on_core(step == last_step - 2, 1, prefill_b_past)
+            on_core(step == last_step - 1, 1, prefill_b_past_end)
+            for s in range(half + 1):
+
+                @pl.when(step == 4 * s)
+                def _():
+                    from_sibling(behind[s])
+
+            @pl.when(step == last_step)
             def _():
-                point(s)
-
-            @pl.when(i == 2 * s)
+                past_from_sibling()
+
+            back = step // 4
+            side = step // 2 % 2
+            turn = step % 2
+            is_last = step == last_step
+            plane = lax.rem(z - back + z_count, z_count)
+            reached = (z >= back) & jnp.logical_not(is_last)
+
+            def load(part):
+                here = keys.at[plane, pl.ds(part * (y_count // 2), y_count // 2)]
+                return pltpu.make_async_copy(here, held.at[part], held_sems.at[part])
+
+            def load_past():
+                return pltpu.make_async_copy(
+                    keys.at[past, y_count - 1, 1], held.at[0, 0, 0], held_sems.at[0]
+                )
+
+            @pl.when(reached & (step % 4 == 0))
             def _():
-                from_sibling(s)
-
-        back = i // 2
-        last_step = i == 2 * half + 2
-        side = jnp.where(last_step, 1, i % 2)
-        plane = lax.rem(z - back + z_count, z_count)
-        reached = (section == 0) & (z >= back)
-        reached = reached & (jnp.logical_not(last_step) | (at_block == 0))
-
-        def load(part):
-            here = keys.at[plane, pl.ds(part * (y_count // 2), y_count // 2)]
-            return pltpu.make_async_copy(here, held.at[part], held_sems.at[part])
-
-        @pl.when(reached & (i % 2 == 0) & jnp.logical_not(last_step))
-        def _():
-            load(0).start()
-            load(1).start()
-
-        @pl.when(reached & last_step)
-        def _():
-            load(1).start()
-
-        @pl.when(reached)
-        def _():
-            load(side).wait()
-
-        needed = reached & ((i != 1) | (at_block >= plane_blocks // 2))
-        needed = needed & ((i != 2 * half) | (at_block <= plane_blocks // 2))
-
-        @pl.when(needed)
-        def _():
-            fold((z - back) * plane_keys + side * chunk, side)
+                load(0).start()
+                load(1).start()
+
+            @pl.when(reached & (turn == 0))
+            def _():
+                load(side).wait()
+
+            mid = plane_blocks // 2
+            rim_own = (back == 0) & (side == 1)
+            rim_far = (back == half) & (side == 0)
+            few = (rim_own | rim_far) & (at_block == mid)
+            none = (rim_own & (at_block < mid)) | (rim_far & (at_block > mid))
+            first_spot = (z - back) * plane_keys + side * chunk
+            few_spot = jnp.where(rim_far, first_spot + chunk - tokens, first_spot)
+
+            @pl.when(reached & jnp.logical_not(few | none))
+            def _():
+                @pl.when(turn == 0)
+                def _():
+                    hide(first_spot, chunk)
+
+                @pl.loop(0, tiles // 2)
+                def _(tile):
+                    fold(turn * (tiles // 2) + tile, held[side].reshape(chunk, width))
+
+            edge = (z > half) & is_last & (at_block == 0)
+
+            @pl.when(edge)
+            def _():
+                load_past().start()
+                load_past().wait()
+
+            @pl.when(edge | (reached & few & (turn == 0)))
+            def _():
+                hide(jnp.where(is_last, first_spot + plane_keys - tokens, few_spot), tokens)
+                spot = jnp.where(rim_far, y_count - 1, 0)
+                block_keys = held[
+                    jnp.where(is_last, 0, side), spot // 2, spot % 2
+                ].reshape(tokens, width)
+
+                @pl.loop(0, tiles)
+                def _(tile):
+                    fold(tile, block_keys)
 
     @pl.when(section == 0)
     def _():
@@ -412,15 +531,12 @@
     def _():
         pltpu.make_async_copy(q, q_out, out_sems.at[0]).wait()
 
-    @pl.when(core == 0)
-    def _():
-        for copy in a_went:
-            copy().wait_send()
-
-    @pl.when(core == 1)
-    def _():
-        for copy in b_went:
-            copy().wait_send()
+    for (section_of, core_of), copies in went.items():
+
+        @pl.when((section == section_of) & (core == core_of))
+        def _():
+            for copy in copies:
+                copy().wait_send()
 
     arrive(own_out.at[1 - core], own_sems.at[2])
     own_away().wait_send()
@@ -464,8 +580,8 @@
             dma((4,)),
             dma((2,)),
             dma((3,)),
-            dma((2, z_count // 2)),
-            dma((2, z_count // 2)),
+            dma((2, z_count // 2, y_count)),
+            dma((2, z_count // 2, y_count)),
             dma((z_count, 4)),
             dma((z_count, 4)),
             dma((z_count,)),
@@ -497,35 +613,69 @@
     total,
     held,
     ready,
+    q_held,
     sems,
-    out_sem,
+    q_sems,
+    out_sems,
 ):
     band = pl.program_id(0)
-    heads, tokens, width = q_ref.shape
+    bands = pl.num_programs(0)
+    _, heads, tokens, width = q_held.shape
     rows = heads * tokens
     all_keys = keys.shape[0]
     nt = (((1,), (1,)), ((), ()))
 
     @pl.when(lax.axis_index("section") == 1)
     def _():
-        prompt = table[lax.axis_index("seq") * pl.num_programs(0) + band] // groups
-        low = lax.fori_loop(0, prompt, lambda k, at: at + lengths[k], jnp.int32(0))
-        last = low + lengths[prompt]
+        def prompt_range(which):
+            prompt = table[lax.axis_index("seq") * bands + which] // groups
+            low = lax.fori_loop(0, prompt, lambda k, at: at + lengths[k], jnp.int32(0))
+            return low, low + lengths[prompt]
+
+        def chunk_at(start, i):
+            return pl.multiple_of(jnp.minimum(start + i * KEY_BLOCK, all_keys - KEY_BLOCK), 16)
+
+        def fetch_from(start, i, slot):
+            return pltpu.make_async_copy(
+                keys.at[pl.ds(chunk_at(start, i), KEY_BLOCK), :], held.at[slot], sems.at[slot]
+            )
+
+        def band_rows(which):
+            return pl.ds(pl.multiple_of(which * tokens, tokens), tokens)
+
+        def fetch_q(which):
+            slot = lax.rem(which, 2)
+            return pltpu.make_async_copy(
+                q_ref.at[:, band_rows(which), :], q_held.at[slot], q_sems.at[slot]
+            )
+
+        def leave(which):
+            slot = lax.rem(which, 2)
+            return pltpu.make_async_copy(
+                ready.at[slot], out_ref.at[:, band_rows(which), :], out_sems.at[slot]
+            )
+
+        low, last = prompt_range(band)
         first = low // 16 * 16
         chunks = (last - first + KEY_BLOCK - 1) // KEY_BLOCK
 
-        def chunk_at(i):
-            return pl.multiple_of(jnp.minimum(first + i * KEY_BLOCK, all_keys - KEY_BLOCK), 16)
-
         def fetch(i):
-            slot = lax.rem(i, 2)
-            return pltpu.make_async_copy(
-                keys.at[pl.ds(chunk_at(i), KEY_BLOCK), :], held.at[slot], sems.at[slot]
-            )
-
-        fetch(0).start()
-
-        q = q_ref[...].reshape(rows, width)
+            slot = jnp.where(i == 0, lax.rem(band, 2), 2 + lax.rem(i, 2))
+            return fetch_from(first, i, slot)
+
+        @pl.when(band == 0)
+        def _():
+            fetch_q(0).start()
+            fetch(0).start()
+
+        @pl.when(band + 1 < bands)
+        def _():
+            fetch_q(band + 1).start()
+            next_low, _ = prompt_range(band + 1)
+            fetch_from(next_low // 16 * 16, 0, lax.rem(band + 1, 2)).start()
+
+        fetch_q(band).wait()
+        q = q_held[lax.rem(band, 2)].reshape(rows, width)
         own = own_keys[...]
         scores = lax.dot_general(q, own, nt, preferred_element_type=jnp.float32)
         asked = lax.broadcasted_iota(jnp.int32, (tokens, tokens), 0)
@@ -567,7 +717,7 @@
 
         @pl.loop(0, chunks)
         def _(i):
-            slot = lax.rem(i, 2)
+            slot = jnp.where(i == 0, lax.rem(band, 2), 2 + lax.rem(i, 2))
             fetch(i).wait()
 
             @pl.when(i + 1 < chunks)
@@ -575,7 +725,7 @@
                 fetch(i + 1).start()
 
             nominal = first + i * KEY_BLOCK
-            at = chunk_at(i)
+            at = chunk_at(first, i)
             whole = (nominal >= low) & (nominal + KEY_BLOCK <= last)
 
             @pl.when(whole)
@@ -592,11 +742,19 @@
                     fold(held[slot, pl.ds(here, EDGE_BLOCK), :], nominal, at + here)
 
         norm = 1.0 / jnp.sum(total[...], axis=1, keepdims=True)
-        ready[...] = (acc[...] * norm).astype(jnp.bfloat16).reshape(heads, tokens, kv_rank)
-        spot = pl.ds(pl.multiple_of(band * tokens, tokens), tokens)
-        done = pltpu.make_async_copy(ready, out_ref.at[:, spot, :], out_sem)
-        done.start()
-        done.wait()
+        @pl.when(band >= 2)
+        def _():
+            leave(band - 2).wait()
+
+        ready[lax.rem(band, 2)] = (
+            (acc[...] * norm).astype(jnp.bfloat16).reshape(heads, tokens, kv_rank)
+        )
+        leave(band).start()
+
+        @pl.when(band == bands - 1)
+        def _():
+            leave(band - 1).wait()
+            leave(band).wait()
 
 
 def shards(query_nope, query_rope, latent, up_key, value_up_weight, lengths, owner_request_table):
@@ -615,7 +773,7 @@
         query_nope[0].swapaxes(0, 1),
         query_rope[0],
         up_key,
-        lengths[:, None],
+        lengths[None, :],
         seq_count,
         exponent_scale,
     )
@@ -627,7 +785,7 @@
             num_scalar_prefetch=2,
             grid=(req_dev,),
             in_specs=[
-                pl.BlockSpec((head_dev, band_tokens, width), lambda i, *_: (0, i, 0)),
+                pl.BlockSpec(memory_space=pl.ANY),
                 pl.BlockSpec(memory_space=pl.ANY),
                 pl.BlockSpec((band_tokens, width), lambda i, *_: (i, 0)),
                 pl.BlockSpec(memory_space=pl.ANY),
@@ -637,14 +795,16 @@
                 pltpu.VMEM((rows, kv_rank), jnp.float32),
                 pltpu.VMEM((rows, LANES), jnp.float32),
                 pltpu.VMEM((rows, LANES), jnp.float32),
-                pltpu.VMEM((2, KEY_BLOCK, width), jnp.bfloat16),
-                pltpu.VMEM((head_dev, band_tokens, kv_rank), jnp.bfloat16),
+                pltpu.VMEM((4, KEY_BLOCK, width), jnp.bfloat16),
+                pltpu.VMEM((2, head_dev, band_tokens, kv_rank), jnp.bfloat16),
+                pltpu.VMEM((2, head_dev, band_tokens, width), jnp.bfloat16),
+                pltpu.SemaphoreType.DMA((4,)),
                 pltpu.SemaphoreType.DMA((2,)),
-                pltpu.SemaphoreType.DMA,
+                pltpu.SemaphoreType.DMA((2,)),
             ],
         ),
         input_output_aliases={5: 0},
-        compiler_params=pltpu.CompilerParams(vmem_limit_bytes=48 << 20),
+        compiler_params=pltpu.CompilerParams(vmem_limit_bytes=58 << 20),
     )(
         lengths,
         owner_request_table,

time: 144 us -> 133 us (0.924)
  Pallas kernels: 133 us -> 125 us
  local copies, waits for them, and re-layouts: 8.76 us -> 4.26 us
  matrix products: 1.24 us -> 3.43 us
    pallas_call x1, Pallas kernels: 129 us -> 122 us  [prefill_part(): pl.pallas_call(functools.partial(prefill_kernel, z_count, y_count, kv_ran...]
    unnamed x11 -> x3, local copies, waits for them, and re-layouts: 5.71 us -> 2.61 us
    dot_general x1, matrix products: 1.24 us -> 3.43 us  [shards(): jnp.einsum('htk,hkv->thv', latent_out, value_up_weight, preferred_element...]
where the time goes in v3:
time: 133 us; the launch traced here: 132 us
  Pallas kernels  125 us (94%)
  local copies, waits for them, and re-layouts  4.26 us (3%)
  matrix products  3.43 us (3%)
    pallas_call x1, Pallas kernels, prefill_part(): pl.pallas_call(functools.partial(prefill_kernel, z_count, y_count, kv_ran...  122 us
    dot_general x1, matrix products, shards(): jnp.einsum('htk,hkv->thv', latent_out, value_up_weight, preferred_element...  3.43 us
    pallas_call x1, Pallas kernels, shards(): pl.pallas_call(functools.partial(decode_kernel, kv_rank, groups, exponent...  2.9 us

profile of v3, /device:TPU:161, one launch (start us, length us, event | category | flops | bytes accessed | tf_op | source)
XLA Modules:
  0.0 132.5 jit_solution(6087558813716957272)
XLA Ops:
  0.0 2.6 %copy.12 = bf16[1,128,32,128]{3,1,2,0:T(8,128)(2,1)} copy(bf16[1,128,32,128]{3,2,1,0:T(8,128)(2,1)} %param.7) | data formatting | bytes 2097152 | tf_op args[0]
  2.6 121.8 %shard_map.73 = (bf16[8,4,2,2,64,576]{5,4,3,2,1,0:T(8,128)(2,1)}, bf16[2,64,576]{2,1,0:T(8,128)(2,1)}, bf16[32,128,576]{2,1,0:T(8,128)(2,1)}, bf16[32,128,512]{2,1,0:T(8,128)(2,1)}) custom-call(bf16[64,576]{1,0:T(8,128)(2,1)} %bitcast.20, bf16[32,128,128]{2,1,0:T(8,128)(2,1)} %bitcast.17, bf16[128,2048]{1,0:T(8,128)(2,1)} %bitcast.18, ...), custom_call_target="tpu_custom_call" | custom-call | tf_op jit(solution)/shard_map/pallas_call | solution.py:557
  124.4 0.0 copy-start
  124.5 2.9 %shard_map.74 = bf16[32,128,512]{2,1,0:T(8,128)(2,1)} custom-call(s32[32]{0:T(128)} %lengths.1, s32[256]{0:T(256)} %table.1, bf16[32,128,576]{2,1,0:T(8,128)(2,1)} %get-tuple-element.9.q_ref, bf16[8192,576]{1,0:T(8,128)(2,1)} %bitcast.16, bf16[128,576]{1,0:T(8,128)(2,1)} %bitcast.19, ...), custom_call_target="tpu_custom_call", output_to_operand_aliasing={{}: (5, {})} | custom-call | tf_op jit(solution)/shard_map/pallas_call | solution.py:781
  127.4 0.0 copy-done
  127.4 3.4 %fusion = bf16[1,128,32,128]{3,1,2,0:T(8,128)(2,1)S(1)} fusion(bf16[32,128,512]{2,1,0:T(8,128)(2,1)} %shard_map.74, bf16[32,512,128]{2,1,0:T(8,128)(2,1)S(1)} %copy-done), kind=kOutput, calls=%fused_computation.1 | convolution fusion | flops 537395200 | bytes 9437184 | tf_op jit(solution)/shard_map/htk,hkv->thv/dot_general | solution.py:817
  130.8 1.6 %copy.10 = bf16[1,128,32,128]{3,2,1,0:T(8,128)(2,1)} copy(bf16[1,128,32,128]{3,1,2,0:T(8,128)(2,1)S(1)} %fusion) | data formatting | bytes 2097152 | tf_op jit(solution)/shard_map/broadcast_in_dim | solution.py:820
Async XLA Ops:
  124.4 2.9 %copy-start = (bf16[32,512,128]{2,1,0:T(8,128)(2,1)S(1)}, bf16[32,512,128]{2,1,0:T(8,128)(2,1)}, u32[]{:S(2)}) copy-start(bf16[32,512,128]{2,1,0:T(8,128)(2,1)} %param.11) | copy-start | bytes 12582916

commit v4 on v3

--- a/solution.py
+++ b/solution.py
@@ -173,7 +173,7 @@
 
         return send
 
-    went = {(section_of, core_of): [] for section_of in range(2) for core_of in range(2)}
+    went = [[], [], []]
 
     def along_y(send, n, c, src, d, k):
         send(src, lambda: device(dy=d), lambda: y_send.at[n, k], lambda: y_recv.at[n, k])
@@ -211,7 +211,7 @@
         )
 
     def decode_a():
-        send = sender(went[1, 0])
+        send = sender(went[1])
         ways = ((0, True), (1, False))
 
         def cell(n, k):
@@ -245,7 +245,7 @@
         to_sibling(send, z_count - 1, 0)
 
     def decode_b():
-        send = sender(went[1, 1])
+        send = sender(went[2])
         ways = ((0, True), (1, False))
 
         def ahead(n, s, j, up_way):
@@ -278,98 +278,65 @@
 
     behind = [0] + [2 * s - 1 for s in range(1, half)] + [z_count - 1]
     past = planes[2 * (half - 1)]
-
-    def prefill_a_start():
-        send = sender(went[0, 0])
-        spread(send, 0, 0)
-        spread_on(send, 0, 0)
-        spread_end(0, 0)
-        along_z(send, lambda: keys.at[z, :, :, 0], True, 0, 0)
-        to_sibling(send, 0, 0)
-
-    def prefill_a(s):
-        send = sender(went[0, 0])
+    forward = sender(went[0])
+
+    def ahead(n, s):
+        along_z(forward, lambda: keys.at[planes[n], y, :, core], True, s, 0)
+
+    def prefill_start():
+        ahead(0, 0)
+        spread(forward, 0, core)
+        prefill_chain(1)
+        spread_on(forward, 0, core)
+        spread_end(0, core)
+        to_sibling(forward, 0, core)
+        prefill_on(1)
+        from_sibling(0)
+
+    def prefill_chain(s):
         n = behind[s]
-        arrive(keys.at[planes[n], :, :, 0], z_recv.at[0, s - 1, 0])
+        arrive(keys.at[planes[n], y, :, core], z_recv.at[0, s - 1, 0])
         if s < half:
-            along_z(send, lambda: keys.at[planes[n], :, :, 0], True, s, 0)
+            ahead(n, s)
         else:
-            along_z(send, lambda: keys.at[planes[n], y_count - 1, 1, 0], True, 0, 1)
-        to_sibling(send, n, 0)
-
-    def prefill_a_end():
-        send = sender(went[0, 0])
-        spot = lambda: keys.at[past, y_count - 1, 1, 0]
-        arrive(spot(), z_recv.at[0, 0, 1])
-        send(
+            along_z(forward, lambda: keys.at[planes[n], y, 1, core], True, 0, 1)
+        spread(forward, n, core)
+
+    def prefill_on(s):
+        spread_on(forward, behind[s], core)
+
+    def prefill_end(s):
+        spread_end(behind[s], core)
+        to_sibling(forward, behind[s], core)
+
+    def prefill_past():
+        arrive(keys.at[past, y, 1, core], z_recv.at[0, 0, 1])
+        n = 2 * (half - 1)
+        along_y(forward, n, core, lambda: keys.at[past, y, 1, core], 1, 0)
+
+    def prefill_past_end():
+        n = 2 * (half - 1)
+        spot = lambda: keys.at[past, low, 1, core]
+        arrive(spot(), y_recv.at[n, 0])
+        forward(
             spot,
-            lambda: device(to_core=1),
-            lambda: sib_send.at[2 * (half - 1)],
-            lambda: sib_recv.at[2 * (half - 1)],
-        )
-
-    def prefill_b_start():
-        send = sender(went[0, 1])
-        along_z(send, lambda: keys.at[z, y, :, 1], True, 0, 0)
-        spread(send, 0, 1)
-        spread_on(send, 0, 1)
-        spread_end(0, 1)
-        to_sibling(send, 0, 1)
-
-    def prefill_b_chain(s):
-        send = sender(went[0, 1])
-        n = behind[s]
-        arrive(keys.at[planes[n], y, :, 1], z_recv.at[0, s - 1, 0])
-        if s < half:
-            along_z(send, lambda: keys.at[planes[n], y, :, 1], True, s, 0)
-        else:
-            along_z(send, lambda: keys.at[planes[n], y, 1, 1], True, 0, 1)
-        spread(send, n, 1)
-
-    def prefill_b_on(s):
-        spread_on(sender(went[0, 1]), behind[s], 1)
-
-    def prefill_b_end(s):
-        spread_end(behind[s], 1)
-        to_sibling(sender(went[0, 1]), behind[s], 1)
-
-    def prefill_b_past():
-        arrive(keys.at[past, y, 1, 1], z_recv.at[0, 0, 1])
-        n = 2 * (half - 1)
-        along_y(sender(went[0, 1]), n, 1, lambda: keys.at[past, y, 1, 1], 1, 0)
-
-    def prefill_b_past_end():
-        n = 2 * (half - 1)
-        spot = lambda: keys.at[past, low, 1, 1]
-        arrive(spot(), y_recv.at[n, 0])
-        sender(went[0, 1])(
-            spot, lambda: device(to_core=0), lambda: sib_send.at[n], lambda: sib_recv.at[n]
+            lambda: device(to_core=1 - core),
+            lambda: sib_send.at[n],
+            lambda: sib_recv.at[n],
         )
 
     def from_sibling(n):
         arrive(keys.at[planes[n], :, :, 1 - core], sib_recv.at[n])
 
-    def past_from_sibling():
-        n = 2 * (half - 1)
-
-        @pl.when(core == 0)
+    def on(at, event):
+        @pl.when(at)
         def _():
-            arrive(keys.at[past, low, 1, 1], sib_recv.at[n])
-
-        @pl.when(core == 1)
-        def _():
-            arrive(keys.at[past, y_count - 1, 1, 0], sib_recv.at[n])
-
-    def on_core(at, c, *events):
-        @pl.when((core == c) if at is True else (at & (core == c)))
-        def _():
-            for event in events:
-                event()
+            event()
 
     @pl.when(section == 1)
     def _():
-        on_core(True, 0, decode_a)
-        on_core(True, 1, decode_b)
+        on(core == 0, decode_a)
+        on(core == 1, decode_b)
         for n in range(z_count):
             from_sibling(n)
 
@@ -425,56 +392,83 @@
         seen = (spot >= row_low) & (spot <= position)
         bias[:, :count] = jnp.where(seen, 0.0, masked_low)
 
+    def past_from_sibling():
+        arrive(keys.at[past, low, 1, 1 - core], sib_recv.at[2 * (half - 1)])
+
     last_step = 4 * (half + 1)
+    events = {
+        0: [prefill_start],
+        1: [functools.partial(prefill_end, 1), functools.partial(prefill_chain, 2)],
+        last_step - 8: [prefill_past],
+        last_step - 6: [prefill_past_end],
+        last_step - 2: [past_from_sibling],
+    }
+    for s in range(1, half + 1):
+        if s > 1:
+            events.setdefault(4 * s - 5 - (s > 3), []).append(functools.partial(prefill_on, s))
+            events.setdefault(4 * s - 4 - (s > 3), []).append(functools.partial(prefill_end, s))
+        if s > 2:
+            events.setdefault(3 * s - 5, []).append(functools.partial(prefill_chain, s))
+        events.setdefault(4 * s - (2 if s == 1 else 3), []).append(
+            functools.partial(from_sibling, behind[s])
+        )
 
     @pl.when(section == 0)
     def _():
         @pl.loop(0, last_step + 1)
         def _(step):
-            on_core(step == 0, 0, prefill_a_start)
-            on_core(step == 0, 1, prefill_b_start)
-            for s in range(1, half + 1):
-                on_core(step == 4 * s - 1, 0, functools.partial(prefill_a, s))
-                on_core(step == 4 * s - 3, 1, functools.partial(prefill_b_chain, s))
-                on_core(step == 4 * s - 2, 1, functools.partial(prefill_b_on, s))
-                on_core(step == 4 * s - 1, 1, functools.partial(prefill_b_end, s))
-            on_core(step == last_step - 1, 0, prefill_a_end)
-            on_core(step == last_step - 2, 1, prefill_b_past)
-            on_core(step == last_step - 1, 1, prefill_b_past_end)
-            for s in range(half + 1):
-
-                @pl.when(step == 4 * s)
-                def _():
-                    from_sibling(behind[s])
-
-            @pl.when(step == last_step)
-            def _():
-                past_from_sibling()
-
-            back = step // 4
-            side = step // 2 % 2
+            for at_step in sorted(events):
+                for event in events[at_step]:
+                    on(step == at_step, event)
+
+            run = step // 2
             turn = step % 2
             is_last = step == last_step
-            plane = lax.rem(z - back + z_count, z_count)
+            own_rest = run == 2 * half + 1
+            back = jnp.where(own_rest, 0, jnp.where(is_last, half + 1, (run + 1) // 2))
+            side = jnp.where(run == 0, 0, (run + 1) % 2)
+            side = jnp.where(run == 2 * half - 1, 1, jnp.where(run == 2 * half, 0, side))
+            side = jnp.where(own_rest, 1, side)
+            slot = jnp.where(own_rest, 1, back % 2)
             reached = (z >= back) & jnp.logical_not(is_last)
-
-            def load(part):
+            edge = (z > half) & (at_block == 0)
+
+            def load(back, part, slot):
+                plane = lax.rem(z - back + z_count, z_count)
                 here = keys.at[plane, pl.ds(part * (y_count // 2), y_count // 2)]
-                return pltpu.make_async_copy(here, held.at[part], held_sems.at[part])
+                return pltpu.make_async_copy(here, held.at[slot, part], held_sems.at[slot, part])
 
             def load_past():
                 return pltpu.make_async_copy(
-                    keys.at[past, y_count - 1, 1], held.at[0, 0, 0], held_sems.at[0]
+                    keys.at[past, y_count - 1, 1], held.at[1, 0, 0, 0], held_sems.at[1, 0]
                 )
 
-            @pl.when(reached & (step % 4 == 0))
-            def _():
-                load(0).start()
-                load(1).start()
+            @pl.when(step == 0)
+            def _():
+                load(0, 0, 0).start()
+
+            for s in range(1, half + 1):
+
+                @pl.when((step == 4 * s - (2 if s == 1 else 3)) & (z >= s))
+                def _():
+                    load(s, 0, s % 2).start()
+                    load(s, 1, s % 2).start()
+
+            @pl.when(step == last_step - 4)
+            def _():
+                load(0, 1, 1).start()
+
+            @pl.when(edge & (step == last_step - 2))
+            def _():
+                load_past().start()
 
             @pl.when(reached & (turn == 0))
             def _():
-                load(side).wait()
+                load(back, side, slot).wait()
+
+            @pl.when(edge & is_last)
+            def _():
+                load_past().wait()
 
             mid = plane_blocks // 2
             rim_own = (back == 0) & (side == 1)
@@ -490,23 +484,16 @@
                 def _():
                     hide(first_spot, chunk)
 
-                @pl.loop(0, tiles // 2)
-                def _(tile):
-                    fold(turn * (tiles // 2) + tile, held[side].reshape(chunk, width))
-
-            edge = (z > half) & is_last & (at_block == 0)
-
-            @pl.when(edge)
-            def _():
-                load_past().start()
-                load_past().wait()
-
-            @pl.when(edge | (reached & few & (turn == 0)))
-            def _():
-                hide(jnp.where(is_last, first_spot + plane_keys - tokens, few_spot), tokens)
+                for tile in range(tiles // 2):
+                    fold(turn * (tiles // 2) + tile, held[slot, side].reshape(chunk, width))
+
+            @pl.when((edge & is_last) | (reached & few & (turn == 0)))
+            def _():
+                past_spot = (z - half - 1) * plane_keys + plane_keys - tokens
+                hide(jnp.where(is_last, past_spot, few_spot), tokens)
                 spot = jnp.where(rim_far, y_count - 1, 0)
                 block_keys = held[
-                    jnp.where(is_last, 0, side), spot // 2, spot % 2
+                    slot, jnp.where(is_last, 0, side), spot // 2, spot % 2
                 ].reshape(tokens, width)
 
                 @pl.loop(0, tiles)
@@ -520,10 +507,13 @@
             part = pl.ds(pl.multiple_of(head * tokens, tokens), tokens)
             norm = 1.0 / jnp.sum(total[part, :], axis=1, keepdims=True)
             q[head, :, :kv_rank] = (acc[part, :] * norm).astype(jnp.bfloat16)
-
-        done = pltpu.make_async_copy(q.at[:, :, pl.ds(0, kv_rank)], latent_out, out_sems.at[1])
-        done.start()
-        done.wait()
+            pltpu.make_async_copy(
+                q.at[head, :, pl.ds(0, kv_rank)], latent_out.at[head], out_sems.at[1]
+            ).start()
+
+        pltpu.make_async_copy(
+            q.at[:, :, pl.ds(0, kv_rank)], latent_out, out_sems.at[1]
+        ).wait()
         for copy in x_copies():
             copy.wait_send()
 
@@ -531,9 +521,10 @@
     def _():
         pltpu.make_async_copy(q, q_out, out_sems.at[0]).wait()
 
-    for (section_of, core_of), copies in went.items():
-
-        @pl.when((section == section_of) & (core == core_of))
+    groups = [section == 0, (section == 1) & (core == 0), (section == 1) & (core == 1)]
+    for group, copies in zip(groups, went):
+
+        @pl.when(group)
         def _():
             for copy in copies:
                 copy().wait_send()
@@ -572,11 +563,11 @@
             pltpu.VMEM((heads * tokens, kv_rank), jnp.float32),
             pltpu.VMEM((heads * tokens, LANES), jnp.float32),
             pltpu.VMEM((heads * tokens, LANES), jnp.float32),
-            pltpu.VMEM((2, y_count // 2, 2, 2, rows, width), bf16),
+            pltpu.VMEM((2, 2, y_count // 2, 2, 2, rows, width), bf16),
             pltpu.VMEM((tokens, chunk), jnp.float32),
             dma((2,)),
             dma((2,)),
-            dma((2,)),
+            dma((2, 2)),
             dma((4,)),
             dma((2,)),
             dma((3,)),

time: 133 us -> 118 us (0.89)
  Pallas kernels: 125 us -> 110 us
    pallas_call x1, Pallas kernels: 122 us -> 107 us  [prefill_part(): pl.pallas_call(functools.partial(prefill_kernel, z_count, y_count, kv_ran...]
where the time goes in v4:
time: 118 us
  Pallas kernels  110 us (93%)
  local copies, waits for them, and re-layouts  4.26 us (4%)
  matrix products  3.43 us (3%)
    pallas_call x1, Pallas kernels, prefill_part(): pl.pallas_call(functools.partial(prefill_kernel, z_count, y_count, kv_ran...  107 us
    dot_general x1, matrix products, shards(): jnp.einsum('htk,hkv->thv', latent_out, value_up_weight, preferred_element...  3.43 us
    pallas_call x1, Pallas kernels, shards(): pl.pallas_call(functools.partial(decode_kernel, kv_rank, groups, exponent...  2.9 us
    unnamed x3, local copies, waits for them, and re-layouts  2.61 us

profile of v4, /device:TPU:161, one launch (start us, length us, event | category | flops | bytes accessed | tf_op | source)
XLA Modules:
  0.0 117.7 jit_solution(5458526801202341009)
XLA Ops:
  0.0 2.6 %copy.12 = bf16[1,128,32,128]{3,1,2,0:T(8,128)(2,1)} copy(bf16[1,128,32,128]{3,2,1,0:T(8,128)(2,1)} %param.7) | data formatting | bytes 2097152 | tf_op args[0]
  2.6 107.1 %shard_map.73 = (bf16[8,4,2,2,64,576]{5,4,3,2,1,0:T(8,128)(2,1)}, bf16[2,64,576]{2,1,0:T(8,128)(2,1)}, bf16[32,128,576]{2,1,0:T(8,128)(2,1)}, bf16[32,128,512]{2,1,0:T(8,128)(2,1)}) custom-call(bf16[64,576]{1,0:T(8,128)(2,1)} %bitcast.20, bf16[32,128,128]{2,1,0:T(8,128)(2,1)} %bitcast.17, bf16[128,2048]{1,0:T(8,128)(2,1)} %bitcast.18, ...), custom_call_target="tpu_custom_call" | custom-call | tf_op jit(solution)/shard_map/pallas_call | solution.py:548
  109.7 0.0 copy-start
  109.7 2.9 %shard_map.74 = bf16[32,128,512]{2,1,0:T(8,128)(2,1)} custom-call(s32[32]{0:T(128)} %lengths.1, s32[256]{0:T(256)} %table.1, bf16[32,128,576]{2,1,0:T(8,128)(2,1)} %get-tuple-element.9.q_ref, bf16[8192,576]{1,0:T(8,128)(2,1)} %bitcast.16, bf16[128,576]{1,0:T(8,128)(2,1)} %bitcast.19, ...), custom_call_target="tpu_custom_call", output_to_operand_aliasing={{}: (5, {})} | custom-call | tf_op jit(solution)/shard_map/pallas_call | solution.py:772
  112.6 0.0 copy-done
  112.6 3.4 %fusion = bf16[1,128,32,128]{3,1,2,0:T(8,128)(2,1)S(1)} fusion(bf16[32,128,512]{2,1,0:T(8,128)(2,1)} %shard_map.74, bf16[32,512,128]{2,1,0:T(8,128)(2,1)S(1)} %copy-done), kind=kOutput, calls=%fused_computation.1 | convolution fusion | flops 537395200 | bytes 9437184 | tf_op jit(solution)/shard_map/htk,hkv->thv/dot_general | solution.py:808
  116.1 1.6 %copy.10 = bf16[1,128,32,128]{3,2,1,0:T(8,128)(2,1)} copy(bf16[1,128,32,128]{3,1,2,0:T(8,128)(2,1)S(1)} %fusion) | data formatting | bytes 2097152 | tf_op jit(solution)/shard_map/broadcast_in_dim | solution.py:811
Async XLA Ops:
  109.7 2.9 %copy-start = (bf16[32,512,128]{2,1,0:T(8,128)(2,1)S(1)}, bf16[32,512,128]{2,1,0:T(8,128)(2,1)}, u32[]{:S(2)}) copy-start(bf16[32,512,128]{2,1,0:T(8,128)(2,1)} %param.11) | copy-start | bytes 12582916

commit v5 on v4

--- a/solution.py
+++ b/solution.py
@@ -18,12 +18,18 @@
 
 KEY_BLOCK = 1024
 EDGE_BLOCK = 512
+
+CHAIN_STEPS = (0, 1, 3, 5)
+ON_STEPS = (0, 2, 5, 8)
+END_STEPS = (1, 3, 7, 10)
+SIBLING_STEPS = (2, 5, 9, 13)
+PAST_STEPS = (8, 10, 15)
 LANES = 128
 
 
 def prefill_kernel(
-    z_count, y_count, kv_rank, exponent_scale, own_in, q_nope, q_rope, up_key, lengths,
-    keys, own_out, q_out, latent_out, block, nope, up, q, acc, top, total, held, bias,
+    z_count, y_count, kv_rank, exponent_scale, own_in, q_nope, q_rope, up_key, value_up, lengths,
+    keys, own_out, q_out, out, block, nope, up, q, acc, top, total, held, bias, ready,
     in_sems, out_sems, held_sems, x_send, x_recv, own_sems,
     z_send, z_recv, y_send, y_recv, sib_send, sib_recv,
 ):
@@ -114,8 +120,8 @@
     def x_copies():
         spot = keys.at[z, y, hi, core]
         return [
+            remote(block, spot, device(to_hi=1 - hi), x_send.at[2], x_recv.at[1]),
             remote(block, spot, device(to_section=1), x_send.at[0], x_recv.at[0]),
-            remote(block, spot, device(to_hi=1 - hi), x_send.at[2], x_recv.at[1]),
             remote(block, spot, device(to_section=1, to_hi=1 - hi), x_send.at[1], x_recv.at[1]),
         ]
 
@@ -142,6 +148,13 @@
             lifted = lax.dot_general(nope[head], up[head], nt, preferred_element_type=jnp.float32)
             q[head, :, :kv_rank] = lifted.astype(jnp.bfloat16)
             q[head, :, kv_rank:] = rope[:, side * (LANES // 2) : (side + 1) * (LANES // 2)]
+
+    def load_value_up():
+        return pltpu.make_async_copy(value_up, up, in_sems.at[1])
+
+    @pl.when(section == 0)
+    def _():
+        load_value_up().start()
 
     @pl.when(section == 1)
     def _():
@@ -387,35 +400,32 @@
             preferred_element_type=jnp.float32,
         )
 
-    def hide(first_spot, count):
-        spot = first_spot + lax.broadcasted_iota(jnp.int32, (1, count), 1)
-        seen = (spot >= row_low) & (spot <= position)
-        bias[:, :count] = jnp.where(seen, 0.0, masked_low)
-
     def past_from_sibling():
         arrive(keys.at[past, low, 1, 1 - core], sib_recv.at[2 * (half - 1)])
 
     last_step = 4 * (half + 1)
-    events = {
-        0: [prefill_start],
-        1: [functools.partial(prefill_end, 1), functools.partial(prefill_chain, 2)],
-        last_step - 8: [prefill_past],
-        last_step - 6: [prefill_past_end],
-        last_step - 2: [past_from_sibling],
-    }
+    timetable = [
+        (prefill_chain, CHAIN_STEPS),
+        (prefill_on, ON_STEPS),
+        (prefill_end, END_STEPS),
+        (lambda s: from_sibling(behind[s]), SIBLING_STEPS),
+    ]
+    events = {0: [prefill_start]}
     for s in range(1, half + 1):
-        if s > 1:
-            events.setdefault(4 * s - 5 - (s > 3), []).append(functools.partial(prefill_on, s))
-            events.setdefault(4 * s - 4 - (s > 3), []).append(functools.partial(prefill_end, s))
-        if s > 2:
-            events.setdefault(3 * s - 5, []).append(functools.partial(prefill_chain, s))
-        events.setdefault(4 * s - (2 if s == 1 else 3), []).append(
-            functools.partial(from_sibling, behind[s])
-        )
+        for event, at_steps in timetable:
+            if at_steps[s - 1] > 0:
+                spot = events.setdefault(at_steps[s - 1], [])
+                spot.append(functools.partial(event, s))
+    for event, at_step in zip((prefill_past, prefill_past_end, past_from_sibling), PAST_STEPS):
+        events.setdefault(at_step, []).append(event)
 
     @pl.when(section == 0)
     def _():
-        @pl.loop(0, last_step + 1)
+        mid = plane_blocks // 2
+        at_first, at_mid = at_block == 0, at_block == mid
+        reaches_past = at_first & (z > half)
+
+        @pl.loop(0, last_step)
         def _(step):
             for at_step in sorted(events):
                 for event in events[at_step]:
@@ -423,97 +433,120 @@
 
             run = step // 2
             turn = step % 2
-            is_last = step == last_step
-            own_rest = run == 2 * half + 1
-            back = jnp.where(own_rest, 0, jnp.where(is_last, half + 1, (run + 1) // 2))
+            rest = run == 2 * half + 1
+            back = jnp.where(rest, 0, (run + 1) // 2)
             side = jnp.where(run == 0, 0, (run + 1) % 2)
-            side = jnp.where(run == 2 * half - 1, 1, jnp.where(run == 2 * half, 0, side))
-            side = jnp.where(own_rest, 1, side)
-            slot = jnp.where(own_rest, 1, back % 2)
-            reached = (z >= back) & jnp.logical_not(is_last)
-            edge = (z > half) & (at_block == 0)
-
-            def load(back, part, slot):
+            side = jnp.where(rest, 1, side)
+            slot = jnp.where(rest, 1, back % 2)
+            reached = z >= back
+
+            def load(back, part, slot, into):
                 plane = lax.rem(z - back + z_count, z_count)
                 here = keys.at[plane, pl.ds(part * (y_count // 2), y_count // 2)]
-                return pltpu.make_async_copy(here, held.at[slot, part], held_sems.at[slot, part])
-
-            def load_past():
+                return pltpu.make_async_copy(here, held.at[slot, into], held_sems.at[slot, into])
+
+            def load_first():
                 return pltpu.make_async_copy(
                     keys.at[past, y_count - 1, 1], held.at[1, 0, 0, 0], held_sems.at[1, 0]
                 )
 
+            def load_mid():
+                return pltpu.make_async_copy(
+                    keys.at[planes[-1], y_count // 2 - 1, 1],
+                    held.at[1, 1, y_count // 2 - 1, 1],
+                    held_sems.at[1, 0],
+                )
+
             @pl.when(step == 0)
             def _():
-                load(0, 0, 0).start()
+                load(0, 0, 0, 0).start()
 
             for s in range(1, half + 1):
 
-                @pl.when((step == 4 * s - (2 if s == 1 else 3)) & (z >= s))
+                @pl.when((step == SIBLING_STEPS[s - 1]) & (z >= s))
                 def _():
-                    load(s, 0, s % 2).start()
-                    load(s, 1, s % 2).start()
-
-            @pl.when(step == last_step - 4)
-            def _():
-                load(0, 1, 1).start()
-
-            @pl.when(edge & (step == last_step - 2))
-            def _():
-                load_past().start()
-
-            @pl.when(reached & (turn == 0))
-            def _():
-                load(back, side, slot).wait()
-
-            @pl.when(edge & is_last)
-            def _():
-                load_past().wait()
-
-            mid = plane_blocks // 2
-            rim_own = (back == 0) & (side == 1)
-            rim_far = (back == half) & (side == 0)
-            few = (rim_own | rim_far) & (at_block == mid)
-            none = (rim_own & (at_block < mid)) | (rim_far & (at_block > mid))
+                    load(s, 0, s % 2, 0).start()
+                    load(s, 1, s % 2, 1).start()
+
+            @pl.when(step == last_step - 5)
+            def _():
+                @pl.when(reaches_past)
+                def _():
+                    load_first().start()
+
+                @pl.when(at_block >= mid)
+                def _():
+                    rest_load = load(0, 1, 1, 1)
+                    rest_load.start()
+                    rest_load.wait()
+
+                @pl.when(at_mid)
+                def _():
+                    load_mid().start()
+
+            @pl.when(reached & (turn == 0) & jnp.logical_not(rest))
+            def _():
+                load(back, side, slot, side).wait()
+
+            at_past = reaches_past & (run == 2 * half)
+
+            @pl.when(at_past & (turn == 0))
+            def _():
+                load_first().wait()
+
+            @pl.when((turn == 0) & rest & at_mid)
+            def _():
+                load_mid().wait()
+
+            none = (rest & (at_block < mid)) | ((run == 2 * half - 1) & (at_block >= mid))
             first_spot = (z - back) * plane_keys + side * chunk
-            few_spot = jnp.where(rim_far, first_spot + chunk - tokens, first_spot)
-
-            @pl.when(reached & jnp.logical_not(few | none))
+
+            @pl.when(reached & jnp.logical_not(none))
             def _():
                 @pl.when(turn == 0)
                 def _():
-                    hide(first_spot, chunk)
-
-                for tile in range(tiles // 2):
-                    fold(turn * (tiles // 2) + tile, held[slot, side].reshape(chunk, width))
-
-            @pl.when((edge & is_last) | (reached & few & (turn == 0)))
-            def _():
-                past_spot = (z - half - 1) * plane_keys + plane_keys - tokens
-                hide(jnp.where(is_last, past_spot, few_spot), tokens)
-                spot = jnp.where(rim_far, y_count - 1, 0)
-                block_keys = held[
-                    slot, jnp.where(is_last, 0, side), spot // 2, spot % 2
-                ].reshape(tokens, width)
-
-                @pl.loop(0, tiles)
-                def _(tile):
-                    fold(tile, block_keys)
+                    lane = lax.broadcasted_iota(jnp.int32, (1, chunk + tokens), 1)
+                    spot = first_spot + lane
+                    shift = (half * plane_keys) + chunk
+                    spot = jnp.where(
+                        rest & at_mid & (lane >= chunk - tokens), spot - shift, spot
+                    )
+                    spot = jnp.where(lane >= chunk, spot - plane_keys - tokens, spot)
+                    seen = (spot >= row_low) & (spot <= position)
+                    bias[...] = jnp.where(seen, 0.0, masked_low)
+
+                here = held.at[slot, side]
+
+                @pl.when(at_past)
+                def _():
+                    behind_it = held[1, 0, 0, 0].reshape(tokens, width)
+                    key_block = jnp.concatenate([here[...].reshape(chunk, width), behind_it])
+
+                    @pl.loop(0, tiles // 2)
+                    def _(tile):
+                        fold(turn * (tiles // 2) + tile, key_block)
+
+                @pl.when(jnp.logical_not(at_past))
+                def _():
+                    for tile in range(tiles // 2):
+                        fold(turn * (tiles // 2) + tile, here[...].reshape(chunk, width))
 
     @pl.when(section == 0)
     def _():
+        load_value_up().wait()
+
         @pl.loop(0, heads)
         def _(head):
             part = pl.ds(pl.multiple_of(head * tokens, tokens), tokens)
             norm = 1.0 / jnp.sum(total[part, :], axis=1, keepdims=True)
-            q[head, :, :kv_rank] = (acc[part, :] * norm).astype(jnp.bfloat16)
-            pltpu.make_async_copy(
-                q.at[head, :, pl.ds(0, kv_rank)], latent_out.at[head], out_sems.at[1]
-            ).start()
-
-        pltpu.make_async_copy(
-            q.at[:, :, pl.ds(0, kv_rank)], latent_out, out_sems.at[1]
-        ).wait()
+            mixed = (acc[part, :] * norm).astype(jnp.bfloat16)
+            ready[head] = jnp.dot(mixed, up[head], preferred_element_type=jnp.float32).astype(
+                jnp.bfloat16
+            )
+
+        done = pltpu.make_async_copy(ready, out, out_sems.at[1])
+        done.start()
+        done.wait()
         for copy in x_copies():
             copy.wait_send()
 
@@ -534,7 +567,7 @@
     own_local().wait()
 
 
-def prefill_part(own, q_nope, q_rope, up_key, lengths, seq_count, exponent_scale):
+def prefill_part(own, q_nope, q_rope, up_key, value_up, lengths, seq_count, exponent_scale):
     rows, width = own.shape
     heads, tokens, _ = q_nope.shape
     kv_rank = up_key.shape[1]
@@ -551,9 +584,9 @@
             jax.ShapeDtypeStruct((z_count, y_count, 2, 2, rows, width), bf16),
             jax.ShapeDtypeStruct((2, rows, width), bf16),
             jax.ShapeDtypeStruct((heads, tokens, width), bf16),
-            jax.ShapeDtypeStruct((heads, tokens, kv_rank), bf16),
+            jax.ShapeDtypeStruct((heads, tokens, value_up.shape[2]), bf16),
         ],
-        in_specs=[vmem, hbm, vmem, hbm, vmem],
+        in_specs=[vmem, hbm, vmem, hbm, hbm, vmem],
         out_specs=[hbm] * 4,
         scratch_shapes=[
             pltpu.VMEM((rows, width), bf16),
@@ -564,7 +597,8 @@
             pltpu.VMEM((heads * tokens, LANES), jnp.float32),
             pltpu.VMEM((heads * tokens, LANES), jnp.float32),
             pltpu.VMEM((2, 2, y_count // 2, 2, 2, rows, width), bf16),
-            pltpu.VMEM((tokens, chunk), jnp.float32),
+            pltpu.VMEM((tokens, chunk + tokens), jnp.float32),
+            pltpu.VMEM((heads, tokens, value_up.shape[2]), bf16),
             dma((2,)),
             dma((2,)),
             dma((2, 2)),
@@ -581,7 +615,7 @@
         compiler_params=pltpu.CompilerParams(
             collective_id=0, has_side_effects=True, vmem_limit_bytes=56 << 20
         ),
-    )(own, q_nope, q_rope, up_key, lengths)
+    )(own, q_nope, q_rope, up_key, value_up, lengths)
 
 
 def over_lanes(value, width):
@@ -597,17 +631,20 @@
     q_ref,
     keys,
     own_keys,
+    value_up,
     _,
     out_ref,
     acc,
     top,
     total,
     held,
+    lat,
+    up,
     ready,
     q_held,
     sems,
     q_sems,
-    out_sems,
+    up_sems,
 ):
     band = pl.program_id(0)
     bands = pl.num_programs(0)
@@ -640,11 +677,8 @@
                 q_ref.at[:, band_rows(which), :], q_held.at[slot], q_sems.at[slot]
             )
 
-        def leave(which):
-            slot = lax.rem(which, 2)
-            return pltpu.make_async_copy(
-                ready.at[slot], out_ref.at[:, band_rows(which), :], out_sems.at[slot]
-            )
+        def load_up():
+            return pltpu.make_async_copy(value_up, up, up_sems.at[0])
 
         low, last = prompt_range(band)
         first = low // 16 * 16
@@ -658,6 +692,7 @@
         def _():
             fetch_q(0).start()
             fetch(0).start()
+            load_up().start()
 
         @pl.when(band + 1 < bands)
         def _():
@@ -667,44 +702,61 @@
 
         fetch_q(band).wait()
         q = q_held[lax.rem(band, 2)].reshape(rows, width)
-        own = own_keys[...]
-        scores = lax.dot_general(q, own, nt, preferred_element_type=jnp.float32)
-        asked = lax.broadcasted_iota(jnp.int32, (tokens, tokens), 0)
-        key = lax.broadcasted_iota(jnp.int32, (tokens, tokens), 1)
-        seen = (asked % SAMPLES == key % SAMPLES) & (key // SAMPLES <= asked // SAMPLES)
-        bias = jnp.where(seen, 0.0, masked_low)
-        bias = jnp.broadcast_to(bias[None], (heads, tokens, tokens)).reshape(rows, tokens)
-        scores = scores + bias
-        own_top = jnp.max(scores, axis=1, keepdims=True)
-        expo = jnp.exp2((scores - own_top) * exponent_scale)
-        lane = lax.broadcasted_iota(jnp.int32, (rows, LANES), 1)
-        total[...] = jnp.where(lane == 0, jnp.sum(expo, axis=1, keepdims=True), 0.0)
-        top[...] = jnp.broadcast_to(own_top, (rows, LANES))
-        acc[...] = jnp.dot(
-            expo.astype(jnp.bfloat16), own[:, :kv_rank], preferred_element_type=jnp.float32
-        )
+        def score(key_block):
+            return lax.dot_general(q, key_block, nt, preferred_element_type=jnp.float32)
+
+        def in_range(at, count, low_spot):
+            spot = at + lax.broadcasted_iota(jnp.int32, (1, count), 1)
+            return jnp.where((spot >= jnp.maximum(low, low_spot)) & (spot < last), 0.0, masked_low)
+
+        def weigh(scores, now):
+            return jnp.exp2((scores - now) * exponent_scale)
+
+        def mix(weights, key_block):
+            return jnp.dot(
+                weights.astype(jnp.bfloat16),
+                key_block[:, :kv_rank],
+                preferred_element_type=jnp.float32,
+            )
+
+        def begin(key_block, at):
+            own = own_keys[...]
+            asked = lax.broadcasted_iota(jnp.int32, (tokens, tokens), 0)
+            key = lax.broadcasted_iota(jnp.int32, (tokens, tokens), 1)
+            seen = (asked % SAMPLES == key % SAMPLES) & (key // SAMPLES <= asked // SAMPLES)
+            bias = jnp.where(seen, 0.0, masked_low)
+            bias = jnp.broadcast_to(bias[None], (heads, tokens, tokens)).reshape(rows, tokens)
+            new = score(own) + bias
+            count = key_block.shape[0]
+            old = score(key_block) + in_range(at, count, low)
+            now = jnp.maximum(
+                jnp.max(new, axis=1, keepdims=True), jnp.max(old, axis=1, keepdims=True)
+            )
+            new = weigh(new, now)
+            old = weigh(old, now)
+            top[...] = jnp.broadcast_to(now, (rows, LANES))
+            lane = lax.broadcasted_iota(jnp.int32, (rows, LANES), 1)
+            summed = jnp.where(lane == 0, jnp.sum(new, axis=1, keepdims=True), 0.0)
+            for c in range(0, count, LANES):
+                summed = summed + old[:, c : c + LANES]
+            total[...] = summed
+            acc[...] = mix(new, own) + mix(old, key_block)
 
         def fold(key_block, low_spot, at):
             count = key_block.shape[0]
-            s = lax.dot_general(q, key_block, nt, preferred_element_type=jnp.float32)
+            s = score(key_block)
             if low_spot is not None:
-                spot = at + lax.broadcasted_iota(jnp.int32, (1, count), 1)
-                here = (spot >= jnp.maximum(low, low_spot)) & (spot < last)
-                s = s + jnp.where(here, 0.0, masked_low)
+                s = s + in_range(at, count, low_spot)
             before = top[...]
             now = jnp.maximum(before, jnp.max(s, axis=1, keepdims=True))
             shrink = jnp.exp2((before - now) * exponent_scale)
-            expo = jnp.exp2((s - over_lanes(now, count)) * exponent_scale)
+            expo = weigh(s, over_lanes(now, count))
             top[...] = now
             summed = total[...] * shrink
             for c in range(0, count, LANES):
                 summed = summed + expo[:, c : c + LANES]
             total[...] = summed
-            acc[...] = acc[...] * over_lanes(shrink, kv_rank) + jnp.dot(
-                expo.astype(jnp.bfloat16),
-                key_block[:, :kv_rank],
-                preferred_element_type=jnp.float32,
-            )
+            acc[...] = acc[...] * over_lanes(shrink, kv_rank) + mix(expo, key_block)
 
         @pl.loop(0, chunks)
         def _(i):
@@ -717,7 +769,13 @@
 
             nominal = first + i * KEY_BLOCK
             at = chunk_at(first, i)
-            whole = (nominal >= low) & (nominal + KEY_BLOCK <= last)
+            whole = (i > 0) & (nominal + KEY_BLOCK <= last)
+            skip = (nominal - at) // EDGE_BLOCK
+
+            @pl.when(i == 0)
+            def _():
+                here = pl.multiple_of(skip * EDGE_BLOCK, EDGE_BLOCK)
+                begin(held[slot, pl.ds(here, EDGE_BLOCK), :], at + here)
 
             @pl.when(whole)
             def _():
@@ -725,27 +783,31 @@
 
             @pl.when(jnp.logical_not(whole))
             def _():
-                skip = (nominal - at) // EDGE_BLOCK
-
-                @pl.loop(skip, (jnp.minimum(last - at, KEY_BLOCK) + EDGE_BLOCK - 1) // EDGE_BLOCK)
+                begun = skip + jnp.where(i == 0, 1, 0)
+
+                @pl.loop(begun, (jnp.minimum(last - at, KEY_BLOCK) + EDGE_BLOCK - 1) // EDGE_BLOCK)
                 def _(j):
                     here = pl.multiple_of(j * EDGE_BLOCK, EDGE_BLOCK)
                     fold(held[slot, pl.ds(here, EDGE_BLOCK), :], nominal, at + here)
 
         norm = 1.0 / jnp.sum(total[...], axis=1, keepdims=True)
-        @pl.when(band >= 2)
-        def _():
-            leave(band - 2).wait()
-
-        ready[lax.rem(band, 2)] = (
+        lat[:, band_rows(band), :] = (
             (acc[...] * norm).astype(jnp.bfloat16).reshape(heads, tokens, kv_rank)
         )
-        leave(band).start()
 
         @pl.when(band == bands - 1)
         def _():
-            leave(band - 1).wait()
-            leave(band).wait()
+            load_up().wait()
+
+            @pl.loop(0, heads)
+            def _(head):
+                ready[head] = jnp.dot(
+                    lat[head], up[head], preferred_element_type=jnp.float32
+                ).astype(jnp.bfloat16)
+
+            done = pltpu.make_async_copy(ready, out_ref, up_sems.at[1])
+            done.start()
+            done.wait()
 
 
 def shards(query_nope, query_rope, latent, up_key, value_up_weight, lengths, owner_request_table):
@@ -759,19 +821,20 @@
     band_tokens = tok_dev // req_dev
     exponent_scale = math.log2(math.e) / math.sqrt(nope_dim + rope_dim)
 
-    keys, pair, queries, latent_out = prefill_part(
+    keys, pair, queries, prefill_out = prefill_part(
         latent[0],
         query_nope[0].swapaxes(0, 1),
         query_rope[0],
         up_key,
+        value_up_weight,
         lengths[None, :],
         seq_count,
         exponent_scale,
     )
     rows = head_dev * band_tokens
-    latent_out = pl.pallas_call(
+    attended = pl.pallas_call(
         functools.partial(decode_kernel, kv_rank, groups, exponent_scale),
-        out_shape=jax.ShapeDtypeStruct((head_dev, tok_dev, kv_rank), jnp.bfloat16),
+        out_shape=jax.ShapeDtypeStruct(prefill_out.shape, jnp.bfloat16),
         grid_spec=pltpu.PrefetchScalarGridSpec(
             num_scalar_prefetch=2,
             grid=(req_dev,),
@@ -780,6 +843,7 @@
                 pl.BlockSpec(memory_space=pl.ANY),
                 pl.BlockSpec((band_tokens, width), lambda i, *_: (i, 0)),
                 pl.BlockSpec(memory_space=pl.ANY),
+                pl.BlockSpec(memory_space=pl.ANY),
             ],
             out_specs=pl.BlockSpec(memory_space=pl.ANY),
             scratch_shapes=[
@@ -787,14 +851,16 @@
                 pltpu.VMEM((rows, LANES), jnp.float32),
                 pltpu.VMEM((rows, LANES), jnp.float32),
                 pltpu.VMEM((4, KEY_BLOCK, width), jnp.bfloat16),
-                pltpu.VMEM((2, head_dev, band_tokens, kv_rank), jnp.bfloat16),
+                pltpu.VMEM((head_dev, tok_dev, kv_rank), jnp.bfloat16),
+                pltpu.VMEM(value_up_weight.shape, jnp.bfloat16),
+                pltpu.VMEM(prefill_out.shape, jnp.bfloat16),
                 pltpu.VMEM((2, head_dev, band_tokens, width), jnp.bfloat16),
                 pltpu.SemaphoreType.DMA((4,)),
                 pltpu.SemaphoreType.DMA((2,)),
                 pltpu.SemaphoreType.DMA((2,)),
             ],
         ),
-        input_output_aliases={5: 0},
+        input_output_aliases={6: 0},
         compiler_params=pltpu.CompilerParams(vmem_limit_bytes=58 << 20),
     )(
         lengths,
@@ -802,13 +868,11 @@
         queries,
         keys.reshape(-1, width),
         pair.reshape(-1, width),
-        latent_out,
+        value_up_weight,
+        prefill_out,
     )
 
-    attended = jnp.einsum(
-        "htk,hkv->thv", latent_out, value_up_weight, preferred_element_type=jnp.float32
-    )
-    return attended.astype(jnp.bfloat16)[None]
+    return attended.swapaxes(0, 1)[None]
 
 
 def solution(mesh):

time: 118 us -> 117 us (level)
  matrix products: 3.43 us -> 0 us
  local copies, waits for them, and re-layouts: 4.26 us -> 5.47 us
    dot_general x1 -> x0, matrix products: 3.43 us -> none  [shards(): jnp.einsum('htk,hkv->thv', latent_out, value_up_weight, preferred_element...]
    pallas_call x1, Pallas kernels: 107 us -> 108 us  [prefill_part(): pl.pallas_call(functools.partial(prefill_kernel, z_count, y_count, kv_ran...]
    broadcast_in_dim x1, local copies, waits for them, and re-layouts: 1.65 us -> 2.87 us  [shards(): return attended.swapaxes(0, 1)[None]]
    unnamed x3 -> x1, local copies, waits for them, and re-layouts: 2.61 us -> 2.6 us
where the time goes in v5:
time: 117 us; the launch traced here: 116 us
  Pallas kernels  111 us (95%)
  local copies, waits for them, and re-layouts  5.47 us (5%)
    pallas_call x1, Pallas kernels, prefill_part(): pl.pallas_call(functools.partial(prefill_kernel, z_count, y_count, kv_ran...  108 us
    broadcast_in_dim x1, local copies, waits for them, and re-layouts, shards(): return attended.swapaxes(0, 1)[None]  2.87 us
    unnamed x1, local copies, waits for them, and re-layouts  2.6 us
    pallas_call x1, Pallas kernels, shards(): pl.pallas_call(functools.partial(decode_kernel, kv_rank, groups, exponent...  2.36 us

profile of v5, /device:TPU:161, one launch (start us, length us, event | category | flops | bytes accessed | tf_op | source)
XLA Modules:
  0.0 116.2 jit_solution(8893819756771647980)
XLA Ops:
  0.0 2.6 %copy.12 = bf16[1,128,32,128]{3,1,2,0:T(8,128)(2,1)} copy(bf16[1,128,32,128]{3,2,1,0:T(8,128)(2,1)} %param.7) | data formatting | bytes 2097152 | tf_op args[0]
  2.6 108.3 %shard_map.73 = (bf16[8,4,2,2,64,576]{5,4,3,2,1,0:T(8,128)(2,1)}, bf16[2,64,576]{2,1,0:T(8,128)(2,1)}, bf16[32,128,576]{2,1,0:T(8,128)(2,1)}, bf16[32,128,128]{2,1,0:T(8,128)(2,1)}) custom-call(bf16[64,576]{1,0:T(8,128)(2,1)} %bitcast.18, bf16[32,128,128]{2,1,0:T(8,128)(2,1)} %bitcast.15, bf16[128,2048]{1,0:T(8,128)(2,1)} %bitcast.16, ...), custom_call_target="tpu_custom_call" | custom-call | tf_op jit(solution)/shard_map/pallas_call | solution.py:581
  110.9 2.4 %shard_map.74 = bf16[32,128,128]{2,1,0:T(8,128)(2,1)} custom-call(s32[32]{0:T(128)} %lengths.1, s32[256]{0:T(256)} %table.1, bf16[32,128,576]{2,1,0:T(8,128)(2,1)} %get-tuple-element.9.q_ref, bf16[8192,576]{1,0:T(8,128)(2,1)} %bitcast.13, bf16[128,576]{1,0:T(8,128)(2,1)} %bitcast.17, bf16[32,512,128]{2,1,0:T(8,128)(2,1)} %value_up.3, ...), custom_call_target="tpu_custom_call", output_to_operand_aliasing={{}: (6, {})} | custom-call | tf_op jit(solution)/shard_map/pallas_call | solution.py:835
  113.3 2.9 %copy.10 = bf16[1,128,32,128]{3,2,1,0:T(8,128)(2,1)} copy(bf16[1,128,32,128]{3,1,2,0:T(8,128)(2,1)} %bitcast.14) | data formatting | bytes 2097152 | tf_op jit(solution)/shard_map/broadcast_in_dim | solution.py:875

commit v6 on v5

--- a/solution.py
+++ b/solution.py
@@ -18,6 +18,7 @@
 
 KEY_BLOCK = 1024
 EDGE_BLOCK = 512
+FAR_HEADS = 8
 
 CHAIN_STEPS = (0, 1, 3, 5)
 ON_STEPS = (0, 2, 5, 8)
@@ -29,7 +30,8 @@
 
 def prefill_kernel(
     z_count, y_count, kv_rank, exponent_scale, own_in, q_nope, q_rope, up_key, value_up, lengths,
-    keys, own_out, q_out, out, block, nope, up, q, acc, top, total, held, bias, ready,
+    keys, own_out, q_out, out, block, nope, up, q, far_nope, far_rope, far_q, acc, top, total,
+    held, bias, ready, far_send, far_recv,
     in_sems, out_sems, held_sems, x_send, x_recv, own_sems,
     z_send, z_recv, y_send, y_recv, sib_send, sib_recv,
 ):
@@ -140,14 +142,45 @@
     for load in loads:
         load.wait()
 
-    @pl.loop(0, heads // 2)
-    def _(pair):
-        rope = q_rope[:, pl.ds(pl.multiple_of(pair * LANES, LANES), LANES)]
-        for side in range(2):
-            head = pair * 2 + side
-            lifted = lax.dot_general(nope[head], up[head], nt, preferred_element_type=jnp.float32)
-            q[head, :, :kv_rank] = lifted.astype(jnp.bfloat16)
-            q[head, :, kv_rank:] = rope[:, side * (LANES // 2) : (side + 1) * (LANES // 2)]
+    near = heads - FAR_HEADS
+    half_lanes = LANES // 2
+
+    def far_copies():
+        to = device(to_section=1 - section)
+        rope_part = q_rope.at[:, pl.ds(near * half_lanes, FAR_HEADS * half_lanes)]
+        return [
+            remote(nope.at[pl.ds(near, FAR_HEADS)], far_nope, to, far_send.at[0], far_recv.at[0]),
+            remote(rope_part, far_rope, to, far_send.at[1], far_recv.at[1]),
+        ]
+
+    def far_result():
+        part = ready.at[pl.ds(near, FAR_HEADS)]
+        return remote(part, part, device(to_section=1 - section), far_send.at[2], far_recv.at[2])
+
+    @pl.when(section == 0)
+    def _():
+        for copy in far_copies():
+            copy.start()
+
+    def absorb(from_nope, from_rope, into, first, count):
+        @pl.loop(0, count // 2)
+        def _(pair):
+            rope = from_rope[:, pl.ds(pl.multiple_of(pair * LANES, LANES), LANES)]
+            for side in range(2):
+                head = pair * 2 + side
+                lifted = lax.dot_general(
+                    from_nope[head], up[first + head], nt, preferred_element_type=jnp.float32
+                )
+                into[head, :, :kv_rank] = lifted.astype(jnp.bfloat16)
+                into[head, :, kv_rank:] = rope[:, side * half_lanes : (side + 1) * half_lanes]
+
+    @pl.when(section == 0)
+    def _():
+        absorb(nope, q_rope, q, 0, near)
+
+    @pl.when(section == 1)
+    def _():
+        absorb(nope, q_rope, q, 0, heads)
 
     def load_value_up():
         return pltpu.make_async_copy(value_up, up, in_sems.at[1])
@@ -223,9 +256,10 @@
             lambda: z_recv.at[j, step, k],
         )
 
-    def decode_a():
+    ways = ((0, True), (1, False))
+
+    def decode_a(stage):
         send = sender(went[1])
-        ways = ((0, True), (1, False))
 
         def cell(n, k):
             return lambda: keys.at[planes[n], columns[k], :, 0]
@@ -234,32 +268,33 @@
             for _, up_way in ways:
                 along_z(send, cell(0, k), up_way, 0, k)
 
-        spread(send, 0, 0)
-        column(0)
-        arrive(keys.at[z, low, :, 0], y_recv.at[0, 0])
-        along_y(send, 0, 0, lambda: keys.at[z, low, 0, 0], 1, 2)
-        column(1)
-        arrive(keys.at[z, high, :, 0], y_recv.at[0, 1])
-        along_y(send, 0, 0, lambda: keys.at[z, high, 1, 0], -1, 3)
-        column(2)
-        spread_end(0, 0)
-        column(3)
-        to_sibling(send, 0, 0)
-        for s in range(1, half):
+        if stage == 0:
+            spread(send, 0, 0)
+            column(0)
+            arrive(keys.at[z, low, :, 0], y_recv.at[0, 0])
+            along_y(send, 0, 0, lambda: keys.at[z, low, 0, 0], 1, 2)
+            column(1)
+            arrive(keys.at[z, high, :, 0], y_recv.at[0, 1])
+            along_y(send, 0, 0, lambda: keys.at[z, high, 1, 0], -1, 3)
+            column(2)
+            spread_end(0, 0)
+            column(3)
+            to_sibling(send, 0, 0)
+        elif stage < half:
             for k in range(y_count):
-                for n, (j, up_way) in zip(steps[s], ways):
-                    arrive(cell(n, k)(), z_recv.at[j, s - 1, k])
-                    if s < half - 1 or k // 2 == j:
-                        along_z(send, cell(n, k), up_way, s, k)
-            for n in steps[s]:
+                for n, (j, up_way) in zip(steps[stage], ways):
+                    arrive(cell(n, k)(), z_recv.at[j, stage - 1, k])
+                    if stage < half - 1 or k // 2 == j:
+                        along_z(send, cell(n, k), up_way, stage, k)
+            for n in steps[stage]:
                 to_sibling(send, n, 0)
-        for k in range(y_count):
-            arrive(cell(z_count - 1, k)(), z_recv.at[k // 2, half - 1, k])
-        to_sibling(send, z_count - 1, 0)
-
-    def decode_b():
+        else:
+            for k in range(y_count):
+                arrive(cell(z_count - 1, k)(), z_recv.at[k // 2, half - 1, k])
+            to_sibling(send, z_count - 1, 0)
+
+    def decode_b(stage):
         send = sender(went[2])
-        ways = ((0, True), (1, False))
 
         def ahead(n, s, j, up_way):
             if s < half - 1:
@@ -268,26 +303,35 @@
                 part = lambda: keys.at[planes[n], y, j, 1]
             along_z(send, part, up_way, s, 0)
 
-        for j, up_way in ways:
-            ahead(0, 0, j, up_way)
-        spread(send, 0, 1)
-        for s in range(1, half):
+        def chain(s):
             for n, (j, up_way) in zip(steps[s], ways):
                 arrive(keys.at[planes[n], y, :, 1], z_recv.at[j, s - 1, 0])
                 ahead(n, s, j, up_way)
                 spread(send, n, 1)
-            if s == 1:
-                spread_on(send, 0, 1)
-        for j in range(2):
-            arrive(keys.at[planes[-1], y, j, 1], z_recv.at[j, half - 1, 0])
-        spread(send, z_count - 1, 1)
-        for n in range(z_count):
-            if n >= 1:
-                spread_on(send, n, 1)
-                spread_end(n - 1, 1)
-                to_sibling(send, n - 1, 1)
-        spread_end(z_count - 1, 1)
-        to_sibling(send, z_count - 1, 1)
+
+        def finish(s):
+            for n in steps[s]:
+                spread_end(n, 1)
+                to_sibling(send, n, 1)
+
+        if stage == 0:
+            for j, up_way in ways:
+                ahead(0, 0, j, up_way)
+            spread(send, 0, 1)
+            chain(1)
+            spread_on(send, 0, 1)
+            return
+        if stage + 1 < half:
+            chain(stage + 1)
+        elif stage + 1 == half:
+            for j in range(2):
+                arrive(keys.at[planes[-1], y, j, 1], z_recv.at[j, half - 1, 0])
+            spread(send, z_count - 1, 1)
+        for n in steps[stage]:
+            spread_on(send, n, 1)
+        finish(stage - 1)
+        if stage == half:
+            finish(stage)
 
     behind = [0] + [2 * s - 1 for s in range(1, half)] + [z_count - 1]
     past = planes[2 * (half - 1)]
@@ -346,18 +390,9 @@
         def _():
             event()
 
-    @pl.when(section == 1)
-    def _():
-        on(core == 0, decode_a)
-        on(core == 1, decode_b)
-        for n in range(z_count):
-            from_sibling(n)
-
-    @pl.when(section == 0)
-    def _():
-        top[...] = jnp.full(top.shape, masked_low, jnp.float32)
-        total[...] = jnp.zeros(total.shape, jnp.float32)
-        acc[...] = jnp.zeros(acc.shape, jnp.float32)
+    top[...] = jnp.full(top.shape, masked_low, jnp.float32)
+    total[...] = jnp.zeros(total.shape, jnp.float32)
+    acc[...] = jnp.zeros(acc.shape, jnp.float32)
 
     token = lax.broadcasted_iota(jnp.int32, (tokens, 1), 0)
     position = seq * tokens + token
@@ -375,14 +410,14 @@
     ).astype(jnp.int32)
 
     chunk = plane_keys // 2
-    tile_heads = 8
-    rows = tile_heads * tokens
-    tiles = heads // tile_heads
-
-    def fold(tile, key_block):
+    tile_heads = near // 2
+
+    def fold(asked_heads, tile, key_block):
         count = key_block.shape[0]
+        tile_heads = asked_heads.shape[0]
+        rows = tile_heads * tokens
         part = pl.ds(pl.multiple_of(tile * rows, rows), rows)
-        asked = q[pl.ds(tile * tile_heads, tile_heads)].reshape(rows, width)
+        asked = asked_heads[...].reshape(rows, width)
         s = lax.dot_general(asked, key_block, nt, preferred_element_type=jnp.float32)
         s = (s.reshape(tile_heads, tokens, count) + bias[:, :count][None]).reshape(rows, count)
         before = top[part, :]
@@ -516,43 +551,114 @@
                     bias[...] = jnp.where(seen, 0.0, masked_low)
 
                 here = held.at[slot, side]
+                tile_q = q.at[pl.ds(turn * tile_heads, tile_heads)]
 
                 @pl.when(at_past)
                 def _():
                     behind_it = held[1, 0, 0, 0].reshape(tokens, width)
                     key_block = jnp.concatenate([here[...].reshape(chunk, width), behind_it])
 
-                    @pl.loop(0, tiles // 2)
-                    def _(tile):
-                        fold(turn * (tiles // 2) + tile, key_block)
+                    fold(tile_q, turn, key_block)
 
                 @pl.when(jnp.logical_not(at_past))
                 def _():
-                    for tile in range(tiles // 2):
-                        fold(turn * (tiles // 2) + tile, here[...].reshape(chunk, width))
+                    fold(tile_q, turn, here[...].reshape(chunk, width))
+
+    def far_run(run):
+        rest, beyond = run == 2 * half + 1, run == 2 * half + 2
+        back = jnp.where(rest, 0, jnp.where(beyond, half + 1, (run + 1) // 2))
+        side = jnp.where(run == 0, 0, jnp.where(rest | beyond, 1, (run + 1) % 2))
+        slot = run % 2
+        middle = plane_blocks // 2
+        wanted = z >= back
+        wanted = wanted & jnp.logical_not(rest & (at_block < middle))
+        wanted = wanted & jnp.logical_not((run == 2 * half - 1) & (at_block > middle))
+        wanted = wanted & jnp.logical_not(beyond & (at_block > 0))
+        plane = lax.rem(z - back + z_count, z_count)
+        load = pltpu.make_async_copy(
+            keys.at[plane, pl.ds(side * (y_count // 2), y_count // 2)],
+            held.at[slot, 0],
+            held_sems.at[slot, 0],
+        )
+        return wanted, load, (z - back) * plane_keys + side * chunk, slot
+
+    def start_far(run):
+        wanted, load, _, _ = far_run(run)
+
+        @pl.when(wanted)
+        def _():
+            load.start()
+
+    def far_runs(begin, end):
+        start_far(jnp.int32(begin))
+
+        @pl.loop(begin, end)
+        def _(run):
+            @pl.when(run + 1 < end)
+            def _():
+                start_far(run + 1)
+
+            wanted, load, first_spot, slot = far_run(run)
+
+            @pl.when(wanted)
+            def _():
+                load.wait()
+                spot = first_spot + lax.broadcasted_iota(jnp.int32, (1, chunk), 1)
+                seen = (spot >= row_low) & (spot <= position)
+                bias[:, :chunk] = jnp.where(seen, 0.0, masked_low)
+                fold(far_q, 0, held[slot, 0].reshape(chunk, width))
+
+    def project(head, part):
+        norm = 1.0 / jnp.sum(total[part, :], axis=1, keepdims=True)
+        mixed = (acc[part, :] * norm).astype(jnp.bfloat16)
+        ready[head] = jnp.dot(mixed, up[head], preferred_element_type=jnp.float32).astype(
+            jnp.bfloat16
+        )
+
+    @pl.when(section == 1)
+    def _():
+        for stage in range(half + 1):
+            on(core == 0, functools.partial(decode_a, stage))
+            on(core == 1, functools.partial(decode_b, stage))
+            if stage == 1:
+                arrive(far_nope, far_recv.at[0])
+                arrive(far_rope, far_recv.at[1])
+                absorb(far_nope, far_rope, far_q, near, FAR_HEADS)
+                load_value_up().start()
+            if 0 < stage < half:
+                for n in steps[stage - 1]:
+                    from_sibling(n)
+                far_runs(max(2 * stage - 3, 0), 2 * stage - 1)
+        for n in steps[half - 1] + steps[half]:
+            from_sibling(n)
+        far_runs(2 * half - 3, 2 * half + 3)
+        load_value_up().wait()
+
+        @pl.loop(0, FAR_HEADS)
+        def _(head):
+            project(near + head, pl.ds(pl.multiple_of(head * tokens, tokens), tokens))
+
+        far_result().start()
 
     @pl.when(section == 0)
     def _():
         load_value_up().wait()
 
-        @pl.loop(0, heads)
+        @pl.loop(0, near)
         def _(head):
-            part = pl.ds(pl.multiple_of(head * tokens, tokens), tokens)
-            norm = 1.0 / jnp.sum(total[part, :], axis=1, keepdims=True)
-            mixed = (acc[part, :] * norm).astype(jnp.bfloat16)
-            ready[head] = jnp.dot(mixed, up[head], preferred_element_type=jnp.float32).astype(
-                jnp.bfloat16
-            )
-
+            project(head, pl.ds(pl.multiple_of(head * tokens, tokens), tokens))
+
+        arrive(ready.at[pl.ds(near, FAR_HEADS)], far_recv.at[2])
         done = pltpu.make_async_copy(ready, out, out_sems.at[1])
         done.start()
         done.wait()
-        for copy in x_copies():
+        for copy in x_copies() + far_copies():
             copy.wait_send()
 
     @pl.when(section == 1)
     def _():
         pltpu.make_async_copy(q, q_out, out_sems.at[0]).wait()
+        far_result().wait_send()
 
     groups = [section == 0, (section == 1) & (core == 0), (section == 1) & (core == 1)]
     for group, copies in zip(groups, went):
@@ -593,12 +699,17 @@
             pltpu.VMEM(q_nope.shape, bf16),
             pltpu.VMEM(up_key.shape, bf16),
             pltpu.VMEM((heads, tokens, width), bf16),
-            pltpu.VMEM((heads * tokens, kv_rank), jnp.float32),
-            pltpu.VMEM((heads * tokens, LANES), jnp.float32),
-            pltpu.VMEM((heads * tokens, LANES), jnp.float32),
+            pltpu.VMEM((FAR_HEADS,) + q_nope.shape[1:], bf16),
+            pltpu.VMEM((tokens, FAR_HEADS * (width - kv_rank)), bf16),
+            pltpu.VMEM((FAR_HEADS, tokens, width), bf16),
+            pltpu.VMEM(((heads - FAR_HEADS) * tokens, kv_rank), jnp.float32),
+            pltpu.VMEM(((heads - FAR_HEADS) * tokens, LANES), jnp.float32),
+            pltpu.VMEM(((heads - FAR_HEADS) * tokens, LANES), jnp.float32),
             pltpu.VMEM((2, 2, y_count // 2, 2, 2, rows, width), bf16),
             pltpu.VMEM((tokens, chunk + tokens), jnp.float32),
             pltpu.VMEM((heads, tokens, value_up.shape[2]), bf16),
+            dma((3,)),
+            dma((3,)),
             dma((2,)),
             dma((2,)),
             dma((2, 2)),

time: 117 us -> 107 us (0.915)
  the two profiles are of different devices: /device:TPU:161 before, /device:TPU:203 now
where the time goes in v6:
time: 107 us
  Pallas kernels  101 us (94%)
  local copies, waits for them, and re-layouts  5.47 us (5%)
    pallas_call x1, Pallas kernels, prefill_part(): pl.pallas_call(functools.partial(prefill_kernel, z_count, y_count, kv_ran...  66.1 us
    pallas_call x1, Pallas kernels, shards(): pl.pallas_call(functools.partial(decode_kernel, kv_rank, groups, exponent...  34.9 us
    broadcast_in_dim x1, local copies, waits for them, and re-layouts, shards(): return attended.swapaxes(0, 1)[None]  2.87 us
    unnamed x1, local copies, waits for them, and re-layouts  2.6 us

profile of v6, /device:TPU:203, one launch (start us, length us, event | category | flops | bytes accessed | tf_op | source)
XLA Modules:
  0.0 106.5 jit_solution(1137732102725092530)
XLA Ops:
  0.0 2.6 %copy.12 = bf16[1,128,32,128]{3,1,2,0:T(8,128)(2,1)} copy(bf16[1,128,32,128]{3,2,1,0:T(8,128)(2,1)} %param.7) | data formatting | bytes 2097152 | tf_op args[0]
  2.6 66.1 %shard_map.73 = (bf16[8,4,2,2,64,576]{5,4,3,2,1,0:T(8,128)(2,1)}, bf16[2,64,576]{2,1,0:T(8,128)(2,1)}, bf16[32,128,576]{2,1,0:T(8,128)(2,1)}, bf16[32,128,128]{2,1,0:T(8,128)(2,1)}) custom-call(bf16[64,576]{1,0:T(8,128)(2,1)} %bitcast.18, bf16[32,128,128]{2,1,0:T(8,128)(2,1)} %bitcast.15, bf16[128,2048]{1,0:T(8,128)(2,1)} %bitcast.16, ...), custom_call_target="tpu_custom_call" | custom-call | tf_op jit(solution)/shard_map/pallas_call | solution.py:687
  68.7 34.9 %shard_map.74 = bf16[32,128,128]{2,1,0:T(8,128)(2,1)} custom-call(s32[32]{0:T(128)} %lengths.1, s32[256]{0:T(256)} %table.1, bf16[32,128,576]{2,1,0:T(8,128)(2,1)} %get-tuple-element.9.q_ref, bf16[8192,576]{1,0:T(8,128)(2,1)} %bitcast.13, bf16[128,576]{1,0:T(8,128)(2,1)} %bitcast.17, bf16[32,512,128]{2,1,0:T(8,128)(2,1)} %value_up.3, ...), custom_call_target="tpu_custom_call", output_to_operand_aliasing={{}: (6, {})} | custom-call | tf_op jit(solution)/shard_map/pallas_call | solution.py:946
  103.7 2.9 %copy.10 = bf16[1,128,32,128]{3,2,1,0:T(8,128)(2,1)} copy(bf16[1,128,32,128]{3,1,2,0:T(8,128)(2,1)} %bitcast.14) | data formatting | bytes 2097152 | tf_op jit(solution)/shard_map/broadcast_in_dim | solution.py:986

commit v7 on v6

--- a/solution.py
+++ b/solution.py
@@ -18,7 +18,7 @@
 
 KEY_BLOCK = 1024
 EDGE_BLOCK = 512
-FAR_HEADS = 8
+FAR_HEADS = 6
 
 CHAIN_STEPS = (0, 1, 3, 5)
 ON_STEPS = (0, 2, 5, 8)
@@ -30,7 +30,7 @@
 
 def prefill_kernel(
     z_count, y_count, kv_rank, exponent_scale, own_in, q_nope, q_rope, up_key, value_up, lengths,
-    keys, own_out, q_out, out, block, nope, up, q, far_nope, far_rope, far_q, acc, top, total,
+    keys, own_out, q_out, out, block, raw, nope, up, q, far_nope, far_rope, far_q, acc, top, total,
     held, bias, ready, far_send, far_recv,
     in_sems, out_sems, held_sems, x_send, x_recv, own_sems,
     z_send, z_recv, y_send, y_recv, sib_send, sib_recv,
@@ -63,7 +63,7 @@
         )
 
     loads = [
-        pltpu.make_async_copy(q_nope, nope, in_sems.at[0]),
+        pltpu.make_async_copy(q_nope, raw, in_sems.at[0]),
         pltpu.make_async_copy(up_key, up, in_sems.at[1]),
     ]
     for load in loads:
@@ -141,6 +141,7 @@
 
     for load in loads:
         load.wait()
+    nope[...] = jnp.swapaxes(raw[...], 0, 1)
 
     near = heads - FAR_HEADS
     half_lanes = LANES // 2
@@ -634,9 +635,11 @@
         far_runs(2 * half - 3, 2 * half + 3)
         load_value_up().wait()
 
-        @pl.loop(0, FAR_HEADS)
-        def _(head):
-            project(near + head, pl.ds(pl.multiple_of(head * tokens, tokens), tokens))
+        @pl.loop(0, FAR_HEADS // 2)
+        def _(pair):
+            for side in range(2):
+                head = pair * 2 + side
+                project(near + head, pl.ds(pl.multiple_of(head * tokens, tokens), tokens))
 
         far_result().start()
 
@@ -644,12 +647,15 @@
     def _():
         load_value_up().wait()
 
-        @pl.loop(0, near)
-        def _(head):
-            project(head, pl.ds(pl.multiple_of(head * tokens, tokens), tokens))
+        @pl.loop(0, near // 2)
+        def _(pair):
+            for side in range(2):
+                head = pair * 2 + side
+                project(head, pl.ds(pl.multiple_of(head * tokens, tokens), tokens))
 
         arrive(ready.at[pl.ds(near, FAR_HEADS)], far_recv.at[2])
-        done = pltpu.make_async_copy(ready, out, out_sems.at[1])
+        raw[...] = jnp.swapaxes(ready[...], 0, 1)
+        done = pltpu.make_async_copy(raw, out, out_sems.at[1])
         done.start()
         done.wait()
         for copy in x_copies() + far_copies():
@@ -675,7 +681,7 @@
 
 def prefill_part(own, q_nope, q_rope, up_key, value_up, lengths, seq_count, exponent_scale):
     rows, width = own.shape
-    heads, tokens, _ = q_nope.shape
+    tokens, heads, nope_dim = q_nope.shape
     kv_rank = up_key.shape[1]
     y_count = 4
     z_count = seq_count // (2 * y_count)
@@ -690,16 +696,17 @@
             jax.ShapeDtypeStruct((z_count, y_count, 2, 2, rows, width), bf16),
             jax.ShapeDtypeStruct((2, rows, width), bf16),
             jax.ShapeDtypeStruct((heads, tokens, width), bf16),
-            jax.ShapeDtypeStruct((heads, tokens, value_up.shape[2]), bf16),
+            jax.ShapeDtypeStruct((tokens, heads, value_up.shape[2]), bf16),
         ],
         in_specs=[vmem, hbm, vmem, hbm, hbm, vmem],
         out_specs=[hbm] * 4,
         scratch_shapes=[
             pltpu.VMEM((rows, width), bf16),
             pltpu.VMEM(q_nope.shape, bf16),
+            pltpu.VMEM((heads, tokens, nope_dim), bf16),
             pltpu.VMEM(up_key.shape, bf16),
             pltpu.VMEM((heads, tokens, width), bf16),
-            pltpu.VMEM((FAR_HEADS,) + q_nope.shape[1:], bf16),
+            pltpu.VMEM((FAR_HEADS, tokens, nope_dim), bf16),
             pltpu.VMEM((tokens, FAR_HEADS * (width - kv_rank)), bf16),
             pltpu.VMEM((FAR_HEADS, tokens, width), bf16),
             pltpu.VMEM(((heads - FAR_HEADS) * tokens, kv_rank), jnp.float32),
@@ -743,7 +750,7 @@
     keys,
     own_keys,
     value_up,
-    _,
+    prefill_out,
     out_ref,
     acc,
     top,
@@ -752,6 +759,7 @@
     lat,
     up,
     ready,
+    turned,
     q_held,
     sems,
     q_sems,
@@ -763,6 +771,18 @@
     rows = heads * tokens
     all_keys = keys.shape[0]
     nt = (((1,), (1,)), ((), ()))
+
+    @pl.when(lax.axis_index("section") == 0)
+    def _():
+        handed = pltpu.make_async_copy(prefill_out, out_ref, up_sems.at[1])
+
+        @pl.when(band == 0)
+        def _():
+            handed.start()
+
+        @pl.when(band == bands - 1)
+        def _():
+            handed.wait()
 
     @pl.when(lax.axis_index("section") == 1)
     def _():
@@ -910,13 +930,18 @@
         def _():
             load_up().wait()
 
-            @pl.loop(0, heads)
-            def _(head):
-                ready[head] = jnp.dot(
-                    lat[head], up[head], preferred_element_type=jnp.float32
-                ).astype(jnp.bfloat16)
-
-            done = pltpu.make_async_copy(ready, out_ref, up_sems.at[1])
+            @pl.loop(0, heads // 4)
+            def _(four):
+                picked = [four * 4 + k for k in range(4)]
+                products = [
+                    jnp.dot(lat[head], up[head], preferred_element_type=jnp.float32)
+                    for head in picked
+                ]
+                for head, product in zip(picked, products):
+                    ready[head] = product.astype(jnp.bfloat16)
+
+            turned[...] = jnp.swapaxes(ready[...], 0, 1)
+            done = pltpu.make_async_copy(turned, out_ref, up_sems.at[1])
             done.start()
             done.wait()
 
@@ -927,6 +952,7 @@
     rope_dim = query_rope.shape[2] // head_dev
     kv_rank = up_key.shape[1]
     width = kv_rank + rope_dim
+    v_dim = value_up_weight.shape[2]
     req_dev = owner_request_table.shape[0] // seq_count
     groups = owner_request_table.shape[0] // lengths.shape[0]
     band_tokens = tok_dev // req_dev
@@ -934,7 +960,7 @@
 
     keys, pair, queries, prefill_out = prefill_part(
         latent[0],
-        query_nope[0].swapaxes(0, 1),
+        query_nope[0],
         query_rope[0],
         up_key,
         value_up_weight,
@@ -964,6 +990,7 @@
                 pltpu.VMEM((4, KEY_BLOCK, width), jnp.bfloat16),
                 pltpu.VMEM((head_dev, tok_dev, kv_rank), jnp.bfloat16),
                 pltpu.VMEM(value_up_weight.shape, jnp.bfloat16),
+                pltpu.VMEM((head_dev, tok_dev, v_dim), jnp.bfloat16),
                 pltpu.VMEM(prefill_out.shape, jnp.bfloat16),
                 pltpu.VMEM((2, head_dev, band_tokens, width), jnp.bfloat16),
                 pltpu.SemaphoreType.DMA((4,)),
@@ -971,7 +998,6 @@
                 pltpu.SemaphoreType.DMA((2,)),
             ],
         ),
-        input_output_aliases={6: 0},
         compiler_params=pltpu.CompilerParams(vmem_limit_bytes=58 << 20),
     )(
         lengths,
@@ -983,7 +1009,7 @@
         prefill_out,
     )
 
-    return attended.swapaxes(0, 1)[None]
+    return attended[None]
 
 
 def solution(mesh):

time: 107 us -> 132 us (1.23)
  the two profiles are of different devices: /device:TPU:203 before, /device:TPU:161 now
where the time goes in v7:
time: 132 us
  Pallas kernels  131 us (99%)
    pallas_call x1, Pallas kernels, prefill_part(): pl.pallas_call(functools.partial(prefill_kernel, z_count, y_count, kv_ran...  97.1 us
    pallas_call x1, Pallas kernels, shards(): pl.pallas_call(functools.partial(decode_kernel, kv_rank, groups, exponent...  34.4 us

profile of v7, /device:TPU:161, one launch (start us, length us, event | category | flops | bytes accessed | tf_op | source)
XLA Modules:
  0.0 131.6 jit_solution(3628304220526221634)
XLA Ops:
  0.0 97.1 %shard_map.73 = (bf16[8,4,2,2,64,576]{5,4,3,2,1,0:T(8,128)(2,1)}, bf16[2,64,576]{2,1,0:T(8,128)(2,1)}, bf16[32,128,576]{2,1,0:T(8,128)(2,1)}, bf16[128,32,128]{2,1,0:T(8,128)(2,1)}) custom-call(bf16[64,576]{1,0:T(8,128)(2,1)} %bitcast.11, bf16[128,32,128]{2,1,0:T(8,128)(2,1)} %bitcast.8, bf16[128,2048]{1,0:T(8,128)(2,1)} %bitcast.9, ...), custom_call_target="tpu_custom_call" | custom-call | tf_op jit(solution)/shard_map/pallas_call | solution.py:693
  97.1 34.4 %shard_map.74 = bf16[128,32,128]{2,1,0:T(8,128)(2,1)} custom-call(s32[32]{0:T(128)} %lengths.1, s32[256]{0:T(256)} %table.1, bf16[32,128,576]{2,1,0:T(8,128)(2,1)} %get-tuple-element.9.q_ref, bf16[8192,576]{1,0:T(8,128)(2,1)} %bitcast.7, bf16[128,576]{1,0:T(8,128)(2,1)} %bitcast.10, bf16[32,512,128]{2,1,0:T(8,128)(2,1)} %value_up.3, ...), custom_call_target="tpu_custom_call" | custom-call | tf_op jit(solution)/shard_map/pallas_call | solution.py:972

commit v8 on v7

--- a/solution.py
+++ b/solution.py
@@ -774,10 +774,13 @@
 
     @pl.when(lax.axis_index("section") == 0)
     def _():
-        handed = pltpu.make_async_copy(prefill_out, out_ref, up_sems.at[1])
+        taken = pltpu.make_async_copy(prefill_out, turned, up_sems.at[0])
+        handed = pltpu.make_async_copy(turned, out_ref, up_sems.at[1])
 
         @pl.when(band == 0)
         def _():
+            taken.start()
+            taken.wait()
             handed.start()
 
         @pl.when(band == bands - 1)

time: 132 us -> 101 us (0.77)
  Pallas kernels: 131 us -> 101 us
    pallas_call x1, Pallas kernels: 34.4 us -> 3.76 us  [shards(): pl.pallas_call(functools.partial(decode_kernel, kv_rank, groups, exponent...]
where the time goes in v8:
time: 101 us
  Pallas kernels  101 us (100%)
    pallas_call x1, Pallas kernels, prefill_part(): pl.pallas_call(functools.partial(prefill_kernel, z_count, y_count, kv_ran...  97.1 us
    pallas_call x1, Pallas kernels, shards(): pl.pallas_call(functools.partial(decode_kernel, kv_rank, groups, exponent...  3.76 us

profile of v8, /device:TPU:161, one launch (start us, length us, event | category | flops | bytes accessed | tf_op | source)
XLA Modules:
  0.0 101.0 jit_solution(9973177281018515869)
XLA Ops:
  0.0 97.1 %shard_map.73 = (bf16[8,4,2,2,64,576]{5,4,3,2,1,0:T(8,128)(2,1)}, bf16[2,64,576]{2,1,0:T(8,128)(2,1)}, bf16[32,128,576]{2,1,0:T(8,128)(2,1)}, bf16[128,32,128]{2,1,0:T(8,128)(2,1)}) custom-call(bf16[64,576]{1,0:T(8,128)(2,1)} %bitcast.11, bf16[128,32,128]{2,1,0:T(8,128)(2,1)} %bitcast.8, bf16[128,2048]{1,0:T(8,128)(2,1)} %bitcast.9, ...), custom_call_target="tpu_custom_call" | custom-call | tf_op jit(solution)/shard_map/pallas_call | solution.py:693
  97.1 3.8 %shard_map.74 = bf16[128,32,128]{2,1,0:T(8,128)(2,1)} custom-call(s32[32]{0:T(128)} %lengths.1, s32[256]{0:T(256)} %table.1, bf16[32,128,576]{2,1,0:T(8,128)(2,1)} %get-tuple-element.9.q_ref, bf16[8192,576]{1,0:T(8,128)(2,1)} %bitcast.7, bf16[128,576]{1,0:T(8,128)(2,1)} %bitcast.10, bf16[32,512,128]{2,1,0:T(8,128)(2,1)} %value_up.3, ...), custom_call_target="tpu_custom_call" | custom-call | tf_op jit(solution)/shard_map/pallas_call | solution.py:975

commit v9 on v8

--- a/solution.py
+++ b/solution.py
@@ -635,11 +635,8 @@
         far_runs(2 * half - 3, 2 * half + 3)
         load_value_up().wait()
 
-        @pl.loop(0, FAR_HEADS // 2)
-        def _(pair):
-            for side in range(2):
-                head = pair * 2 + side
-                project(near + head, pl.ds(pl.multiple_of(head * tokens, tokens), tokens))
+        for head in range(FAR_HEADS):
+            project(near + head, pl.ds(head * tokens, tokens))
 
         far_result().start()
 
@@ -647,10 +644,10 @@
     def _():
         load_value_up().wait()
 
-        @pl.loop(0, near // 2)
-        def _(pair):
-            for side in range(2):
-                head = pair * 2 + side
+        @pl.loop(0, 2)
+        def _(part):
+            for place in range(near // 2):
+                head = part * (near // 2) + place
                 project(head, pl.ds(pl.multiple_of(head * tokens, tokens), tokens))
 
         arrive(ready.at[pl.ds(near, FAR_HEADS)], far_recv.at[2])
@@ -933,9 +930,9 @@
         def _():
             load_up().wait()
 
-            @pl.loop(0, heads // 4)
-            def _(four):
-                picked = [four * 4 + k for k in range(4)]
+            @pl.loop(0, heads // 8)
+            def _(eight):
+                picked = [eight * 8 + k for k in range(8)]
                 products = [
                     jnp.dot(lat[head], up[head], preferred_element_type=jnp.float32)
                     for head in picked

time: 101 us -> 103 us (1.020)
  the two profiles are of different devices: /device:TPU:161 before, /device:TPU:239 now
where the time goes in v9:
time: 103 us; the launch traced here: 102 us
  Pallas kernels  102 us (99%)
    pallas_call x1, Pallas kernels, prefill_part(): pl.pallas_call(functools.partial(prefill_kernel, z_count, y_count, kv_ran...  60.3 us
    pallas_call x1, Pallas kernels, shards(): pl.pallas_call(functools.partial(decode_kernel, kv_rank, groups, exponent...  42 us

profile of v9, /device:TPU:239, one launch (start us, length us, event | category | flops | bytes accessed | tf_op | source)
XLA Modules:
  0.0 102.5 jit_solution(16103467383904422306)
XLA Ops:
  0.0 60.3 %shard_map.73 = (bf16[8,4,2,2,64,576]{5,4,3,2,1,0:T(8,128)(2,1)}, bf16[2,64,576]{2,1,0:T(8,128)(2,1)}, bf16[32,128,576]{2,1,0:T(8,128)(2,1)}, bf16[128,32,128]{2,1,0:T(8,128)(2,1)}) custom-call(bf16[64,576]{1,0:T(8,128)(2,1)} %bitcast.11, bf16[128,32,128]{2,1,0:T(8,128)(2,1)} %bitcast.8, bf16[128,2048]{1,0:T(8,128)(2,1)} %bitcast.9, ...), custom_call_target="tpu_custom_call" | custom-call | tf_op jit(solution)/shard_map/pallas_call | solution.py:690
  60.3 42.0 %shard_map.74 = bf16[128,32,128]{2,1,0:T(8,128)(2,1)} custom-call(s32[32]{0:T(128)} %lengths.1, s32[256]{0:T(256)} %table.1, bf16[32,128,576]{2,1,0:T(8,128)(2,1)} %get-tuple-element.9.q_ref, bf16[8192,576]{1,0:T(8,128)(2,1)} %bitcast.7, bf16[128,576]{1,0:T(8,128)(2,1)} %bitcast.10, bf16[32,512,128]{2,1,0:T(8,128)(2,1)} %value_up.3, ...), custom_call_target="tpu_custom_call" | custom-call | tf_op jit(solution)/shard_map/pallas_call | solution.py:972

commit v10 on v9

--- a/solution.py
+++ b/solution.py
@@ -758,6 +758,7 @@
     ready,
     turned,
     q_held,
+    own_held,
     sems,
     q_sems,
     up_sems,
@@ -811,6 +812,9 @@
         def load_up():
             return pltpu.make_async_copy(value_up, up, up_sems.at[0])
 
+        def load_own():
+            return pltpu.make_async_copy(own_keys, own_held, up_sems.at[2])
+
         low, last = prompt_range(band)
         first = low // 16 * 16
         chunks = (last - first + KEY_BLOCK - 1) // KEY_BLOCK
@@ -821,9 +825,11 @@
 
         @pl.when(band == 0)
         def _():
+            load_own().start()
             fetch_q(0).start()
             fetch(0).start()
             load_up().start()
+            load_own().wait()
 
         @pl.when(band + 1 < bands)
         def _():
@@ -851,7 +857,7 @@
             )
 
         def begin(key_block, at):
-            own = own_keys[...]
+            own = own_held[band_rows(band), :]
             asked = lax.broadcasted_iota(jnp.int32, (tokens, tokens), 0)
             key = lax.broadcasted_iota(jnp.int32, (tokens, tokens), 1)
             seen = (asked % SAMPLES == key % SAMPLES) & (key // SAMPLES <= asked // SAMPLES)
@@ -978,7 +984,7 @@
             in_specs=[
                 pl.BlockSpec(memory_space=pl.ANY),
                 pl.BlockSpec(memory_space=pl.ANY),
-                pl.BlockSpec((band_tokens, width), lambda i, *_: (i, 0)),
+                pl.BlockSpec(memory_space=pl.ANY),
                 pl.BlockSpec(memory_space=pl.ANY),
                 pl.BlockSpec(memory_space=pl.ANY),
             ],
@@ -993,9 +999,10 @@
                 pltpu.VMEM((head_dev, tok_dev, v_dim), jnp.bfloat16),
                 pltpu.VMEM(prefill_out.shape, jnp.bfloat16),
                 pltpu.VMEM((2, head_dev, band_tokens, width), jnp.bfloat16),
+                pltpu.VMEM((tok_dev, width), jnp.bfloat16),
                 pltpu.SemaphoreType.DMA((4,)),
                 pltpu.SemaphoreType.DMA((2,)),
-                pltpu.SemaphoreType.DMA((2,)),
+                pltpu.SemaphoreType.DMA((3,)),
             ],
         ),
         compiler_params=pltpu.CompilerParams(vmem_limit_bytes=58 << 20),

time: 103 us -> 99.5 us (0.966)
  the two profiles are of different devices: /device:TPU:239 before, /device:TPU:161 now
where the time goes in v10:
time: 99.5 us; the launch traced here: 97.9 us
  Pallas kernels  97.7 us (98%)
    pallas_call x1, Pallas kernels, prefill_part(): pl.pallas_call(functools.partial(prefill_kernel, z_count, y_count, kv_ran...  94.7 us
    pallas_call x1, Pallas kernels, shards(): pl.pallas_call(functools.partial(decode_kernel, kv_rank, groups, exponent...  2.98 us

profile of v10, /device:TPU:161, one launch (start us, length us, event | category | flops | bytes accessed | tf_op | source)
XLA Modules:
  0.0 97.9 jit_solution(1117872393379661664)
XLA Ops:
  0.0 94.7 %shard_map.73 = (bf16[8,4,2,2,64,576]{5,4,3,2,1,0:T(8,128)(2,1)}, bf16[2,64,576]{2,1,0:T(8,128)(2,1)}, bf16[32,128,576]{2,1,0:T(8,128)(2,1)}, bf16[128,32,128]{2,1,0:T(8,128)(2,1)}) custom-call(bf16[64,576]{1,0:T(8,128)(2,1)} %bitcast.11, bf16[128,32,128]{2,1,0:T(8,128)(2,1)} %bitcast.8, bf16[128,2048]{1,0:T(8,128)(2,1)} %bitcast.9, ...), custom_call_target="tpu_custom_call" | custom-call | tf_op jit(solution)/shard_map/pallas_call | solution.py:690
  94.7 3.0 %shard_map.74 = bf16[128,32,128]{2,1,0:T(8,128)(2,1)} custom-call(s32[32]{0:T(128)} %lengths.1, s32[256]{0:T(256)} %table.1, bf16[32,128,576]{2,1,0:T(8,128)(2,1)} %get-tuple-element.9.q_ref, bf16[8192,576]{1,0:T(8,128)(2,1)} %bitcast.7, bf16[128,576]{1,0:T(8,128)(2,1)} %bitcast.10, bf16[32,512,128]{2,1,0:T(8,128)(2,1)} %value_up.3, ...), custom_call_target="tpu_custom_call" | custom-call | tf_op jit(solution)/shard_map/pallas_call | solution.py:978

commit v11 on v10

--- a/solution.py
+++ b/solution.py
@@ -650,11 +650,21 @@
                 head = part * (near // 2) + place
                 project(head, pl.ds(pl.multiple_of(head * tokens, tokens), tokens))
 
+        middle = heads // 2
+
+        def leave(part):
+            some = pl.ds(part * middle, middle)
+            return pltpu.make_async_copy(
+                raw.at[:, some, :], out.at[:, some, :], out_sems.at[part]
+            )
+
+        raw[:, :middle, :] = jnp.swapaxes(ready[:middle], 0, 1)
+        leave(0).start()
         arrive(ready.at[pl.ds(near, FAR_HEADS)], far_recv.at[2])
-        raw[...] = jnp.swapaxes(ready[...], 0, 1)
-        done = pltpu.make_async_copy(raw, out, out_sems.at[1])
-        done.start()
-        done.wait()
+        raw[:, middle:, :] = jnp.swapaxes(ready[middle:], 0, 1)
+        leave(1).start()
+        leave(0).wait()
+        leave(1).wait()
         for copy in x_copies() + far_copies():
             copy.wait_send()
 
@@ -772,18 +782,28 @@
 
     @pl.when(lax.axis_index("section") == 0)
     def _():
-        taken = pltpu.make_async_copy(prefill_out, turned, up_sems.at[0])
-        handed = pltpu.make_async_copy(turned, out_ref, up_sems.at[1])
+        some = [pl.ds(part * (turned.shape[0] // 2), turned.shape[0] // 2) for part in range(2)]
+        taken = [
+            pltpu.make_async_copy(prefill_out.at[part], turned.at[part], sem)
+            for part, sem in zip(some, (up_sems.at[0], up_sems.at[2]))
+        ]
+        handed = [
+            pltpu.make_async_copy(turned.at[part], out_ref.at[part], sem)
+            for part, sem in zip(some, (up_sems.at[1], q_sems.at[0]))
+        ]
 
         @pl.when(band == 0)
         def _():
-            taken.start()
-            taken.wait()
-            handed.start()
+            for copy in taken:
+                copy.start()
+            for came, goes in zip(taken, handed):
+                came.wait()
+                goes.start()
 
         @pl.when(band == bands - 1)
         def _():
-            handed.wait()
+            for copy in handed:
+                copy.wait()
 
     @pl.when(lax.axis_index("section") == 1)
     def _():

time: 99.5 us -> 97.8 us (0.983); the launches traced: 97.9 us -> 97.5 us
  no operation moved by 1% of the time
where the time goes in v11:
time: 97.8 us; the launch traced here: 97.5 us
  Pallas kernels  97.3 us (99%)
    pallas_call x1, Pallas kernels, prefill_part(): pl.pallas_call(functools.partial(prefill_kernel, z_count, y_count, kv_ran...  94.5 us
    pallas_call x1, Pallas kernels, shards(): pl.pallas_call(functools.partial(decode_kernel, kv_rank, groups, exponent...  2.79 us

profile of v11, /device:TPU:161, one launch (start us, length us, event | category | flops | bytes accessed | tf_op | source)
XLA Modules:
  0.0 97.5 jit_solution(1551234058764521487)
XLA Ops:
  0.0 94.5 %shard_map.73 = (bf16[8,4,2,2,64,576]{5,4,3,2,1,0:T(8,128)(2,1)}, bf16[2,64,576]{2,1,0:T(8,128)(2,1)}, bf16[32,128,576]{2,1,0:T(8,128)(2,1)}, bf16[128,32,128]{2,1,0:T(8,128)(2,1)}) custom-call(bf16[64,576]{1,0:T(8,128)(2,1)} %bitcast.11, bf16[128,32,128]{2,1,0:T(8,128)(2,1)} %bitcast.8, bf16[128,2048]{1,0:T(8,128)(2,1)} %bitcast.9, ...), custom_call_target="tpu_custom_call" | custom-call | tf_op jit(solution)/shard_map/pallas_call | solution.py:700
  94.5 2.8 %shard_map.74 = bf16[128,32,128]{2,1,0:T(8,128)(2,1)} custom-call(s32[32]{0:T(128)} %lengths.1, s32[256]{0:T(256)} %table.1, bf16[32,128,576]{2,1,0:T(8,128)(2,1)} %get-tuple-element.9.q_ref, bf16[8192,576]{1,0:T(8,128)(2,1)} %bitcast.7, bf16[128,576]{1,0:T(8,128)(2,1)} %bitcast.10, bf16[32,512,128]{2,1,0:T(8,128)(2,1)} %value_up.3, ...), custom_call_target="tpu_custom_call" | custom-call | tf_op jit(solution)/shard_map/pallas_call | solution.py:998
